TPU v7x, 32 devices: a whole 2x2x4 slice. The times are simulated.
32 devices in a mesh: dp: 4 (over x, core), ctx: 4 (over z), mp: 2 (over y).
Axes of the slice: x: 2, y: 2, z: 4, core: 2. Of those that a mesh axis runs over, the one named last changes fastest.
Arguments:
- tokens: bfloat16 [8, 2048, 2048], P('dp', 'ctx'), may hold values from -40 to 40
- group_order: int32 [8, 8], P('dp'), may hold values from 0 to 7, each once within a row
- grad_out: bfloat16 [8, 2048, 2048], P('dp', 'ctx'), may hold values from -6 to 6
- norm_gain: bfloat16 [2048], P(('dp', 'ctx')), may hold values from 0.5 to 1.5
- norm_bias: bfloat16 [2048], P(('dp', 'ctx')), may hold values from -1.25 to 1.25
- w_qkv: bfloat16 [2048, 3, 2048], P(('dp', 'ctx'), None, 'mp'), may hold values from -0.125 to 0.125
- b_qkv: bfloat16 [3, 32, 64], P(None, 'mp', ('dp', 'ctx')), may hold values from -1.75 to 1.75
- w_out: bfloat16 [2048, 2048], P('mp', ('dp', 'ctx')), may hold values from -2 to 2
- b_out: bfloat16 [2048], P(('dp', 'ctx')), may hold values from -1.25 to 1.25
- w_fc1: bfloat16 [2048, 8192], P(('dp', 'ctx'), 'mp'), may hold values from -1 to 1
- b_fc1: bfloat16 [128, 64], P('mp', ('dp', 'ctx')), may hold values from -1.75 to 1.75
- w_fc2: bfloat16 [8192, 2048], P('mp', ('dp', 'ctx')), may hold values from -1 to 1
- b_fc2: bfloat16 [2048], P(('dp', 'ctx')), may hold values from -1.25 to 1.25
Outputs:
- block_out: bfloat16 [8, 2048, 2048], P('dp', 'ctx')
- grad_tokens: float32 [8, 2048, 2048], P('dp', 'ctx')
- grad_norm_gain: float32 [2048], P(('dp', 'ctx'))
- grad_norm_bias: float32 [2048], P(('dp', 'ctx'))
- grad_w_qkv: float32 [2048, 3, 2048], P(('dp', 'ctx'), None, 'mp')
- grad_b_qkv: float32 [3, 32, 64], P(None, 'mp', ('dp', 'ctx'))
- grad_w_out: float32 [2048, 2048], P('mp', ('dp', 'ctx'))
- grad_b_out: float32 [2048], P(('dp', 'ctx'))
- grad_w_fc1: float32 [2048, 8192], P(('dp', 'ctx'), 'mp')
- grad_b_fc1: float32 [128, 64], P('mp', ('dp', 'ctx'))
- grad_w_fc2: float32 [8192, 2048], P('mp', ('dp', 'ctx'))
- grad_b_fc2: float32 [2048], P(('dp', 'ctx'))
- root_means: float32 [3], replicated
Inputs may be any that keep to these rules, and one draw needn't show every extreme that they name: `group_order`: each row lists every block of positions once.
All inputs are finite; a program needn't handle non-finite values.
Results may differ from a plain program's by a relative error of at most 0.019.
Values may be sent and summed in bfloat16 or wider, within the bound.
No kernel may reach another device: no remote copies, remote signals or barrier semaphores. Data moves between devices by JAX's collectives and lax.ppermute only.
A program may use at most 384 MiB of HBM per device.

v0:
```python
from functools import partial

import jax
import jax.numpy as jnp
from jax import lax
from jax.sharding import PartitionSpec as P

HD = 64
ROT = 32
SEQ_LEN = 2048


norm_eps = 1e-05
rotary_base = 10000.0
masked_fill = -1e30


def slot_positions(order_rows, first_slot, slot_count):
    group_count = order_rows.shape[1]
    block_len = SEQ_LEN // group_count
    slot_ids = first_slot + jnp.arange(slot_count, dtype=jnp.int32)
    group_ids = slot_ids // block_len
    picked = (group_ids[:, None] == jnp.arange(group_count, dtype=jnp.int32)[None, :]).astype(
        jnp.int32
    )
    starts = jnp.sum(order_rows[:, None, :] * picked[None, :, :], axis=-1)
    return starts * block_len + (slot_ids % block_len)[None, :]


def rotary_tables(positions):
    half_rot = ROT // 2
    inverse = jnp.power(rotary_base, -jnp.arange(half_rot, dtype=jnp.float32) * (2.0 / ROT))
    angles = positions.astype(jnp.float32)[..., None] * inverse
    return (jnp.cos(angles)[..., None, :], jnp.sin(angles)[..., None, :])


def rotate(values, cosine_table, sine_table):
    half_rot = ROT // 2
    first = values[..., :half_rot]
    second = values[..., half_rot:ROT]
    return jnp.concatenate(
        [
            first * cosine_table - second * sine_table,
            second * cosine_table + first * sine_table,
            values[..., ROT:],
        ],
        axis=-1,
    )


def on_device(
    tokens,
    group_order,
    grad_out,
    norm_gain,
    norm_bias,
    w_qkv,
    b_qkv,
    w_out,
    b_out,
    w_fc1,
    b_fc1,
    w_fc2,
    b_fc2,
):
    gathered = (
        lax.all_gather(norm_gain, ("dp", "ctx"), axis=0, tiled=True),
        lax.all_gather(norm_bias, ("dp", "ctx"), axis=0, tiled=True),
        lax.all_gather(w_qkv, ("dp", "ctx"), axis=0, tiled=True),
        lax.all_gather(b_qkv, ("dp", "ctx"), axis=2, tiled=True),
        lax.all_gather(w_out, ("dp", "ctx"), axis=1, tiled=True),
        lax.all_gather(b_out, ("dp", "ctx"), axis=0, tiled=True),
        lax.all_gather(w_fc1, ("dp", "ctx"), axis=0, tiled=True),
        lax.all_gather(b_fc1, ("dp", "ctx"), axis=1, tiled=True),
        lax.all_gather(w_fc2, ("dp", "ctx"), axis=1, tiled=True),
        lax.all_gather(b_fc2, ("dp", "ctx"), axis=0, tiled=True),
    )
    seq_count = tokens.shape[0]
    slot_count = tokens.shape[1]
    model_width = tokens.shape[2]
    row_count = seq_count * slot_count
    gain_full = gathered[0].astype(jnp.float32)
    shift_full = gathered[1].astype(jnp.float32)
    qkv_weight = gathered[2]
    heads_width = qkv_weight.shape[2]
    head_count = heads_width // HD
    qkv_bias = gathered[3].reshape(3 * heads_width).astype(jnp.float32)
    out_weight = gathered[4]
    out_bias = gathered[5].astype(jnp.float32)
    fc1_weight = gathered[6]
    hidden_width = fc1_weight.shape[1]
    fc1_bias = gathered[7].reshape(hidden_width).astype(jnp.float32)
    fc2_weight = gathered[8]
    fc2_bias = gathered[9].astype(jnp.float32)
    score_scale = HD ** (-0.5)
    tokens_in = tokens.astype(jnp.float32).reshape(row_count, model_width)
    row_mean = jnp.mean(tokens_in, axis=-1, keepdims=True)
    centered = tokens_in - row_mean
    variance = jnp.mean(centered * centered, axis=-1, keepdims=True)
    inv_std = lax.rsqrt(variance + norm_eps)
    normed = centered * inv_std
    ln_out = (normed * gain_full + shift_full).astype(jnp.bfloat16)
    qkv_proj = (
        jnp.dot(
            ln_out,
            qkv_weight.reshape(model_width, 3 * heads_width),
            preferred_element_type=jnp.float32,
        )
        + qkv_bias
    )
    qkv_proj = qkv_proj.reshape(seq_count, slot_count, 3, head_count, HD)
    local_pos = slot_positions(group_order, lax.axis_index("ctx") * slot_count, slot_count)
    cosine_table, sine_table = rotary_tables(local_pos)
    queries = rotate(qkv_proj[:, :, 0], cosine_table, sine_table).astype(jnp.bfloat16)
    keys_here = (
        rotate(qkv_proj[:, :, 1], cosine_table, sine_table)
        .astype(jnp.bfloat16)
        .reshape(seq_count, slot_count, heads_width)
    )
    values_here = qkv_proj[:, :, 2].astype(jnp.bfloat16).reshape(seq_count, slot_count, heads_width)
    start_state = (
        jnp.full((seq_count, slot_count, head_count), masked_fill, jnp.float32),
        jnp.zeros((seq_count, slot_count, head_count), jnp.float32),
        jnp.zeros((seq_count, slot_count, head_count, HD), jnp.float32),
    )
    key_block = lax.all_gather(keys_here, "ctx", axis=1, tiled=True)
    value_block = lax.all_gather(values_here, "ctx", axis=1, tiled=True)
    key_count = key_block.shape[1]
    key_place = slot_positions(group_order, jnp.int32(0), key_count)

    def one_sequence(packed):
        query_seq, key_seq, value_seq, query_pos, key_pos, run_max, run_sum, run_acc = packed
        key_heads = key_seq.reshape(key_count, head_count, HD)
        value_heads = value_seq.reshape(key_count, head_count, HD)
        scores = (
            jnp.einsum("qhd,khd->qhk", query_seq, key_heads, preferred_element_type=jnp.float32)
            * score_scale
        )
        allowed = key_pos[None, None, :] <= query_pos[:, None, None]
        new_max = jnp.maximum(run_max, jnp.max(jnp.where(allowed, scores, masked_fill), axis=-1))
        weights = jnp.where(allowed, jnp.exp(scores - new_max[..., None]), 0.0)
        decay_rate = jnp.exp(run_max - new_max)
        new_sum = run_sum * decay_rate + jnp.sum(weights, axis=-1)
        new_acc = run_acc * decay_rate[..., None] + jnp.einsum(
            "qhk,khd->qhd",
            weights.astype(jnp.bfloat16),
            value_heads,
            preferred_element_type=jnp.float32,
        )
        return (new_max, new_sum, new_acc)

    run_max, run_sum, run_acc = lax.map(
        one_sequence,
        (
            queries,
            key_block,
            value_block,
            local_pos,
            key_place,
            start_state[0],
            start_state[1],
            start_state[2],
        ),
    )
    log_total = run_max + jnp.log(run_sum)
    attention = run_acc / run_sum[..., None]
    mixed_low = attention.astype(jnp.bfloat16).reshape(row_count, heads_width)
    attn_part = jnp.dot(mixed_low, out_weight, preferred_element_type=jnp.float32)
    pre_act = jnp.dot(ln_out, fc1_weight, preferred_element_type=jnp.float32) + fc1_bias
    activation = jax.nn.gelu(pre_act, approximate=True).astype(jnp.bfloat16)
    mlp_part = jnp.dot(activation, fc2_weight, preferred_element_type=jnp.float32)
    share_width = model_width // lax.axis_size("mp")
    first_col = lax.axis_index("mp") * share_width
    token_share = lax.dynamic_slice_in_dim(tokens_in, first_col, share_width, 1)
    attn_sum, mlp_sum = (
        lax.psum(attn_part.astype(jnp.bfloat16), "mp").astype(jnp.float32),
        lax.psum(mlp_part.astype(jnp.bfloat16), "mp").astype(jnp.float32),
    )
    attn_out = attn_sum + out_bias
    mlp_out = mlp_sum + fc2_bias
    block_out = (tokens_in + attn_out + mlp_out).astype(jnp.bfloat16)
    attn_share = lax.dynamic_slice_in_dim(attn_out, first_col, share_width, 1)
    mlp_share = lax.dynamic_slice_in_dim(mlp_out, first_col, share_width, 1)
    square_sums = lax.psum(
        (
            jnp.sum(token_share * token_share),
            jnp.sum(attn_share * attn_share),
            jnp.sum(mlp_share * mlp_share),
        ),
        ("dp", "ctx", "mp"),
    )
    cell_count = row_count * model_width * lax.axis_size("dp") * lax.axis_size("ctx")
    root_means = jnp.sqrt(jnp.stack(square_sums) / cell_count)
    back_weights = (
        lax.all_gather(norm_gain, ("dp", "ctx"), axis=0, tiled=True),
        lax.all_gather(w_qkv, ("dp", "ctx"), axis=0, tiled=True),
        lax.all_gather(w_out, ("dp", "ctx"), axis=1, tiled=True),
        lax.all_gather(w_fc1, ("dp", "ctx"), axis=0, tiled=True),
        lax.all_gather(w_fc2, ("dp", "ctx"), axis=1, tiled=True),
    )
    gain_back = back_weights[0].astype(jnp.float32)
    qkv_back = back_weights[1].reshape(model_width, 3 * heads_width)
    out_back = back_weights[2]
    fc1_back = back_weights[3]
    fc2_back = back_weights[4]
    grad_rows = grad_out.reshape(row_count, model_width)
    grad_float = grad_rows.astype(jnp.float32)
    grad_bias_out = jnp.sum(grad_float, axis=0)
    grad_out_weight = jnp.einsum(
        "tf,td->fd", mixed_low, grad_rows, preferred_element_type=jnp.float32
    )
    grad_fc2_weight = jnp.einsum(
        "tf,td->fd", activation, grad_rows, preferred_element_type=jnp.float32
    )
    grad_mixed = jnp.einsum(
        "td,fd->tf", grad_rows, out_back, preferred_element_type=jnp.float32
    ).astype(jnp.bfloat16)
    grad_act = jnp.einsum("td,fd->tf", grad_rows, fc2_back, preferred_element_type=jnp.float32)
    gelu_pull = jax.vjp(partial(jax.nn.gelu, approximate=True), pre_act)[1]
    grad_pre = gelu_pull(grad_act)[0].astype(jnp.bfloat16)
    grad_fc1_bias = jnp.sum(grad_pre.astype(jnp.float32), axis=0).reshape(hidden_width // HD, HD)
    grad_fc1_weight = jnp.einsum("td,tf->df", ln_out, grad_pre, preferred_element_type=jnp.float32)
    grad_heads = grad_mixed.reshape(seq_count, slot_count, head_count, HD)
    delta_rows = jnp.sum(grad_heads.astype(jnp.float32) * attention, axis=-1)
    keys_all, values_all = (
        lax.all_gather(keys_here, "ctx", axis=1, tiled=True),
        lax.all_gather(values_here, "ctx", axis=1, tiled=True),
    )
    total_slots = keys_all.shape[1]
    all_pos = slot_positions(group_order, 0, total_slots)

    def back_sequence(packed):
        query_seq, key_seq, value_seq, grad_seq, lse_seq, delta_seq, query_pos, key_pos = packed
        key_heads = key_seq.reshape(total_slots, head_count, HD)
        value_heads = value_seq.reshape(total_slots, head_count, HD)
        scores = (
            jnp.einsum("qhd,khd->qhk", query_seq, key_heads, preferred_element_type=jnp.float32)
            * score_scale
        )
        allowed = key_pos[None, None, :] <= query_pos[:, None, None]
        probs_exact = jnp.where(allowed, jnp.exp(scores - lse_seq[..., None]), 0.0)
        grad_probs = jnp.einsum(
            "qhd,khd->qhk", grad_seq, value_heads, preferred_element_type=jnp.float32
        )
        grad_scores = (probs_exact * (grad_probs - delta_seq[..., None])).astype(jnp.bfloat16)
        grad_query = (
            jnp.einsum("qhk,khd->qhd", grad_scores, key_heads, preferred_element_type=jnp.float32)
            * score_scale
        )
        grad_key = (
            jnp.einsum("qhk,qhd->khd", grad_scores, query_seq, preferred_element_type=jnp.float32)
            * score_scale
        )
        grad_value = jnp.einsum(
            "qhk,qhd->khd",
            probs_exact.astype(jnp.bfloat16),
            grad_seq,
            preferred_element_type=jnp.float32,
        )
        return (
            grad_query,
            grad_key.reshape(total_slots, heads_width),
            grad_value.reshape(total_slots, heads_width),
        )

    grad_query, grad_key_all, grad_value_all = lax.map(
        back_sequence,
        (queries, keys_all, values_all, grad_heads, log_total, delta_rows, local_pos, all_pos),
    )
    grad_key_home, grad_value_home = (
        lax.psum_scatter(
            grad_key_all.astype(jnp.bfloat16), "ctx", scatter_dimension=1, tiled=True
        ).astype(jnp.float32),
        lax.psum_scatter(
            grad_value_all.astype(jnp.bfloat16), "ctx", scatter_dimension=1, tiled=True
        ).astype(jnp.float32),
    )
    grad_query_pre = rotate(grad_query, cosine_table, -sine_table)
    grad_key_pre = rotate(
        grad_key_home.reshape(seq_count, slot_count, head_count, HD), cosine_table, -sine_table
    )
    grad_qkv = (
        jnp.stack(
            [
                grad_query_pre,
                grad_key_pre,
                grad_value_home.reshape(seq_count, slot_count, head_count, HD),
            ],
            axis=2,
        )
        .reshape(row_count, 3 * heads_width)
        .astype(jnp.bfloat16)
    )
    grad_qkv_bias = jnp.sum(grad_qkv.astype(jnp.float32), axis=0).reshape(3, head_count, HD)
    grad_qkv_weight = jnp.einsum(
        "td,tc->dc", ln_out, grad_qkv, preferred_element_type=jnp.float32
    ).reshape(model_width, 3, heads_width)
    grad_norm_part = jnp.einsum(
        "tc,dc->td", grad_qkv, qkv_back, preferred_element_type=jnp.float32
    ) + jnp.einsum("tf,df->td", grad_pre, fc1_back, preferred_element_type=jnp.float32)
    grad_norm = lax.psum(grad_norm_part.astype(jnp.bfloat16), "mp").astype(jnp.float32)
    grad_gain = jnp.sum(grad_norm * normed, axis=0)
    grad_shift = jnp.sum(grad_norm, axis=0)
    grad_scaled = grad_norm * gain_back
    grad_rows_in = grad_float + inv_std * (
        grad_scaled
        - jnp.mean(grad_scaled, axis=-1, keepdims=True)
        - normed * jnp.mean(grad_scaled * normed, axis=-1, keepdims=True)
    )
    grad_shards = (
        lax.psum_scatter(
            grad_gain.astype(jnp.bfloat16), ("dp", "ctx"), scatter_dimension=0, tiled=True
        ).astype(jnp.float32),
        lax.psum_scatter(
            grad_shift.astype(jnp.bfloat16), ("dp", "ctx"), scatter_dimension=0, tiled=True
        ).astype(jnp.float32),
        lax.psum_scatter(
            grad_qkv_weight.astype(jnp.bfloat16), ("dp", "ctx"), scatter_dimension=0, tiled=True
        ).astype(jnp.float32),
        lax.psum_scatter(
            grad_qkv_bias.astype(jnp.bfloat16), ("dp", "ctx"), scatter_dimension=2, tiled=True
        ).astype(jnp.float32),
        lax.psum_scatter(
            grad_out_weight.astype(jnp.bfloat16), ("dp", "ctx"), scatter_dimension=1, tiled=True
        ).astype(jnp.float32),
        lax.psum_scatter(
            grad_bias_out.astype(jnp.bfloat16), ("dp", "ctx"), scatter_dimension=0, tiled=True
        ).astype(jnp.float32),
        lax.psum_scatter(
            grad_fc1_weight.astype(jnp.bfloat16), ("dp", "ctx"), scatter_dimension=0, tiled=True
        ).astype(jnp.float32),
        lax.psum_scatter(
            grad_fc1_bias.astype(jnp.bfloat16), ("dp", "ctx"), scatter_dimension=1, tiled=True
        ).astype(jnp.float32),
        lax.psum_scatter(
            grad_fc2_weight.astype(jnp.bfloat16), ("dp", "ctx"), scatter_dimension=1, tiled=True
        ).astype(jnp.float32),
        lax.psum_scatter(
            grad_bias_out.astype(jnp.bfloat16), ("dp", "ctx"), scatter_dimension=0, tiled=True
        ).astype(jnp.float32),
    )
    return (
        block_out.reshape(seq_count, slot_count, model_width),
        grad_rows_in.reshape(seq_count, slot_count, model_width),
        grad_shards[0],
        grad_shards[1],
        grad_shards[2],
        grad_shards[3],
        grad_shards[4],
        grad_shards[5],
        grad_shards[6],
        grad_shards[7],
        grad_shards[8],
        grad_shards[9],
        root_means,
    )


def solution(mesh):
    return jax.shard_map(
        on_device,
        mesh=mesh,
        in_specs=(
            P("dp", "ctx", None),
            P("dp", None),
            P("dp", "ctx", None),
            P(("dp", "ctx")),
            P(("dp", "ctx")),
            P(("dp", "ctx"), None, "mp"),
            P(None, "mp", ("dp", "ctx")),
            P("mp", ("dp", "ctx")),
            P(("dp", "ctx")),
            P(("dp", "ctx"), "mp"),
            P("mp", ("dp", "ctx")),
            P("mp", ("dp", "ctx")),
            P(("dp", "ctx")),
        ),
        out_specs=(
            P("dp", "ctx", None),
            P("dp", "ctx", None),
            P(("dp", "ctx")),
            P(("dp", "ctx")),
            P(("dp", "ctx"), None, "mp"),
            P(None, "mp", ("dp", "ctx")),
            P("mp", ("dp", "ctx")),
            P(("dp", "ctx")),
            P(("dp", "ctx"), "mp"),
            P("mp", ("dp", "ctx")),
            P("mp", ("dp", "ctx")),
            P(("dp", "ctx")),
            P(),
        ),
        check_vma=False,
    )
```

profile of v0, /device:TPU:0, one launch (start us, length us, event | category | flops | bytes accessed | tf_op | source)
XLA Modules:
  0.0 2299.9 jit_solution(16866031071761609584)
XLA Ops:
  10.4 34.1 %all-gather = bf16[16,1,128]{2,1,0:T(2,128)(2,1)S(1)} all-gather(bf16[1,1,128]{2,1,0:T(2,128)(2,1)} %bitcast.326), channel_id=1, replica_groups=mesh['dp'=4,'ctx'=4,'mp'=2] {'dp','ctx'}, dimensions={0}, use_global_device_ids=true | all-gather | bytes 4352 | tf_op jit(solution)/shard_map/all_gather | solution.py:67
  44.5 33.7 %all-gather.1 = bf16[16,1,128]{2,1,0:T(2,128)(2,1)S(1)} all-gather(bf16[1,1,128]{2,1,0:T(2,128)(2,1)} %bitcast.327), channel_id=1, replica_groups=mesh['dp'=4,'ctx'=4,'mp'=2] {'dp','ctx'}, dimensions={0}, use_global_device_ids=true | all-gather | bytes 4352 | tf_op jit(solution)/shard_map/all_gather | solution.py:68
  78.9 34.5 %all_gather.46 = bf16[3,16,64]{1,0,2:T(4,128)(2,1)S(1)} all-gather(bf16[3,16,4]{1,0,2:T(4,128)(2,1)S(1)} %copy.116), channel_id=1, replica_groups=mesh['dp'=4,'ctx'=4,'mp'=2] {'dp','ctx'}, dimensions={2}, use_global_device_ids=true | all-gather | bytes 6528 | tf_op jit(solution)/shard_map/all_gather | solution.py:70
  228.8 116.9 %all-gather.14.cloned.1.call-done = bf16[2,2048,1024]{1,2,0:T(8,128)(2,1)} async-done(((bf16[2,512,1024]{1,2,0:T(8,128)(2,1)}), bf16[2,2048,1024]{1,2,0:T(8,128)(2,1)}) %all-gather.14.cloned.1.call-update) | async-done | bytes 8388624 | tf_op jit(solution)/shard_map/all_gather | solution.py:126
  345.7 149.9 %all-gather.16.cloned.1.call-done = bf16[2,2048,1024]{1,2,0:T(8,128)(2,1)} async-done(((bf16[2,512,1024]{1,2,0:T(8,128)(2,1)}), bf16[2,2048,1024]{1,2,0:T(8,128)(2,1)}) %all-gather.16.cloned.1.call-update) | async-done | bytes 8388624 | tf_op jit(solution)/shard_map/all_gather | solution.py:127
  499.3 250.1 %while.28 = (s32[]{:T(128)}, f32[2,512,16]{1,2,0:T(8,128)S(1)}, f32[2,512,16]{1,2,0:T(8,128)S(1)}, f32[2,512,16,64]{1,0,3,2:T(2,128)}, s32[2,2048]{1,0:T(2,128)S...) while((s32[]{:T(128)}, f32[2,512,16]{1,2,0:T(8,128)S(1)}, ...), condition=%wide.region_7.8_spmd, body=%wide.region_4.7_spmd.sunk | while | flops 4481130496 | bytes 242645648 | solution.py:152
  564.5 38.1 %dynamic_update_slice.30 = f32[2,512,16,64]{1,0,3,2:T(2,128)} dynamic-update-slice(f32[2,512,16,64]{1,0,3,2:T(2,128)} %get-tuple-element.545, f32[1,512,16,64]{1,0,3,2:T(1,128)S(1)} %copy.173, s32[]{:T(128)} %get-tuple-element.542, s32[]{:T(128)} %constant.141.clone.1..sunk, s32[]{:T(128)} %constant.141.clone.1..sunk, s32[]{:T(128)} %constant.141.clone.1..sunk) | dynamic-update-slice | bytes 4194308 | tf_op jit(solution)/shard_map/while/body/jit(dynamic_update_index_in_dim)/dynamic_update_slice | solution.py:152
  689.5 38.1 %dynamic_update_slice.30 = f32[2,512,16,64]{1,0,3,2:T(2,128)} dynamic-update-slice(f32[2,512,16,64]{1,0,3,2:T(2,128)} %get-tuple-element.545, f32[1,512,16,64]{1,0,3,2:T(1,128)S(1)} %copy.173, s32[]{:T(128)} %get-tuple-element.542, s32[]{:T(128)} %constant.141.clone.1..sunk, s32[]{:T(128)} %constant.141.clone.1..sunk, s32[]{:T(128)} %constant.141.clone.1..sunk) | dynamic-update-slice | bytes 4194308 | tf_op jit(solution)/shard_map/while/body/jit(dynamic_update_index_in_dim)/dynamic_update_slice | solution.py:152
  759.9 354.3 %while.29 = (s32[]{:T(128)}, f32[2,512,16,64]{1,0,3,2:T(2,128)}, bf16[2,2048,1024]{1,2,0:T(8,128)(2,1)}, bf16[2,2048,1024]{1,2,0:T(8,128)(2,1)}, bf16[2,2048,102...) while((s32[]{:T(128)}, f32[2,512,16,64]{1,0,3,2:T(2,128)}, ...), condition=%wide.region_12.13_spmd, body=%wide.region_11.12_spmd.sunk | while | flops 10910957568 | bytes 416613056 | solution.py:266
  789.8 38.9 %fusion.150 = bf16[512,16,2048]{0,2,1:T(8,128)(2,1)} fusion(f32[16,2048,512]{2,1,0:T(8,128)} %fusion.149, f32[512,16]{0,1:T(8,128)S(1)} %bitcast.305, f32[512,16]{0,1:T(8,128)S(1)} %dynamic-slice_bitcast_fusion.2, pred[512,2048]{0,1:T(8,128)(4,1)S(1)} %broadcast_compare_fusion.5, bf16[2048,16,64]{0,2,1:T(8,128)(2,1)S(1)} %bitcast.280, ...), kind=kOutput, calls=%fused_computation.32.clone.2 | convolution fusion | flops 2248146944 | bytes 107020800 | tf_op jit(solution)/shard_map/while/body/eval_jaxpr/qhd,khd->qhk/dot_general | solution.py:242
  899.1 38.0 %dynamic_update_slice.32 = f32[2,512,16,64]{1,0,3,2:T(2,128)} dynamic-update-slice(f32[2,512,16,64]{1,0,3,2:T(2,128)} %get-tuple-element.579, f32[1,512,16,64]{1,0,3,2:T(1,128)} %copy.175, s32[]{:T(128)} %get-tuple-element.578, s32[]{:T(128)} %constant.141.clone.1..sunk.1, s32[]{:T(128)} %constant.141.clone.1..sunk.1, s32[]{:T(128)} %constant.141.clone.1..sunk.1) | dynamic-update-slice | bytes 4194308 | tf_op jit(solution)/shard_map/while/body/jit(dynamic_update_index_in_dim)/dynamic_update_slice | solution.py:152
  966.7 38.9 %fusion.150 = bf16[512,16,2048]{0,2,1:T(8,128)(2,1)} fusion(f32[16,2048,512]{2,1,0:T(8,128)} %fusion.149, f32[512,16]{0,1:T(8,128)S(1)} %bitcast.305, f32[512,16]{0,1:T(8,128)S(1)} %dynamic-slice_bitcast_fusion.2, pred[512,2048]{0,1:T(8,128)(4,1)S(1)} %broadcast_compare_fusion.5, bf16[2048,16,64]{0,2,1:T(8,128)(2,1)S(1)} %bitcast.280, ...), kind=kOutput, calls=%fused_computation.32.clone.2 | convolution fusion | flops 2248146944 | bytes 107020800 | tf_op jit(solution)/shard_map/while/body/eval_jaxpr/qhd,khd->qhk/dot_general | solution.py:242
  1076.0 38.0 %dynamic_update_slice.32 = f32[2,512,16,64]{1,0,3,2:T(2,128)} dynamic-update-slice(f32[2,512,16,64]{1,0,3,2:T(2,128)} %get-tuple-element.579, f32[1,512,16,64]{1,0,3,2:T(1,128)} %copy.175, s32[]{:T(128)} %get-tuple-element.578, s32[]{:T(128)} %constant.141.clone.1..sunk.1, s32[]{:T(128)} %constant.141.clone.1..sunk.1, s32[]{:T(128)} %constant.141.clone.1..sunk.1) | dynamic-update-slice | bytes 4194308 | tf_op jit(solution)/shard_map/while/body/jit(dynamic_update_index_in_dim)/dynamic_update_slice | solution.py:152
  1115.1 29.4 %all-gather.3 = bf16[16,4,64]{2,1,0:T(4,128)(2,1)S(1)} all-gather(bf16[1,4,64]{2,1,0:T(4,128)(2,1)S(1)} %bitcast.325), channel_id=1, replica_groups=mesh['dp'=4,'ctx'=4,'mp'=2] {'dp','ctx'}, dimensions={0}, use_global_device_ids=true | all-gather | bytes 8704 | tf_op jit(solution)/shard_map/all_gather | solution.py:74
  1187.4 29.9 %convolution_convert_fusion = bf16[4096,2048]{1,0:T(8,128)(2,1)} fusion(bf16[1024,2048]{1,0:T(8,128)(2,1)} %bitcast.284, f32[1024,4096]{1,0:T(8,128)} %fusion.78, f32[4096]{0:T(1024)S(1)} %reshape.446), kind=kOutput, calls=%fused_computation.76 | convolution fusion | flops 17230200832 | bytes 37765120 | tf_op jit(solution)/shard_map/tf,td->fd/dot_general | solution.py:212
  1238.2 34.9 %fusion.74 = (bf16[4096]{0:T(1024)(128)(2,1)}, bf16[1024,4096]{1,0:T(8,128)(2,1)}) fusion(f32[1024,4096]{1,0:T(8,128)} %fusion.78, f32[4096]{0:T(1024)S(1)} %reshape.446, bf16[1024,2048]{1,0:T(8,128)(2,1)} %bitcast.285, bf16[4096,2048]{1,0:T(8,128)(2,1)} %all-gather.22.cloned.1.call-done), kind=kOutput, calls=%fused_computation.173 | convolution fusion | flops 17272139776 | bytes 46161920 | tf_op jit(solution)/shard_map/td,fd->tf/dot_general | solution.py:218
  1341.5 63.1 %reduce-scatter.15.cloned.1.call-done = bf16[2,512,1024]{1,2,0:T(8,128)(2,1)} async-done(((bf16[2,2048,1024]{1,2,0:T(8,128)(2,1)}), bf16[2,512,1024]{1,2,0:T(8,128)(2,1)}) %reduce-scatter.15.cloned.1.call-update) | async-done | bytes 2097168 | tf_op jit(solution)/shard_map/reduce_scatter | solution.py:274
  1418.0 32.4 %fusion.76 = (bf16[3,16,64]{2,1,0:T(8,128)(2,1)S(1)}, bf16[2,512,3,16,64]{1,0,4,3,2:T(2,128)(2,1)S(1)}) fusion(bf16[2,512,1,16,64]{1,0,4,3,2:T(2,128)(2,1)S(1)} %bitcast.290, bf16[2,512,1,16,64]{1,0,4,3,2:T(2,128)(2,1)S(1)} %maximum_bitcast_fusion.1, bf16[2,512,1,16,64]{1,0,4,3,2:T(2,128)(2,1)S(1)} %maximum_bitcast_fusion), kind=kLoop, calls=%fused_computation.174 | loop fusion | flops 9434112 | bytes 12589056 | tf_op jit(solution)/shard_map/reduce_sum | solution.py:294
  1518.5 33.1 %all-gather.2 = bf16[16,1,128]{2,1,0:T(2,128)(2,1)S(1)} all-gather(bf16[1,1,128]{2,1,0:T(2,128)(2,1)S(1)} %bitcast.328), channel_id=1, replica_groups=mesh['dp'=4,'ctx'=4,'mp'=2] {'dp','ctx'}, dimensions={0}, use_global_device_ids=true | all-gather | bytes 4352 | tf_op jit(solution)/shard_map/all_gather | solution.py:72
  1592.9 71.5 %reduce-scatter.23.cloned.1.call-done = bf16[128,4096]{1,0:T(8,128)(2,1)} async-done(((bf16[2048,4096]{1,0:T(8,128)(2,1)}), bf16[128,4096]{1,0:T(8,128)(2,1)}) %reduce-scatter.23.cloned.1.call-update) | async-done | bytes 1048592
  1667.6 179.0 %reduce-scatter.19.cloned.1.call-done = bf16[128,4096]{1,0:T(8,128)(2,1)} async-done(((bf16[2048,4096]{1,0:T(8,128)(2,1)}), bf16[128,4096]{1,0:T(8,128)(2,1)}) %reduce-scatter.19.cloned.1.call-update) | async-done | bytes 1048592 | tf_op jit(solution)/shard_map/reduce_scatter | solution.py:329
  1849.4 289.1 %all-reduce.10.cloned.1.call-done = (bf16[1024,2048]{1,0:T(8,128)(2,1)}, bf16[1024,2048]{1,0:T(8,128)(2,1)}, bf16[1024,2048]{1,0:T(8,128)(2,1)}) async-done(((bf16[1024,2048]{1,0:T(8,128)(2,1)}, bf16[1024,2048]{1,0:T(8,128)(2,1)}, bf16[1024,2048]{1,0:T(8,128)(2,1)}), (bf16[1024,2048]{1,0:T(8,128)(2,1)}, bf16[1024,2048]{1,0:T(8,128)(2,1)}, bf16[1024,2048]{1,0:T(8,128)(2,1)})) %all-reduce.10.cloned.1.call-update) | async-done | bytes 12582928 | tf_op jit(solution)/shard_map/psum | solution.py:176
  2173.7 44.5 %all-reduce.5 = (f32[1]{0:T(128)}, f32[1]{0:T(128)}, f32[1]{0:T(128)}) all-reduce(f32[1]{0:T(128)} %bitcast.57, f32[1]{0:T(128)} %bitcast.56, f32[1]{0:T(128)} %bitcast.55), channel_id=1, replica_groups=mesh['dp'=4,'ctx'=4,'mp'=2] {'dp','ctx','mp'}, use_global_device_ids=true, to_apply=%region_37.38 | all-reduce | flops 3 | bytes 24 | tf_op jit(solution)/shard_map/psum | solution.py:184
  2221.0 64.1 %all-reduce.6 = (bf16[2048]{0:T(1024)(128)(2,1)S(1)}, bf16[2048]{0:T(1024)(128)(2,1)S(1)}, bf16[3,16,64]{1,2,0:T(8,128)(2,1)S(1)}, bf16[2048]{0:T(1024)(128)(2,1)S(1)}, bf16[64,64]{1,0:T(8,128)(2,1)S(1)}) all-reduce(bf16[2048]{0:T(1024)(128)(2,1)S(1)} %get-tuple-element.280, ...), channel_id=4, replica_groups=mesh['dp'=4,'ctx'=4,'mp'=2] {'dp','ctx'}, use_global_device_ids=true, to_apply=%region_19.20.clone | all-reduce | flops 13312 | bytes 53248
  (263 shorter events, 812.8 us)
Async XLA Ops:
  7.2 120.7 %all-gather.12.cloned.1.call-start = ((), (), s32[]{:S(2)}) async-start(), calls=%async_computation.6 | async-start | bytes 13369344 | tf_op jit(solution)/shard_map/all_gather | solution.py:69
  9.5 195.5 %all-gather.18.cloned.1.call-start = ((), (), s32[]{:S(2)}) async-start(), calls=%async_computation.9 | async-start | bytes 4456448 | tf_op jit(solution)/shard_map/all_gather | solution.py:71
  10.3 335.4 %all-gather.14.cloned.1.call-start = ((), (), s32[]{:S(2)}) async-start(), calls=%async_computation.7 | async-start | bytes 10485760 | tf_op jit(solution)/shard_map/all_gather | solution.py:126
  44.4 83.4 %copy-start.15 = (f32[16,1,128]{2,1,0:T(1,128)}, f32[16,1,128]{2,1,0:T(1,128)S(1)}, u32[]{:S(2)}) copy-start(f32[16,1,128]{2,1,0:T(1,128)S(1)} %convert_element_type.253) | copy-start | bytes 24580
  78.2 49.7 %copy-start.18 = (f32[16,1,128]{2,1,0:T(1,128)}, f32[16,1,128]{2,1,0:T(1,128)S(1)}, u32[]{:S(2)}) copy-start(f32[16,1,128]{2,1,0:T(1,128)S(1)} %convert_element_type.254) | copy-start | bytes 24580
  124.8 64.5 %copy-start.12 = (f32[2,512,16]{1,0,2:T(2,128)}, f32[2,512,16]{1,0,2:T(2,128)S(1)}, u32[]{:S(2)}) copy-start(f32[2,512,16]{1,0,2:T(2,128)S(1)} %get-tuple-element.374) | copy-start | bytes 196612
  197.9 297.7 %all-gather.16.cloned.1.call-start = ((), (), s32[]{:S(2)}) async-start(), calls=%async_computation.8 | async-start | bytes 10485760 | tf_op jit(solution)/shard_map/all_gather | solution.py:127
  203.5 960.4 %all-gather.20.cloned.1.call-start = ((), (), s32[]{:S(2)}) async-start(), calls=%async_computation.10 | async-start | bytes 17825792 | tf_op jit(solution)/shard_map/all_gather | solution.py:73
  204.1 1034.1 %all-gather.22.cloned.1.call-start = ((), (), s32[]{:S(2)}) async-start(), calls=%async_computation.11 | async-start | bytes 17825792 | tf_op jit(solution)/shard_map/all_gather | solution.py:75
  204.7 1130.1 %reduce-scatter.13.cloned.1.call-start = ((), (), s32[]{:S(2)}) async-start(), calls=%async_computation.12 | async-start | bytes 10485760 | tf_op jit(solution)/shard_map/reduce_scatter | solution.py:271
  219.6 279.7 %copy-start.3 = (bf16[2,512,16,64]{1,0,3,2:T(2,128)(2,1)}, bf16[2,512,16,64]{1,0,3,2:T(2,128)(2,1)S(1)}, u32[]{:S(2)}) copy-start(bf16[2,512,16,64]{1,0,3,2:T(2,128)(2,1)S(1)} %reshape.441) | copy-start | bytes 6291460
  1114.2 290.4 %reduce-scatter.15.cloned.1.call-start = ((), (), s32[]{:S(2)}) async-start(), calls=%async_computation.13 | async-start | bytes 10485760 | tf_op jit(solution)/shard_map/reduce_scatter | solution.py:274
  1115.0 475.9 %reduce-scatter.21.cloned.1.call-start = ((), (), s32[]{:S(2)}) async-start(), calls=%async_computation.16 | async-start | bytes 4456448
  1115.0 42.4 %copy-start.20 = (f32[1,4,2,128]{3,1,2,0:T(4,128)}, f32[1,4,2,128]{3,1,2,0:T(4,128)S(1)}, u32[]{:S(2)}) copy-start(f32[1,4,2,128]{3,1,2,0:T(4,128)S(1)} %copy.166) | copy-start | bytes 12292
  1163.8 500.6 %reduce-scatter.23.cloned.1.call-start = ((), (), s32[]{:S(2)}) async-start(), calls=%async_computation.17 | async-start | bytes 17825792
  1238.1 608.5 %reduce-scatter.19.cloned.1.call-start = ((), (), s32[]{:S(2)}) async-start(), calls=%async_computation.15 | async-start | bytes 17825792 | tf_op jit(solution)/shard_map/reduce_scatter | solution.py:329
  1297.0 841.5 %all-reduce.10.cloned.1.call-start = ((), (), s32[]{:S(2)}) async-start(), calls=%async_computation.18 | async-start | bytes 25165824 | tf_op jit(solution)/shard_map/psum | solution.py:176
  1334.7 73.6 %copy-start.13 = (f32[2,512,16]{1,0,2:T(2,128)S(1)}, f32[2,512,16]{1,0,2:T(2,128)}, u32[]{:S(2)}) copy-start(f32[2,512,16]{1,0,2:T(2,128)} %copy-done.12) | copy-start | bytes 196612
  1334.7 73.6 %copy-start.14 = (f32[2,512,16]{1,0,2:T(2,128)S(1)}, f32[2,512,16]{1,0,2:T(2,128)}, u32[]{:S(2)}) copy-start(f32[2,512,16]{1,0,2:T(2,128)} %get-tuple-element.372) | copy-start | bytes 196612
  1496.5 793.8 %reduce-scatter.17.cloned.1.call-start = ((), (), s32[]{:S(2)}) async-start(), calls=%async_computation.14 | async-start | bytes 13369344 | tf_op jit(solution)/shard_map/reduce_scatter | solution.py:317
  1517.8 65.9 %copy-start.32 = (u32[32]{0:T(128)S(1)}, u32[32]{0:T(128)}, u32[]{:S(2)}) copy-start(u32[32]{0:T(128)} %constant.172) | copy-start | bytes 388
  1589.0 549.4 %copy-start.17 = (f32[16,1,128]{2,1,0:T(1,128)S(1)}, f32[16,1,128]{2,1,0:T(1,128)}, u32[]{:S(2)}) copy-start(f32[16,1,128]{2,1,0:T(1,128)} %copy-done.15) | copy-start | bytes 24580
  1589.1 549.4 %copy-start.21 = (f32[1,4,2,128]{3,1,2,0:T(4,128)S(1)}, f32[1,4,2,128]{3,1,2,0:T(4,128)}, u32[]{:S(2)}) copy-start(f32[1,4,2,128]{3,1,2,0:T(4,128)} %copy-done.20) | copy-start | bytes 12292
  1589.1 549.4 %copy-start.23 = (f32[1,4,2,128]{3,1,2,0:T(4,128)S(1)}, f32[1,4,2,128]{3,1,2,0:T(4,128)}, u32[]{:S(2)}) copy-start(f32[1,4,2,128]{3,1,2,0:T(4,128)} %copy-done.22) | copy-start | bytes 12292
  (28 other events, 506.1 us)
Sparse Core Ops, SparseCore 0:
  10.7 107.4 all-gather.11
  120.3 51.3 all-gather.17
  198.0 147.6 all-gather.13
  347.7 147.8 all-gather.15
  497.6 125.0 all-gather.19
  624.6 128.5 all-gather.21
  1114.3 142.6 reduce-scatter.12
  1259.4 145.1 reduce-scatter.14
  1408.4 73.3 reduce-scatter.20
  1486.4 177.9 reduce-scatter.22
  1669.1 177.5 reduce-scatter.18
  1850.0 288.4 all-reduce.9
  2143.1 138.2 reduce-scatter.16
where the time goes:
time: 2320 us; the launch traced here: 2300 us
  waiting for transfers between devices  872 us (38%)
  matrix products  598 us (26%)
  local copies, waits for them, and re-layouts  326 us (14%)
  blocking collectives  303 us (13%)
  other arithmetic  183 us (8%)
    psum x1, waiting for transfers between devices, on_device(): lax.psum(attn_part.astype(jnp.bfloat16), 'mp').astype(jnp.float32)  289 us
    reduce_scatter x1, waiting for transfers between devices, on_device(): lax.psum_scatter(grad_fc1_weight.astype(jnp.bfloat16), ('dp', 'ctx'), sca...  179 us
    dynamic_update_slice x8, local copies, waits for them, and re-layouts, on_device(): lax.map(one_sequence, (queries, key_block, value_block, local_pos, key_pl...  167 us
    all_gather x1, waiting for transfers between devices, on_device(): value_block = lax.all_gather(values_here, 'ctx', axis=1, tiled=True)  150 us
    all_gather x1, waiting for transfers between devices, on_device(): key_block = lax.all_gather(keys_here, 'ctx', axis=1, tiled=True)  117 us
    dot_general x2, matrix products, back_sequence(): jnp.einsum('qhd,khd->qhk', grad_seq, value_heads, preferred_element_type=...  77.8 us
    unnamed x15, waiting for transfers between devices  74.1 us
    unnamed x1, blocking collectives  64.1 us
  transfers between devices with their start and end apart: 13, of which 6 were waited for; matrix products, arithmetic and copies ran while one was open for 48% of the time, Pallas kernels for 0%

commit v1 on v0

v1 whole, which is shorter than its diff:
```python
from functools import partial

import jax
import jax.numpy as jnp
from jax import lax
from jax.experimental import pallas as pl
from jax.experimental.pallas import tpu as pltpu
from jax.sharding import PartitionSpec as P

HD = 64
ROT = 32
SEQ_LEN = 2048
PAIR = 2 * HD
TILE = 256

norm_eps = 1e-05
rotary_base = 10000.0
masked_fill = -1e30
low = jnp.bfloat16
wide = jnp.float32


def rotary_rows(seq):
    half = ROT // 2
    lane = jnp.arange(PAIR, dtype=jnp.int32)[None, :] % HD
    inverse = jnp.power(rotary_base, -(lane % half).astype(wide) * (2.0 / ROT))
    angles = jnp.arange(seq, dtype=wide)[:, None] * inverse
    cosine, sine = jnp.cos(angles), jnp.sin(angles)
    return (
        jnp.where(lane < ROT, cosine, 1.0),
        jnp.where(lane < half, -sine, 0.0),
        jnp.where((lane >= half) & (lane < ROT), sine, 0.0),
    )


def attention_kernel(
    order_ref, qkv_ref, do_ref, cos_ref, up_ref, down_ref, mixed_ref, grad_ref,
    sorted_qkv, sorted_do, q_nat, k_nat, v_nat, do_nat, q_t, k_t, v_t, do_t,
    s_ref, dk_acc, dv_acc, out_s, grad_s, *, pieces, piece,
):
    blocks = pieces * piece // TILE
    scale = HD**-0.5
    dot = partial(jnp.dot, preferred_element_type=wide)

    def rows_of(b):
        return pl.ds(pl.multiple_of(b * TILE, TILE), TILE)

    def fold(t, how):
        return how(t.reshape(TILE // 8, 8, TILE), axis=0)

    def gather(r, _):
        src = pl.multiple_of(order_ref[r] * piece, piece)
        dst = pl.multiple_of(r * piece, piece)
        sorted_qkv[pl.ds(dst, piece), :] = qkv_ref[pl.ds(src, piece), :]
        sorted_do[pl.ds(dst, piece), :] = do_ref[pl.ds(src, piece), :]
        return 0

    lax.fori_loop(0, pieces, gather, 0)
    first = lax.broadcasted_iota(jnp.int32, (TILE, PAIR), 1) < HD

    def turn(t, rows, sign):
        up = pltpu.roll(t, PAIR - ROT // 2, 1) * up_ref[rows, :]
        down = pltpu.roll(t, ROT // 2, 1) * down_ref[rows, :]
        return t * cos_ref[rows, :] + sign * (up + down)

    def prepare(b, _):
        rows = rows_of(b)
        q = turn(sorted_qkv[rows, 0:PAIR], rows, 1.0).astype(low).astype(wide) * scale
        k = turn(sorted_qkv[rows, PAIR : 2 * PAIR], rows, 1.0)
        v = sorted_qkv[rows, 2 * PAIR : 3 * PAIR]
        g = sorted_do[rows, :].astype(wide)
        for val, nat, tr in ((q, q_nat, q_t), (k, k_nat, k_t), (v, v_nat, v_t), (g, do_nat, do_t)):
            nat[0, b] = jnp.where(first, val, 0.0).astype(low)
            nat[1, b] = jnp.where(first, 0.0, val).astype(low)
            tr[b] = val.T.astype(low)
        dk_acc[b] = jnp.zeros((TILE, PAIR), wide)
        dv_acc[b] = jnp.zeros((TILE, PAIR), wide)
        return 0

    lax.fori_loop(0, blocks, prepare, 0)
    key_row = lax.broadcasted_iota(jnp.int32, (TILE, TILE), 0)
    query_col = lax.broadcasted_iota(jnp.int32, (TILE, TILE), 1)
    allowed = key_row <= query_col

    def one_block(i, _):
        q_i = q_t[i]
        do_i = do_t[i]

        def score(j, tops):
            new = []
            for h in range(2):
                s = dot(k_nat[h, j], q_i)
                s_ref[h, j] = s
                new.append(jnp.maximum(tops[h], fold(s, jnp.max)))
            return tuple(new)

        partial_tops = lax.fori_loop(
            0, i, score, (jnp.full((8, TILE), masked_fill, wide),) * 2
        )
        tops = []
        for h in range(2):
            s = jnp.where(allowed, dot(k_nat[h, i], q_i), masked_fill)
            s_ref[h, i] = s
            tops.append(
                jnp.max(jnp.maximum(partial_tops[h], fold(s, jnp.max)), axis=0, keepdims=True)
            )

        def weigh(j, carry):
            sums, accs = carry
            new_sums, new_accs = [], []
            for h in range(2):
                p = jnp.exp(s_ref[h, j] - tops[h])
                s_ref[h, j] = p
                new_sums.append(sums[h] + fold(p, jnp.sum))
                new_accs.append(accs[h] + dot(v_t[j, h * HD : (h + 1) * HD, :], p.astype(low)))
            return tuple(new_sums), tuple(new_accs)

        sums, accs = lax.fori_loop(
            0,
            i + 1,
            weigh,
            ((jnp.zeros((8, TILE), wide),) * 2, (jnp.zeros((HD, TILE), wide),) * 2),
        )
        invs, deltas, outs = [], [], []
        for h in range(2):
            inv = 1.0 / jnp.sum(sums[h], axis=0, keepdims=True)
            o = accs[h] * inv
            outs.append(o)
            invs.append(inv)
            g = do_i[h * HD : (h + 1) * HD, :].astype(wide)
            deltas.append(jnp.sum(o * g, axis=0, keepdims=True))
        out_s[i] = jnp.concatenate(outs, axis=0).T.astype(low)

        def pull(j, dq):
            new = []
            dv = dk = None
            for h in range(2):
                dp = dot(v_nat[h, j], do_i)
                p = s_ref[h, j] * invs[h]
                ds = (p * (dp - deltas[h])).astype(low)
                dv_h = dot(p.astype(low), do_nat[h, i])
                dk_h = dot(ds, q_nat[h, i])
                dv = dv_h if dv is None else dv + dv_h
                dk = dk_h if dk is None else dk + dk_h
                new.append(dq[h] + dot(k_t[j, h * HD : (h + 1) * HD, :], ds))
            dv_acc[j] += dv
            dk_acc[j] += dk
            return tuple(new)

        dq = lax.fori_loop(0, i + 1, pull, (jnp.zeros((HD, TILE), wide),) * 2)
        rows = rows_of(i)
        dq_rows = jnp.concatenate(dq, axis=0).T * scale
        grad_s[rows, 0:PAIR] = turn(dq_rows, rows, -1.0).astype(low)
        return 0

    lax.fori_loop(0, blocks, one_block, 0)

    def finish(b, _):
        rows = rows_of(b)
        grad_s[rows, PAIR : 2 * PAIR] = turn(dk_acc[b], rows, -1.0).astype(low)
        grad_s[rows, 2 * PAIR : 3 * PAIR] = dv_acc[b].astype(low)
        sorted_do[rows, :] = out_s[b]
        return 0

    lax.fori_loop(0, blocks, finish, 0)

    def scatter(r, _):
        src = pl.multiple_of(order_ref[r] * piece, piece)
        dst = pl.multiple_of(r * piece, piece)
        mixed_ref[pl.ds(src, piece), :] = sorted_do[pl.ds(dst, piece), :]
        grad_ref[pl.ds(src, piece), :] = grad_s[pl.ds(dst, piece), :]
        return 0

    lax.fori_loop(0, pieces, scatter, 0)


def attention(order, qkv, grad_mixed):
    seq, width = grad_mixed.shape
    pairs = width // PAIR
    pieces = order.shape[0]
    blocks = seq // TILE
    vmem = pltpu.VMEM
    table = pl.BlockSpec((seq, PAIR), lambda p, o: (0, 0))
    one = pl.BlockSpec((seq, PAIR), lambda p, o: (0, p))
    three = pl.BlockSpec((seq, 3 * PAIR), lambda p, o: (0, p))
    return pl.pallas_call(
        partial(attention_kernel, pieces=pieces, piece=seq // pieces),
        grid_spec=pltpu.PrefetchScalarGridSpec(
            num_scalar_prefetch=1,
            grid=(pairs,),
            in_specs=[three, one, table, table, table],
            out_specs=[one, three],
            scratch_shapes=[
                vmem((seq, 3 * PAIR), wide),
                vmem((seq, PAIR), low),
                *[vmem((2, blocks, TILE, PAIR), low)] * 4,
                *[vmem((blocks, PAIR, TILE), low)] * 4,
                vmem((2, blocks, TILE, TILE), wide),
                vmem((blocks, TILE, PAIR), wide),
                vmem((blocks, TILE, PAIR), wide),
                vmem((blocks, TILE, PAIR), low),
                vmem((seq, 3 * PAIR), low),
            ],
        ),
        out_shape=[
            jax.ShapeDtypeStruct((seq, width), low),
            jax.ShapeDtypeStruct((seq, 3 * width), low),
        ],
        compiler_params=pltpu.CompilerParams(
            vmem_limit_bytes=48 * 1024 * 1024, dimension_semantics=("arbitrary",)
        ),
        cost_estimate=pl.CostEstimate(
            flops=pairs * 24 * seq * seq * PAIR, bytes_accessed=30_000_000, transcendentals=0
        ),
        name="attention",
    )(order, qkv, grad_mixed, *rotary_rows(seq))


def mm(a, b):
    return jnp.dot(a, b, preferred_element_type=wide)


def mm_nt(a, b):
    return lax.dot_general(a, b, (((1,), (1,)), ((), ())), preferred_element_type=wide)


def mm_tn(a, b):
    return lax.dot_general(a, b, (((0,), (0,)), ((), ())), preferred_element_type=wide)


def on_device(
    tokens,
    group_order,
    grad_out,
    norm_gain,
    norm_bias,
    w_qkv,
    b_qkv,
    w_out,
    b_out,
    w_fc1,
    b_fc1,
    w_fc2,
    b_fc2,
):
    n_dp, n_ctx, n_mp = lax.axis_size("dp"), lax.axis_size("ctx"), lax.axis_size("mp")
    n_seq, n_slot, model = tokens.shape
    groups = group_order.shape[1]
    assert n_dp == 4 and 2 * n_seq == n_ctx == 4
    dp, z, y = lax.axis_index("dp"), lax.axis_index("ctx"), lax.axis_index("mp")
    x, c = dp // 2, dp % 2
    half = model // 2
    part = n_slot // (2 * n_mp)
    rows_own = n_ctx * part
    block_len = SEQ_LEN // groups

    def to_core(v):
        return lax.ppermute(v, "dp", [(i, i ^ 1) for i in range(n_dp)])

    def to_x(v):
        return lax.ppermute(v, "dp", [(i, i ^ 2) for i in range(n_dp)])

    def by_core(mine, other, axis):
        return jnp.where(
            c == 0,
            jnp.concatenate([mine, other], axis),
            jnp.concatenate([other, mine], axis),
        )

    def roll_x(v):
        return jnp.where(x == 0, v, jnp.concatenate([v[..., half:], v[..., :half]], axis=-1))

    d_own = w_qkv.shape[0]
    pairs = w_qkv.shape[2] // PAIR // 2
    qkv_cols = pairs * 3 * PAIR
    out_cols = pairs * PAIR
    hid = w_fc1.shape[1] // 2
    qkv_split = w_qkv.reshape(d_own, 3, 2, pairs, PAIR).transpose(2, 0, 3, 1, 4)
    qkv_split = qkv_split.reshape(2, d_own, qkv_cols)
    out_split = w_out.T.reshape(d_own, 2, out_cols).transpose(1, 0, 2)
    heads_split = jnp.concatenate([qkv_split, out_split], axis=-1)
    fc1_split = w_fc1.reshape(d_own, 2, hid).transpose(1, 0, 2)
    fc2_split = w_fc2.T.reshape(d_own, 2, hid).transpose(1, 0, 2)

    def gather_weight(split):
        mine = lax.dynamic_index_in_dim(split, c, 0, keepdims=True)
        other = to_core(lax.dynamic_index_in_dim(split, 1 - c, 0, keepdims=True))
        both = by_core(mine, other, 0)
        near = lax.all_gather(both, "ctx", axis=1, tiled=True).reshape(half, split.shape[-1])
        return near, to_x(near)

    heads_near, heads_far = gather_weight(heads_split)
    fc1_near, fc1_far = gather_weight(fc1_split)
    fc2_near, fc2_far = gather_weight(fc2_split)

    small = jnp.concatenate(
        [
            norm_gain,
            norm_bias,
            b_out,
            b_fc2,
            b_qkv.reshape(-1),
            b_fc1.reshape(-1),
        ]
    )
    small_all = lax.all_gather(small, ("dp", "ctx"), axis=0, tiled=False)
    n_own = n_dp * n_ctx
    at = 0

    def take(count):
        nonlocal at
        got = small_all[:, at : at + count]
        at += count
        return got

    gain = roll_x(take(d_own).reshape(model).astype(wide))
    shift = roll_x(take(d_own).reshape(model).astype(wide))
    out_bias = roll_x(take(d_own).reshape(model).astype(wide))
    fc2_bias = roll_x(take(d_own).reshape(model).astype(wide))
    heads_here = b_qkv.shape[1]
    dims_here = b_qkv.shape[2]
    qkv_bias = take(b_qkv.size).reshape(n_own, 3, heads_here, dims_here)
    qkv_bias = qkv_bias.transpose(1, 2, 0, 3).reshape(3, 2, pairs, PAIR)
    qkv_bias = lax.dynamic_index_in_dim(qkv_bias, c, 1, keepdims=False)
    qkv_bias = qkv_bias.transpose(1, 0, 2).reshape(qkv_cols).astype(wide)
    fc1_bias = take(b_fc1.size).reshape(n_own, b_fc1.shape[0], b_fc1.shape[1])
    fc1_bias = fc1_bias.transpose(1, 0, 2).reshape(2, hid)
    fc1_bias = lax.dynamic_index_in_dim(fc1_bias, c, 0, keepdims=False).astype(wide)

    def away(k):
        return [
            (
                (2 * xx + cc) * n_ctx + zz,
                (2 * xx + (zz ^ k) // 2) * n_ctx + 2 * cc + (zz ^ k) % 2,
            )
            for xx in range(2)
            for cc in range(2)
            for zz in range(n_ctx)
        ]

    def send_away(v):
        cut = v.reshape(n_seq, 2, n_mp, part, model)
        got = []
        for k in range(n_ctx):
            there = z ^ k
            piece = lax.dynamic_slice(
                cut, (there % 2, there // 2, y, 0, 0), (1, 1, 1, part, model)
            ).reshape(part, model)
            got.append(lax.ppermute(roll_x(piece), ("dp", "ctx"), away(k)))
        return jnp.concatenate(got, axis=0)

    def send_home(v):
        cut = v.reshape(n_ctx, part, model)
        homes = []
        for k in range(n_ctx):
            back = [(b, a) for a, b in away(k)]
            piece = lax.ppermute(roll_x(cut[k]), ("dp", "ctx"), back)
            if n_mp == 2:
                other = lax.ppermute(piece, "mp", [(0, 1), (1, 0)])
                piece = jnp.where(
                    y == 0,
                    jnp.concatenate([piece, other], axis=0),
                    jnp.concatenate([other, piece], axis=0),
                )
            else:
                piece = lax.all_gather(piece, "mp", axis=0, tiled=True)
            homes.append(piece)
        stacked = jnp.stack(homes, axis=0)
        placed = [
            lax.dynamic_index_in_dim(stacked, (2 * cc + i) ^ z, 0, keepdims=False)
            for i in range(n_seq)
            for cc in range(2)
        ]
        return jnp.stack(placed, axis=0).reshape(n_seq, n_slot, model)

    def gather_rows(own):
        if n_mp == 2:
            own = jnp.concatenate([own, lax.ppermute(own, "mp", [(0, 1), (1, 0)])], axis=0)
        else:
            own = lax.all_gather(own, "mp", axis=0, tiled=True)
        return jnp.concatenate([own, to_core(own)], axis=0)

    def sum_rows(left, right):
        split = left.shape[0] // 2
        far = to_core(mm_nt(left[split:], right).astype(low))
        near = mm_nt(left[:split], right) + far.astype(wide)
        if n_mp == 2:
            other = lax.ppermute(near[rows_own:].astype(low), "mp", [(0, 1), (1, 0)])
            return near[:rows_own] + other.astype(wide)
        return lax.psum_scatter(near.astype(low), "mp", scatter_dimension=0, tiled=True).astype(wide)

    rows_in = send_away(tokens)
    rows_grad = send_away(grad_out)

    tokens_in = rows_in.astype(wide)
    row_mean = jnp.mean(tokens_in, axis=-1, keepdims=True)
    centered = tokens_in - row_mean
    variance = jnp.mean(centered * centered, axis=-1, keepdims=True)
    inv_std = lax.rsqrt(variance + norm_eps)
    normed = centered * inv_std
    ln_out = gather_rows((normed * gain + shift).astype(low))
    grad_rows = gather_rows(rows_grad)

    other_order = to_core(group_order)
    order_row = jnp.where(z // 2 == c, group_order, other_order)
    order_row = lax.dynamic_index_in_dim(order_row, z % 2, 0, keepdims=False)
    ids = jnp.arange(2 * n_mp * n_ctx, dtype=jnp.int32)
    at_core = (ids // (n_mp * n_ctx)) ^ c
    at_mp = (ids // n_ctx) % n_mp
    at_mp = at_mp ^ y if n_mp == 2 else at_mp
    at_ctx = (2 * at_core + z % 2) ^ (ids % n_ctx)
    slot = at_ctx * n_slot + at_core * (n_slot // 2) + at_mp * part
    position = order_row[slot // block_len] * block_len + slot % block_len
    order = jnp.sum(jnp.where((position // part)[None, :] == ids[:, None], ids[None, :], 0), axis=1)

    heads_w = jnp.concatenate([heads_near, heads_far], axis=0)
    qkv_w, out_w = heads_w[:, :qkv_cols], heads_w[:, qkv_cols:]
    qkv = mm(ln_out, qkv_w) + qkv_bias
    grad_mixed = mm(grad_rows, out_w).astype(low)
    mixed, grad_qkv = attention(order, qkv, grad_mixed)
    attn_out = sum_rows(mixed, out_w) + out_bias

    def scatter_weight(far, near):
        cols = near.shape[1]
        total = (near + to_x(far.astype(low)).astype(wide)).astype(low)
        mine = lax.psum_scatter(
            total.reshape(2, half // 2, cols), "ctx", scatter_dimension=1, tiled=True
        )
        other = to_core(lax.dynamic_index_in_dim(mine, 1 - c, 0, keepdims=True))
        mine = lax.dynamic_index_in_dim(mine, c, 0, keepdims=True)
        return by_core(mine, other, 0).astype(wide)

    def weight_grad(left, right):
        return mm_tn(left[:, half:], right), mm_tn(left[:, :half], right)

    grad_qkv_w = scatter_weight(*weight_grad(ln_out, grad_qkv))
    grad_out_w = scatter_weight(*weight_grad(grad_rows, mixed))

    fc1_w = jnp.concatenate([fc1_near, fc1_far], axis=0)
    fc2_w = jnp.concatenate([fc2_near, fc2_far], axis=0)
    pre_act = mm(ln_out, fc1_w) + fc1_bias
    gelu = partial(jax.nn.gelu, approximate=True)
    act = gelu(pre_act).astype(low)
    grad_fc2_w = scatter_weight(*weight_grad(grad_rows, act))
    mlp_out = sum_rows(act, fc2_w) + fc2_bias
    grad_act = mm(grad_rows, fc2_w)
    grad_pre = jax.vjp(gelu, pre_act)[1](grad_act)[0].astype(low)
    grad_fc1_w = scatter_weight(*weight_grad(ln_out, grad_pre))

    block_out = send_home((tokens_in + attn_out + mlp_out).astype(low))
    grad_ln = sum_rows(
        jnp.concatenate([grad_pre, grad_qkv], axis=1), jnp.concatenate([fc1_w, qkv_w], axis=1)
    )
    grad_scaled = grad_ln * gain
    grad_norm = inv_std * (
        grad_scaled
        - jnp.mean(grad_scaled, axis=-1, keepdims=True)
        - normed * jnp.mean(grad_scaled * normed, axis=-1, keepdims=True)
    )
    grad_tokens = grad_out.astype(wide) + send_home(grad_norm.astype(low)).astype(wide)

    shared = jnp.concatenate(
        [
            roll_x(jnp.sum(grad_ln * normed, axis=0)),
            roll_x(jnp.sum(grad_ln, axis=0)),
            roll_x(jnp.sum(rows_grad.astype(wide), axis=0)),
            jnp.stack(
                [
                    jnp.sum(tokens_in * tokens_in),
                    jnp.sum(attn_out * attn_out),
                    jnp.sum(mlp_out * mlp_out),
                ]
            ),
        ]
    )
    shared = lax.psum(shared, ("dp", "ctx", "mp"))
    own = jnp.concatenate(
        [jnp.sum(grad_qkv.astype(wide), axis=0), jnp.sum(grad_pre.astype(wide), axis=0)]
    )
    own = own + to_x(own)
    own = lax.psum(own, "ctx")
    own = by_core(own[None], to_core(own)[None], 0)
    place = dp * n_ctx + z

    def own_slice(v):
        return lax.dynamic_slice_in_dim(v, place * d_own, d_own, 0)

    grad_gain = own_slice(shared[:model])
    grad_shift = own_slice(shared[model : 2 * model])
    grad_bias_out = own_slice(shared[2 * model : 3 * model])
    cells = n_dp * n_seq * SEQ_LEN * model
    root_means = jnp.sqrt(shared[3 * model :] / cells)
    grad_b_qkv = own[:, :qkv_cols].reshape(2, pairs, 3, PAIR).transpose(2, 0, 1, 3)
    grad_b_qkv = grad_b_qkv.reshape(3, heads_here, HD)
    grad_b_qkv = lax.dynamic_slice_in_dim(grad_b_qkv, place * dims_here, dims_here, 2)
    grad_b_fc1 = own[:, qkv_cols:].reshape(b_fc1.shape[0], HD)
    grad_b_fc1 = lax.dynamic_slice_in_dim(grad_b_fc1, place * dims_here, dims_here, 1)

    def join(v):
        return v.transpose(1, 0, 2).reshape(d_own, -1)

    grad_qkv_w = grad_qkv_w.reshape(2, d_own, pairs, 3, PAIR).transpose(1, 3, 0, 2, 4)
    return (
        block_out,
        grad_tokens,
        grad_gain,
        grad_shift,
        grad_qkv_w.reshape(d_own, 3, -1),
        grad_b_qkv,
        join(grad_out_w).T,
        grad_bias_out,
        join(grad_fc1_w),
        grad_b_fc1,
        join(grad_fc2_w).T,
        grad_bias_out,
        root_means,
    )


def solution(mesh):
    owners = ("dp", "ctx")
    return jax.shard_map(
        on_device,
        mesh=mesh,
        in_specs=(
            P("dp", "ctx", None),
            P("dp", None),
            P("dp", "ctx", None),
            P(owners),
            P(owners),
            P(owners, None, "mp"),
            P(None, "mp", owners),
            P("mp", owners),
            P(owners),
            P(owners, "mp"),
            P("mp", owners),
            P("mp", owners),
            P(owners),
        ),
        out_specs=(
            P("dp", "ctx", None),
            P("dp", "ctx", None),
            P(owners),
            P(owners),
            P(owners, None, "mp"),
            P(None, "mp", owners),
            P("mp", owners),
            P(owners),
            P(owners, "mp"),
            P("mp", owners),
            P("mp", owners),
            P(owners),
            P(),
        ),
        check_vma=False,
    )
```

time: 2320 us -> 1490 us (0.64)
  waiting for transfers between devices: 872 us -> 489 us
  matrix products: 598 us -> 268 us
  local copies, waits for them, and re-layouts: 326 us -> 132 us
  Pallas kernels: 0 us -> 184 us
  other arithmetic: 183 us -> 84.2 us
  starting transfers between devices: 0.52 us -> 57 us
  blocking collectives: 303 us -> 253 us
    ppermute x0 -> x51, waiting for transfers between devices: none -> 489 us  [the longest x8 257 us: to_x(): return lax.ppermute(v, 'dp', [(i, i ^ 2) for i in range(n_dp)])]
    dot_general x26 -> x18, matrix products: 598 us -> 268 us  [the longest x4 93.4 us: mm(): return jnp.dot(a, b, preferred_element_type=wide)]
    psum x1 -> x0, waiting for transfers between devices: 289 us -> none  [on_device(): lax.psum(attn_part.astype(jnp.bfloat16), 'mp').astype(jnp.float32)]
    all_gather x6 -> x3, waiting for transfers between devices: 267 us -> 0.01 us  [gather_weight(): lax.all_gather(both, 'ctx', axis=1, tiled=True)]
    reduce_scatter x4 -> x1, waiting for transfers between devices: 242 us -> 0.01 us  [scatter_weight(): lax.psum_scatter(total.reshape(2, half // 2, cols), 'ctx', scatter_dimens...]
    all_gather x6 -> x0, blocking collectives: 194 us -> none  [the longest x1 34.5 us: on_device(): lax.all_gather(b_qkv, ('dp', 'ctx'), axis=2, tiled=True)]
    pallas_call x0 -> x1, Pallas kernels: none -> 184 us  [attention(): pl.pallas_call(partial(attention_kernel, pieces=pieces, piece=seq // piec...]
    dynamic_update_slice x10 -> x0, local copies, waits for them, and re-layouts: 184 us -> none  [the longest x8 167 us: on_device(): lax.map(one_sequence, (queries, key_block, value_block, local_pos, key_pl...]
  transfers between devices with their start and end apart: 13 -> 58, of which waited for: 6 -> 21; matrix products, arithmetic and copies ran while one was open for 48% -> 32% of each run, Pallas kernels for 0% -> 12%
where the time goes in v1:
time: 1490 us; the launch traced here: 1480 us
  waiting for transfers between devices  489 us (33%)
  matrix products  268 us (18%)
  blocking collectives  253 us (17%)
  Pallas kernels  184 us (12%)
  local copies, waits for them, and re-layouts  132 us (9%)
  other arithmetic  84.2 us (6%)
  starting transfers between devices  57 us (4%)
  between operations  16.7 us (1%)
    ppermute x8, waiting for transfers between devices, to_x(): return lax.ppermute(v, 'dp', [(i, i ^ 2) for i in range(n_dp)])  257 us
    unnamed x1, blocking collectives  187 us
    pallas_call x1, Pallas kernels, attention(): pl.pallas_call(partial(attention_kernel, pieces=pieces, piece=seq // piec...  184 us
    dot_general x4, matrix products, mm(): return jnp.dot(a, b, preferred_element_type=wide)  93.4 us
    ppermute x3, waiting for transfers between devices, sum_rows(): other = lax.ppermute(near[rows_own:].astype(low), 'mp', [(0, 1), (1, 0)])  90.2 us
    dot_general x6, matrix products, mm_nt(): lax.dot_general(a, b, (((1,), (1,)), ((), ())), preferred_element_type=wide)  87.6 us
    dot_general x8, matrix products, mm_tn(): lax.dot_general(a, b, (((0,), (0,)), ((), ())), preferred_element_type=wide)  87.3 us
    unnamed x139, local copies, waits for them, and re-layouts  70.5 us
  transfers between devices with their start and end apart: 58, of which 21 were waited for; matrix products, arithmetic and copies ran while one was open for 32% of the time, Pallas kernels for 12%

profile of v1, /device:TPU:0, one launch (start us, length us, event | category | flops | bytes accessed | tf_op | source)
XLA Modules:
  0.0 1483.6 jit_solution(5745720466879108401)
XLA Ops:
  35.5 186.8 %all-reduce = bf16[15360]{0:T(1024)(128)(2,1)S(1)} all-reduce(bf16[15360]{0:T(1024)(128)(2,1)S(1)} %dynamic-update-slice), channel_id=2, replica_groups=mesh['dp'=4,'ctx'=4,'mp'=2] {'dp','ctx'}, use_global_device_ids=true, to_apply=%add | all-reduce | flops 15360 | bytes 61440
  272.7 20.7 %collective-permute-done.13 = bf16[512,2048]{1,0:T(8,128)(2,1)} collective-permute-done((bf16[512,2048]{1,0:T(8,128)(2,1)}, bf16[512,2048]{1,0:T(8,128)(2,1)}, u32[]{:S(2)}, u32[]{:S(2)}) %collective-permute-start.13) | collective-permute-done | bytes 2097184 | tf_op jit(solution)/shard_map/ppermute | solution.py:378
  297.5 40.5 %collective-permute-done.5 = bf16[512,2048]{1,0:T(8,128)(2,1)S(1)} collective-permute-done((bf16[512,2048]{1,0:T(8,128)(2,1)S(1)}, bf16[512,2048]{1,0:T(8,128)(2,1)S(1)}, u32[]{:S(2)}, u32[]{:S(2)}) %collective-permute-start.5) | collective-permute-done | bytes 2097184 | tf_op jit(solution)/shard_map/ppermute | solution.py:378
  384.1 56.6 %collective-permute-done.18 = bf16[1024,2048]{1,0:T(8,128)(2,1)} collective-permute-done((bf16[1024,2048]{1,0:T(8,128)(2,1)}, bf16[1024,2048]{1,0:T(8,128)(2,1)}, u32[]{:S(2)}, u32[]{:S(2)}) %collective-permute-start.18) | collective-permute-done | bytes 4194336 | tf_op jit(solution)/shard_map/ppermute | solution.py:261
  440.6 30.8 %multiply_convert_fusion = (bf16[2048,2048]{1,0:T(8,128)(2,1)}, f32[2048,2048]{1,0:T(8,128)}) fusion(f32[2048]{0:T(1024)S(1)} %bitcast.228, bf16[1024,2048]{1,0:T(8,128)(2,1)} %collective-permute-done.18, bf16[1024,2048]{1,0:T(8,128)(2,1)} %bitcast.185, bf16[1024,2048]{1,0:T(8,128)(2,1)} %collective-permute-done.6, bf16[512,2048]{1,0:T(8,128)(2,1)} %copy-done.15, ...), kind=kOutput, calls=%fused_computation.11 | convolution fusion | flops 17263755264 | bytes 41951232 | tf_op jit(solution)/shard_map/dot_general | solution.py:220
  471.4 14.2 convolution_convert_fusion.1
  487.4 133.0 %collective-permute-done.8 = bf16[1024,2048]{1,0:T(8,128)(2,1)} collective-permute-done((bf16[1024,2048]{1,0:T(8,128)(2,1)}, bf16[1024,2048]{1,0:T(8,128)(2,1)}, u32[]{:S(2)}, u32[]{:S(2)}) %collective-permute-start.8) | collective-permute-done | bytes 4194336 | tf_op jit(solution)/shard_map/ppermute | solution.py:261
  633.3 20.6 %convolution_add_fusion.qkv_ref = f32[2048,1536]{1,0:T(8,128)} fusion(bf16[2048,1536]{1,0:T(8,128)(2,1)} %fusion.16, f32[1536]{0:T(1024)S(1)} %reshape.1096, bf16[1024,2048]{1,0:T(8,128)(2,1)} %collective-permute-done.6, bf16[512,2048]{1,0:T(8,128)(2,1)} %copy-done.15, bf16[512,2048]{1,0:T(8,128)(2,1)S(1)} %copy-done.13), kind=kOutput, calls=%fused_computation.16 | convolution fusion | flops 12913213440 | bytes 27269120 | tf_op jit(solution)/shard_map/dot_general | solution.py:220
  653.9 184.3 %attention.1 = (bf16[2048,512]{1,0:T(8,128)(2,1)S(1)}, bf16[2048,1536]{1,0:T(8,128)(2,1)}) custom-call(s32[16]{0:T(128)S(1)} %select_reduce_fusion.order_ref, f32[2048,1536]{1,0:T(8,128)} %convolution_add_fusion.qkv_ref, bf16[2048,512]{1,0:T(8,128)(2,1)} %convolution_convert_fusion.4.do_ref, f32[2048,128]{1,0:T(8,128)S(1)} %get-tuple-element.189.cos_ref, ...), custom_call_target="tpu_custom_call" | custom-call | flops 51539607552 | bytes 30000000 | tf_op jit(solution)/shard_map/attention/pallas_call | solution.py:186
  855.0 36.1 %convert_reduce_fusion = (f32[2048]{0:T(1024)S(1)}, bf16[2048,2048]{1,0:T(8,128)(2,1)}) fusion(f32[2048,2048]{1,0:T(8,128)} %get-tuple-element.191, f32[2048]{0:T(1024)S(1)} %bitcast.229, bf16[2048,2048]{1,0:T(8,128)(2,1)} %constant_dynamic-update-slice_fusion.9, bf16[1024,2048]{1,0:T(8,128)(2,1)} %collective-permute-done.20, ...), kind=kOutput, calls=%fused_computation.10 | convolution fusion | flops 17293113344 | bytes 41959424 | tf_op jit(solution)/shard_map/dot_general | solution.py:220
  891.1 13.2 convolution_convert_fusion.2
  918.1 20.3 %collective-permute-done.41 = bf16[1024,1536]{1,0:T(8,128)(2,1)} collective-permute-done((bf16[1024,1536]{1,0:T(8,128)(2,1)}, bf16[1024,1536]{1,0:T(8,128)(2,1)}, u32[]{:S(2)}, u32[]{:S(2)}) %collective-permute-start.41) | collective-permute-done | bytes 3145760 | tf_op jit(solution)/shard_map/ppermute | solution.py:261
  955.0 24.2 %fusion.42 = bf16[1024,2048]{1,0:T(8,128)(2,1)} fusion(bf16[2048,1536]{1,0:T(8,128)(2,1)} %fusion.16, bf16[1024,2048]{1,0:T(8,128)(2,1)} %collective-permute-done.18, bf16[1024,2048]{1,0:T(8,128)(2,1)} %bitcast.186, bf16[2048,1536]{1,0:T(8,128)(2,1)} %get-tuple-element.16, bf16[2048,2048]{1,0:T(8,128)(2,1)} %get-tuple-element.193), kind=kOutput, calls=%fused_computation.79 | convolution fusion | flops 15093202944 | bytes 33554432 | tf_op jit(solution)/shard_map/dot_general | solution.py:224
  979.7 47.1 %collective-permute-done.43 = f32[3584]{0:T(1024)S(1)} collective-permute-done((f32[3584]{0:T(1024)S(1)}, f32[3584]{0:T(1024)S(1)}, u32[]{:S(2)}, u32[]{:S(2)}) %collective-permute-start.43) | collective-permute-done | bytes 14368 | tf_op jit(solution)/shard_map/ppermute | solution.py:261
  1026.8 19.6 %psum.15 = f32[3584]{0:T(1024)S(1)} all-reduce(f32[3584]{0:T(1024)S(1)} %fusion.108), channel_id=1, replica_groups=mesh['dp'=4,'ctx'=4,'mp'=2] {'ctx'}, use_global_device_ids=true, to_apply=%region_15.16 | all-reduce | flops 3584 | bytes 28672 | tf_op jit(solution)/shard_map/psum | solution.py:481
  1046.4 14.5 fusion.43
  1065.3 15.3 %add_convert_fusion = bf16[1024,2048]{1,0:T(8,128)(2,1)} fusion(bf16[1024,2048]{1,0:T(8,128)(2,1)} %collective-permute-done.49, bf16[2048,2048]{1,0:T(8,128)(2,1)} %get-tuple-element.190, bf16[2048,2048]{1,0:T(8,128)(2,1)} %constant_dynamic-update-slice_fusion.9), kind=kOutput, calls=%fused_computation.26 | convolution fusion | flops 8596226048 | bytes 20971520 | tf_op jit(solution)/shard_map/dot_general | solution.py:228
  1091.6 15.7 %add_convert_fusion.1 = bf16[1024,2048]{1,0:T(8,128)(2,1)} fusion(bf16[1024,2048]{1,0:T(8,128)(2,1)} %collective-permute-done.47, bf16[2048,2048]{1,0:T(8,128)(2,1)} %get-tuple-element.193, bf16[2048,2048]{1,0:T(8,128)(2,1)} %pad_maximum_fusion.1), kind=kOutput, calls=%fused_computation.27 | convolution fusion | flops 8596226048 | bytes 20971520 | tf_op jit(solution)/shard_map/dot_general | solution.py:228
  1118.2 25.2 %convert_add_fusion.1 = f32[1024,2048]{1,0:T(8,128)} fusion(bf16[1024,2048]{1,0:T(8,128)(2,1)} %collective-permute-done.31, bf16[2048,1536]{1,0:T(8,128)(2,1)} %fusion.16, bf16[1024,2048]{1,0:T(8,128)(2,1)} %collective-permute-done.18, bf16[1024,2048]{1,0:T(8,128)(2,1)} %bitcast.187, bf16[2048,2048]{1,0:T(8,128)(2,1)} %get-tuple-element.193, ...), kind=kOutput, calls=%fused_computation.28 | convolution fusion | flops 15095300096 | bytes 41943040 | tf_op jit(solution)/shard_map/dot_general | solution.py:224
  1159.8 14.7 convert_add_fusion.2
  1179.2 17.0 %collective-permute-done.32 = bf16[512,2048]{1,0:T(8,128)(2,1)} collective-permute-done((bf16[512,2048]{1,0:T(8,128)(2,1)}, bf16[512,2048]{1,0:T(8,128)(2,1)}, u32[]{:S(2)}, u32[]{:S(2)}) %collective-permute-start.32) | collective-permute-done | bytes 2097184 | tf_op jit(solution)/shard_map/ppermute | solution.py:388
  1212.6 28.6 %collective-permute-done.16 = bf16[512,2048]{1,0:T(8,128)(2,1)} collective-permute-done((bf16[512,2048]{1,0:T(8,128)(2,1)}, bf16[512,2048]{1,0:T(8,128)(2,1)}, u32[]{:S(2)}, u32[]{:S(2)}) %collective-permute-start.16) | collective-permute-done | bytes 2097184 | tf_op jit(solution)/shard_map/ppermute | solution.py:388
  1241.1 44.6 %collective-permute-done.22 = bf16[512,2048]{1,0:T(8,128)(2,1)} collective-permute-done((bf16[512,2048]{1,0:T(8,128)(2,1)}, bf16[512,2048]{1,0:T(8,128)(2,1)}, u32[]{:S(2)}, u32[]{:S(2)}) %collective-permute-start.22) | collective-permute-done | bytes 2097184 | tf_op jit(solution)/shard_map/ppermute | solution.py:388
  1297.6 46.3 %psum.14 = f32[6147]{0:T(1024)S(1)} all-reduce(f32[6147]{0:T(1024)S(1)} %concatenate.453), channel_id=1, replica_groups=mesh['dp'=4,'ctx'=4,'mp'=2] {'dp','ctx','mp'}, use_global_device_ids=true, to_apply=%region_11.12 | all-reduce | flops 6147 | bytes 49176 | tf_op jit(solution)/shard_map/psum | solution.py:476
  (400 shorter events, 397.1 us)
Async XLA Ops:
  7.2 333.6 %all-gather.7.cloned.1.call-start = ((), (), s32[]{:S(2)}) async-start(), calls=%async_computation.5 | async-start | bytes 5242880 | tf_op jit(solution)/shard_map/all_gather | solution.py:289
  12.2 346.1 %all-gather.9.cloned.1.call-start = ((), (), s32[]{:S(2)}) async-start(), calls=%async_computation.6 | async-start | bytes 5242880 | tf_op jit(solution)/shard_map/all_gather | solution.py:289
  16.0 211.5 %collective-permute-start.9 = (bf16[128,2048]{1,0:T(8,128)(2,1)}, bf16[128,2048]{1,0:T(8,128)(2,1)}, u32[]{:S(2)}, u32[]{:S(2)}) collective-permute-start(bf16[128,2048]{1,0:T(8,128)(2,1)} %maximum_select_fusion.18), channel_id=1, source_target_pairs={{0,0},{2,2},{4,8},{6,10},{8,4},{10,6},{12,12},{14,14},{16,16},{18,... | collective-permute-start | bytes 1572872 | tf_op jit(solution)/shard_map/ppermute | solution.py:349
  22.3 207.7 %collective-permute-start.10 = (bf16[128,2048]{1,0:T(8,128)(2,1)}, bf16[128,2048]{1,0:T(8,128)(2,1)}, u32[]{:S(2)}, u32[]{:S(2)}) collective-permute-start(bf16[128,2048]{1,0:T(8,128)(2,1)} %maximum_select_fusion.19), channel_id=1, source_target_pairs={{0,2},{2,0},{4,10},{6,8},{8,6},{10,4},{12,14},{14,12},{16,18},{18,... | collective-permute-start | bytes 1572872 | tf_op jit(solution)/shard_map/ppermute | solution.py:349
  25.4 211.8 %collective-permute-start.11 = (bf16[128,2048]{1,0:T(8,128)(2,1)S(1)}, bf16[128,2048]{1,0:T(8,128)(2,1)}, u32[]{:S(2)}, u32[]{:S(2)}) collective-permute-start(bf16[128,2048]{1,0:T(8,128)(2,1)S(1)} %maximum_select_fusion.20), channel_id=1, source_target_pairs={{0,8},{2,10},{4,0},{6,2},{8,12},{10,14},{12,4},{14,6},{16,24},{18,... | collective-permute-start | bytes 1572872 | tf_op jit(solution)/shard_map/ppermute | solution.py:349
  28.8 210.8 %collective-permute-start.12 = (bf16[128,2048]{1,0:T(8,128)(2,1)}, bf16[128,2048]{1,0:T(8,128)(2,1)}, u32[]{:S(2)}, u32[]{:S(2)}) collective-permute-start(bf16[128,2048]{1,0:T(8,128)(2,1)} %maximum_select_fusion.21), channel_id=1, source_target_pairs={{0,10},{2,8},{4,2},{6,0},{8,14},{10,12},{12,6},{14,4},{16,26},{18,... | collective-permute-start | bytes 1572872 | tf_op jit(solution)/shard_map/ppermute | solution.py:349
  30.6 334.2 %all-gather.5.cloned.1.call-start = ((), (), s32[]{:S(2)}) async-start(), calls=%async_computation.4 | async-start | bytes 5242880 | tf_op jit(solution)/shard_map/all_gather | solution.py:289
  31.6 211.4 %collective-permute-start = (bf16[128,2048]{1,0:T(8,128)(2,1)}, bf16[128,2048]{1,0:T(8,128)(2,1)S(1)}, u32[]{:S(2)}, u32[]{:S(2)}) collective-permute-start(bf16[128,2048]{1,0:T(8,128)(2,1)} %maximum_select_fusion.14), channel_id=1, source_target_pairs={{0,0},{2,2},{4,8},{6,10},{8,4},{10,6},{12,12},{14,14},{16,16},{18,... | collective-permute-start | bytes 1572872 | tf_op jit(solution)/shard_map/ppermute | solution.py:349
  266.6 794.5 %reduce-scatter.11.cloned.1.call-start = ((), (), s32[]{:S(2)}) async-start(), calls=%async_computation.7 | async-start | bytes 1310720 | tf_op jit(solution)/shard_map/reduce_scatter | solution.py:426
  346.9 93.7 %collective-permute-start.18 = (bf16[1024,2048]{1,0:T(8,128)(2,1)}, bf16[1024,2048]{1,0:T(8,128)(2,1)}, u32[]{:S(2)}, u32[]{:S(2)}) collective-permute-start(bf16[1024,2048]{1,0:T(8,128)(2,1)} %bitcast.184), channel_id=1, source_target_pairs={{0,16},{8,24},{16,0},{24,8},{1,17},{9,25},{17,1},{25,9},{2,18},{10... | collective-permute-start | bytes 12582920 | tf_op jit(solution)/shard_map/ppermute | solution.py:261
  364.5 490.5 %collective-permute-start.20 = (bf16[1024,2048]{1,0:T(8,128)(2,1)}, bf16[1024,2048]{1,0:T(8,128)(2,1)}, u32[]{:S(2)}, u32[]{:S(2)}) collective-permute-start(bf16[1024,2048]{1,0:T(8,128)(2,1)} %bitcast.188), channel_id=1, source_target_pairs={{0,16},{8,24},{16,0},{24,8},{1,17},{9,25},{17,1},{25,9},{2,18},{10... | collective-permute-start | bytes 12582920 | tf_op jit(solution)/shard_map/ppermute | solution.py:261
  371.1 249.3 %collective-permute-start.8 = (bf16[1024,2048]{1,0:T(8,128)(2,1)}, bf16[1024,2048]{1,0:T(8,128)(2,1)}, u32[]{:S(2)}, u32[]{:S(2)}) collective-permute-start(bf16[1024,2048]{1,0:T(8,128)(2,1)} %bitcast.162), channel_id=1, source_target_pairs={{0,16},{8,24},{16,0},{24,8},{1,17},{9,25},{17,1},{25,9},{2,18},{10... | collective-permute-start | bytes 12582920 | tf_op jit(solution)/shard_map/ppermute | solution.py:261
  485.6 579.7 %collective-permute-start.49 = (bf16[1024,2048]{1,0:T(8,128)(2,1)}, bf16[1024,2048]{1,0:T(8,128)(2,1)}, u32[]{:S(2)}, u32[]{:S(2)}) collective-permute-start(bf16[1024,2048]{1,0:T(8,128)(2,1)} %convolution_convert_fusion.1), channel_id=1, source_target_pairs={{0,16},{8,24},{16,0},{24,8},{1,17},{9,25},{17,1},{25,9},{2,18},{10... | collective-permute-start | bytes 12582920 | tf_op jit(solution)/shard_map/ppermute | solution.py:261
  904.3 187.3 %collective-permute-start.47 = (bf16[1024,2048]{1,0:T(8,128)(2,1)}, bf16[1024,2048]{1,0:T(8,128)(2,1)}, u32[]{:S(2)}, u32[]{:S(2)}) collective-permute-start(bf16[1024,2048]{1,0:T(8,128)(2,1)} %convolution_convert_fusion.2), channel_id=1, source_target_pairs={{0,16},{8,24},{16,0},{24,8},{1,17},{9,25},{17,1},{25,9},{2,18},{10... | collective-permute-start | bytes 12582920 | tf_op jit(solution)/shard_map/ppermute | solution.py:261
  909.9 116.9 %collective-permute-start.43 = (f32[3584]{0:T(1024)S(1)}, f32[3584]{0:T(1024)S(1)}, u32[]{:S(2)}, u32[]{:S(2)}) collective-permute-start(f32[3584]{0:T(1024)S(1)} %pad_maximum_fusion.25), channel_id=1, source_target_pairs={{0,16},{8,24},{16,0},{24,8},{1,17},{9,25},{17,1},{25,9},{2,18},{10... | collective-permute-start | bytes 43016 | tf_op jit(solution)/shard_map/ppermute | solution.py:261
  918.0 518.2 %reduce-scatter.13.cloned.1.call-start = ((), (), s32[]{:S(2)}) async-start(), calls=%async_computation.8 | async-start | bytes 3932160
  954.9 487.2 %reduce-scatter.17.cloned.1.call-start = ((), (), s32[]{:S(2)}) async-start(), calls=%async_computation.10 | async-start | bytes 5242880
  979.2 139.0 %collective-permute-start.31 = (bf16[1024,2048]{1,0:T(8,128)(2,1)}, bf16[1024,2048]{1,0:T(8,128)(2,1)}, u32[]{:S(2)}, u32[]{:S(2)}) collective-permute-start(bf16[1024,2048]{1,0:T(8,128)(2,1)} %fusion.42), channel_id=1, source_target_pairs={{0,8},{8,0},{16,24},{24,16},{1,9},{9,1},{17,25},{25,17},{2,10},{10... | collective-permute-start | bytes 12582920 | tf_op jit(solution)/shard_map/ppermute | solution.py:258
  979.2 169.7 %collective-permute-start.15 = (bf16[1024,2048]{1,0:T(8,128)(2,1)}, bf16[1024,2048]{1,0:T(8,128)(2,1)}, u32[]{:S(2)}, u32[]{:S(2)}) collective-permute-start(bf16[1024,2048]{1,0:T(8,128)(2,1)} %convolution_convert_fusion.3), channel_id=1, source_target_pairs={{0,8},{8,0},{16,24},{24,16},{1,9},{9,1},{17,25},{25,17},{2,10},{10... | collective-permute-start | bytes 12582920 | tf_op jit(solution)/shard_map/ppermute | solution.py:258
  1064.2 94.6 %collective-permute-start.21 = (bf16[1024,2048]{1,0:T(8,128)(2,1)}, bf16[1024,2048]{1,0:T(8,128)(2,1)}, u32[]{:S(2)}, u32[]{:S(2)}) collective-permute-start(bf16[1024,2048]{1,0:T(8,128)(2,1)} %fusion.43), channel_id=1, source_target_pairs={{0,8},{8,0},{16,24},{24,16},{1,9},{9,1},{17,25},{25,17},{2,10},{10... | collective-permute-start | bytes 12582920 | tf_op jit(solution)/shard_map/ppermute | solution.py:258
  1091.5 359.5 %reduce-scatter.15.cloned.1.call-start = ((), (), s32[]{:S(2)}) async-start(), calls=%async_computation.9 | async-start | bytes 5242880
  1178.5 107.3 %collective-permute-start.22 = (bf16[512,2048]{1,0:T(8,128)(2,1)}, bf16[512,2048]{1,0:T(8,128)(2,1)}, u32[]{:S(2)}, u32[]{:S(2)}) collective-permute-start(bf16[512,2048]{1,0:T(8,128)(2,1)} %slice.597), channel_id=1, source_target_pairs={{0,1},{1,0},{2,3},{3,2},{4,5},{5,4},{6,7},{7,6},{8,9},{9,8},{10,11... | collective-permute-start | bytes 6291464 | tf_op jit(solution)/shard_map/ppermute | solution.py:388
  1209.9 133.9 %collective-permute-start.37 = (bf16[128,2048]{1,0:T(8,128)(2,1)}, bf16[128,2048]{1,0:T(8,128)(2,1)S(1)}, u32[]{:S(2)}, u32[]{:S(2)}) collective-permute-start(bf16[128,2048]{1,0:T(8,128)(2,1)} %get-tuple-element.96), channel_id=1, source_target_pairs={{8,0},{10,2},{0,4},{2,6},{12,8},{14,10},{4,12},{6,14},{24,16},{26,... | collective-permute-start | bytes 1572872 | tf_op jit(solution)/shard_map/ppermute | solution.py:357
  1241.1 105.1 %collective-permute-start.39 = (bf16[128,2048]{1,0:T(8,128)(2,1)}, bf16[128,2048]{1,0:T(8,128)(2,1)S(1)}, u32[]{:S(2)}, u32[]{:S(2)}) collective-permute-start(bf16[128,2048]{1,0:T(8,128)(2,1)} %get-tuple-element.95), channel_id=1, source_target_pairs={{10,0},{8,2},{2,4},{0,6},{14,8},{12,10},{6,12},{4,14},{26,16},{24,... | collective-permute-start | bytes 1572872 | tf_op jit(solution)/shard_map/ppermute | solution.py:357
  (88 other events, 3591.1 us)
Sparse Core Ops, SparseCore 0:
  12.3 130.8 all-gather.6
  144.8 81.7 all-gather.8
  266.7 84.6 all-gather.4
  918.2 28.8 reduce-scatter.10
  955.1 62.1 reduce-scatter.12
  1091.7 75.3 reduce-scatter.16
  1179.4 108.0 reduce-scatter.14

commit v2 on v1

v2 whole, which is shorter than its diff:
```python
from functools import partial

import jax
import jax.numpy as jnp
import numpy as np
from jax import lax
from jax.experimental import pallas as pl
from jax.experimental.pallas import tpu as pltpu
from jax.sharding import PartitionSpec as P

HD = 64
ROT = 32
SEQ_LEN = 2048
PAIR = 2 * HD
TILE = 512

norm_eps = 1e-05
rotary_base = 10000.0
masked_fill = -1e30
low = jnp.bfloat16
wide = jnp.float32
gelu_in = (2.0 / 3.141592653589793) ** 0.5
gelu_cubic = 0.044715
vmem_limit = 48 * 1024 * 1024


def rotary_rows(seq):
    half = ROT // 2
    lane = np.arange(PAIR, dtype=np.int32)[None, :] % HD
    inverse = np.power(np.float32(rotary_base), -(lane % half).astype(np.float32) * np.float32(2.0 / ROT))
    angles = np.arange(seq, dtype=np.float32)[:, None] * inverse
    cosine, sine = np.cos(angles), np.sin(angles)
    return tuple(
        jnp.asarray(v.astype(np.float32))
        for v in (
            np.where(lane < ROT, cosine, 1.0),
            np.where(lane < half, -sine, 0.0),
            np.where((lane >= half) & (lane < ROT), sine, 0.0),
        )
    )


def attention_kernel(
    order_ref, qkv_ref, do_ref, cos_ref, up_ref, down_ref, mixed_ref, grad_ref,
    sorted_qkv, sorted_do, q_nat, k_nat, v_nat, do_nat, q_t, k_t, v_t, do_t,
    s_ref, dk_acc, dv_acc, out_s, grad_s, *, pieces, piece,
):
    blocks = pieces * piece // TILE
    scale = HD**-0.5
    dot = partial(jnp.dot, preferred_element_type=wide)

    def rows_of(b):
        return pl.ds(pl.multiple_of(b * TILE, TILE), TILE)

    def fold(t, how):
        return how(t.reshape(TILE // 8, 8, TILE), axis=0)

    def gather(r, _):
        src = pl.multiple_of(order_ref[r] * piece, piece)
        dst = pl.multiple_of(r * piece, piece)
        sorted_qkv[pl.ds(dst, piece), :] = qkv_ref[pl.ds(src, piece), :]
        sorted_do[pl.ds(dst, piece), :] = do_ref[pl.ds(src, piece), :]
        return 0

    lax.fori_loop(0, pieces, gather, 0)
    first = lax.broadcasted_iota(jnp.int32, (TILE, PAIR), 1) < HD

    def turn(t, rows, sign):
        up = pltpu.roll(t, PAIR - ROT // 2, 1) * up_ref[rows, :]
        down = pltpu.roll(t, ROT // 2, 1) * down_ref[rows, :]
        return t * cos_ref[rows, :] + sign * (up + down)

    def prepare(b, _):
        rows = rows_of(b)
        q = turn(sorted_qkv[rows, 0:PAIR], rows, 1.0).astype(low).astype(wide) * scale
        k = turn(sorted_qkv[rows, PAIR : 2 * PAIR], rows, 1.0)
        v = sorted_qkv[rows, 2 * PAIR : 3 * PAIR]
        g = sorted_do[rows, :].astype(wide)
        for val, nat, tr in ((q, q_nat, q_t), (k, k_nat, k_t), (v, v_nat, v_t), (g, do_nat, do_t)):
            nat[0, b] = jnp.where(first, val, 0.0).astype(low)
            nat[1, b] = jnp.where(first, 0.0, val).astype(low)
            tr[b] = val.T.astype(low)
        dk_acc[b] = jnp.zeros((TILE, PAIR), wide)
        dv_acc[b] = jnp.zeros((TILE, PAIR), wide)
        return 0

    for b in range(blocks):
        prepare(b, 0)
    key_row = lax.broadcasted_iota(jnp.int32, (TILE, TILE), 0)
    query_col = lax.broadcasted_iota(jnp.int32, (TILE, TILE), 1)
    allowed = key_row <= query_col

    def one_block(i, _):
        q_i = q_t[i]
        do_i = do_t[i]

        def score(j, tops):
            new = []
            for h in range(2):
                s = dot(k_nat[h, j], q_i)
                s_ref[h, j] = s
                new.append(jnp.maximum(tops[h], fold(s, jnp.max)))
            return tuple(new)

        partial_tops = (jnp.full((8, TILE), masked_fill, wide),) * 2
        for j in range(i):
            partial_tops = score(j, partial_tops)
        tops = []
        for h in range(2):
            s = jnp.where(allowed, dot(k_nat[h, i], q_i), masked_fill)
            s_ref[h, i] = s
            tops.append(
                jnp.max(jnp.maximum(partial_tops[h], fold(s, jnp.max)), axis=0, keepdims=True)
            )

        def weigh(j, carry):
            sums, accs = carry
            new_sums, new_accs = [], []
            for h in range(2):
                p = jnp.exp(s_ref[h, j] - tops[h])
                s_ref[h, j] = p
                new_sums.append(sums[h] + fold(p, jnp.sum))
                new_accs.append(accs[h] + dot(v_t[j, h * HD : (h + 1) * HD, :], p.astype(low)))
            return tuple(new_sums), tuple(new_accs)

        carry = ((jnp.zeros((8, TILE), wide),) * 2, (jnp.zeros((HD, TILE), wide),) * 2)
        for j in range(i + 1):
            carry = weigh(j, carry)
        sums, accs = carry
        invs, deltas, outs = [], [], []
        for h in range(2):
            inv = 1.0 / jnp.sum(sums[h], axis=0, keepdims=True)
            o = accs[h] * inv
            outs.append(o)
            invs.append(inv)
            g = do_i[h * HD : (h + 1) * HD, :].astype(wide)
            deltas.append(jnp.sum(o * g, axis=0, keepdims=True))
        out_s[i] = jnp.concatenate(outs, axis=0).T.astype(low)

        def pull(j, dq):
            new = []
            dv = dk = None
            for h in range(2):
                dp = dot(v_nat[h, j], do_i)
                p = s_ref[h, j] * invs[h]
                ds = (p * (dp - deltas[h])).astype(low)
                dv_h = dot(p.astype(low), do_nat[h, i])
                dk_h = dot(ds, q_nat[h, i])
                dv = dv_h if dv is None else dv + dv_h
                dk = dk_h if dk is None else dk + dk_h
                new.append(dq[h] + dot(k_t[j, h * HD : (h + 1) * HD, :], ds))
            dv_acc[j] += dv
            dk_acc[j] += dk
            return tuple(new)

        dq = (jnp.zeros((HD, TILE), wide),) * 2
        for j in range(i + 1):
            dq = pull(j, dq)
        rows = rows_of(i)
        dq_rows = jnp.concatenate(dq, axis=0).T * scale
        grad_s[rows, 0:PAIR] = turn(dq_rows, rows, -1.0).astype(low)
        return 0

    for b in range(blocks):
        one_block(b, 0)

    def finish(b, _):
        rows = rows_of(b)
        grad_s[rows, PAIR : 2 * PAIR] = turn(dk_acc[b], rows, -1.0).astype(low)
        grad_s[rows, 2 * PAIR : 3 * PAIR] = dv_acc[b].astype(low)
        sorted_do[rows, :] = out_s[b]
        return 0

    for b in range(blocks):
        finish(b, 0)

    def scatter(r, _):
        src = pl.multiple_of(order_ref[r] * piece, piece)
        dst = pl.multiple_of(r * piece, piece)
        mixed_ref[pl.ds(src, piece), :] = sorted_do[pl.ds(dst, piece), :]
        grad_ref[pl.ds(src, piece), :] = grad_s[pl.ds(dst, piece), :]
        return 0

    lax.fori_loop(0, pieces, scatter, 0)


def attention(order, qkv, grad_mixed, tables, deps):
    seq, width = grad_mixed.shape
    pairs = width // PAIR
    pieces = order.shape[0]
    blocks = seq // TILE
    vmem = pltpu.VMEM
    table = pl.BlockSpec((seq, PAIR), lambda p, o: (0, 0))
    one = pl.BlockSpec((seq, PAIR), lambda p, o: (0, p))
    three = pl.BlockSpec((seq, 3 * PAIR), lambda p, o: (0, p))
    kernel = partial(attention_kernel, pieces=pieces, piece=seq // pieces)
    count = len(deps)

    def inner(order_ref, *refs):
        kernel(order_ref, *refs[count:])

    return pl.pallas_call(
        inner,
        grid_spec=pltpu.PrefetchScalarGridSpec(
            num_scalar_prefetch=1,
            grid=(pairs,),
            in_specs=[pl.BlockSpec(memory_space=pl.ANY)] * count + [three, one, table, table, table],
            out_specs=[one, three],
            scratch_shapes=[
                vmem((seq, 3 * PAIR), wide),
                vmem((seq, PAIR), low),
                *[vmem((2, blocks, TILE, PAIR), low)] * 4,
                *[vmem((blocks, PAIR, TILE), low)] * 4,
                vmem((2, blocks, TILE, TILE), wide),
                vmem((blocks, TILE, PAIR), wide),
                vmem((blocks, TILE, PAIR), wide),
                vmem((blocks, TILE, PAIR), low),
                vmem((seq, 3 * PAIR), low),
            ],
        ),
        out_shape=[
            jax.ShapeDtypeStruct((seq, width), low),
            jax.ShapeDtypeStruct((seq, 3 * width), low),
        ],
        compiler_params=pltpu.CompilerParams(
            vmem_limit_bytes=48 * 1024 * 1024, dimension_semantics=("arbitrary",)
        ),
        cost_estimate=pl.CostEstimate(
            flops=pairs * 24 * seq * seq * PAIR, bytes_accessed=30_000_000, transcendentals=0
        ),
        name="attention",
    )(order, *deps, qkv, grad_mixed, *tables)


def call(body, name, grid, flags, in_specs, args, out_specs, out_shape, flops, moved, deps):
    count = len(deps)

    def inner(flag_ref, *refs):
        body(flag_ref, *refs[count:])

    in_specs = [pl.BlockSpec(memory_space=pl.ANY)] * count + in_specs
    args = [*deps, *args]
    return pl.pallas_call(
        inner,
        grid_spec=pltpu.PrefetchScalarGridSpec(
            num_scalar_prefetch=1, grid=grid, in_specs=in_specs, out_specs=out_specs
        ),
        out_shape=out_shape,
        compiler_params=pltpu.CompilerParams(vmem_limit_bytes=vmem_limit),
        cost_estimate=pl.CostEstimate(flops=flops, bytes_accessed=moved, transcendentals=0),
        name=name,
    )(flags, *args)


def quarter(n):
    return (n % 2) * 2 + n // 2


def product_nn(flags, a, chunks, width, kind, extra, deps):
    rows, model = a.shape
    fourth = model // 4
    step = min(rows, 512)
    count = len(chunks)

    def body(flag_ref, *refs):
        left = [ref[...] for ref in refs[:4]]
        outs = refs[4 + count + (extra is not None) :]
        for n in range(count):
            at = slice(n * width, (n + 1) * width)
            got = None
            for q in range(4):
                w = refs[4 + n][q * fourth : (q + 1) * fourth, :]
                one = jnp.dot(left[q], w, preferred_element_type=wide)
                got = one if got is None else got + one
            if kind == "plain":
                outs[0][:, at] = got.astype(low)
                continue
            more = refs[4 + count][:, at]
            if kind == "bias":
                outs[0][:, at] = got + more
            elif kind == "times":
                outs[0][:, at] = (got * more.astype(wide)).astype(low)
            else:
                v = got + more
                sq = v * v
                up = 0.5 + 0.5 * jnp.tanh(v * (gelu_in + gelu_in * gelu_cubic * sq))
                act = v * up
                outs[0][:, at] = act.astype(low)
                inner = 2.0 * gelu_in + 6.0 * gelu_in * gelu_cubic * sq
                outs[1][:, at] = (up + act * (1.0 - up) * inner).astype(low)

    total = count * width
    own = pl.BlockSpec((step, total), lambda i, f: (i, 0))
    in_specs = [
        pl.BlockSpec((step, fourth), partial(lambda col, i, f: (i, col), quarter(q)))
        for q in range(4)
    ]
    args = [a] * 4
    for weight, col in chunks:
        in_specs.append(pl.BlockSpec((model, width), partial(lambda col, i, f: (0, col), col)))
        args.append(weight)
    if kind == "times":
        extra, col = extra
        in_specs.append(pl.BlockSpec((step, total), lambda i, f: (i, col)))
        args.append(extra)
    elif extra is not None:
        in_specs.append(pl.BlockSpec((1, total), lambda i, f: (0, 0)))
        args.append(extra)
    outs = 2 if kind == "gelu" else 1
    out = call(
        body,
        "rows_" + kind,
        (rows // step,),
        flags,
        in_specs,
        args,
        [own] * outs,
        [jax.ShapeDtypeStruct((rows, total), wide if kind == "bias" else low)] * outs,
        2 * rows * model * total,
        2 * (rows * model + model * total + 2 * rows * total),
        deps,
    )
    return out if outs == 2 else out[0]


def product_tn(flags, outs, side, n_ctx, add, deps):
    rows, model = outs[0][0][0].shape
    half = model // 2
    step = half // 2
    d_own = step // n_ctx
    terms = [term for out in outs for term in out]
    count = len(terms)

    def body(flag_ref, *refs):
        n = 0
        for o, out in enumerate(outs):
            at = 0
            for _, _, _, width in out:
                got = lax.dot_general(
                    refs[n][...],
                    refs[count + n][...],
                    (((0,), (0,)), ((), ())),
                    preferred_element_type=wide,
                ).reshape(n_ctx, d_own, width)
                if add is not None:
                    got += refs[2 * count][:, 0, :, at : at + width].astype(wide)
                refs[-len(outs) + o][:, 0, :, at : at + width] = got.astype(low)
                n += 1
                at += width

    totals = [sum(term[3] for term in out) for out in outs]
    out_specs = [pl.BlockSpec((n_ctx, 1, d_own, t), lambda i, f: (0, i, 0, 0)) for t in totals]
    in_specs = [pl.BlockSpec((rows, step), lambda i, f: (0, 2 * (f[0] ^ side) + i))] * count
    in_specs += [
        pl.BlockSpec((rows, width), partial(lambda col, i, f: (0, col), col))
        for _, _, col, width in terms
    ]
    args = [term[0] for term in terms] + [term[1] for term in terms]
    if add is not None:
        in_specs.append(out_specs[0])
        args.append(add)
    return call(
        body,
        "weight_sums",
        (2,),
        flags,
        in_specs,
        args,
        out_specs,
        [jax.ShapeDtypeStruct((n_ctx, 2, d_own, t), low) for t in totals],
        2 * rows * half * sum(totals),
        2 * (rows * half * count + (rows + half) * sum(totals)),
        deps,
    )


def product_nt(flags, lefts, weights, cols, block, rows, add, split, deps):
    model = weights[0].shape[0]
    step = model // 4
    count = len(lefts)
    ks = [k for _, _, k in lefts]

    def body(flag_ref, *refs):
        got = None
        for a, w in zip(refs[:count], refs[count : 2 * count]):
            one = lax.dot_general(
                a[...], w[...], (((1,), (1,)), ((), ())), preferred_element_type=wide
            )
            got = one if got is None else got + one
        if add is not None:
            got += refs[2 * count][...].astype(wide)
        if split:
            refs[-2][...] = got[: rows // 2]
            refs[-1][...] = got[rows // 2 :].astype(low)
        else:
            refs[-1][...] = got.astype(low)

    in_specs = [
        pl.BlockSpec((rows, k), partial(lambda col, j, f: (block, col), col)) for _, col, k in lefts
    ]
    for (_, _, k), col in zip(lefts, cols):
        in_specs.append(pl.BlockSpec((step, k), partial(lambda col, j, f: (quarter(j), col), col)))
    args = [left for left, _, _ in lefts] + list(weights)
    if add is not None:
        in_specs.append(pl.BlockSpec((rows, step), lambda j, f: (0, j)))
        args.append(add)
    kept = rows // 2 if split else rows
    types = [wide, low] if split else [low]
    out = call(
        body,
        "feature_sums",
        (4,),
        flags,
        in_specs,
        args,
        [pl.BlockSpec((kept, step), lambda j, f: (0, j))] * len(types),
        [jax.ShapeDtypeStruct((kept, model), t) for t in types],
        2 * rows * model * sum(ks),
        2 * (rows + model) * sum(ks) + 4 * rows * model,
        deps,
    )
    return out if split else out[0]


def place_rows(flags, mine, other, n_seq, n_slot, base):
    model = mine.shape[1]
    part = n_slot // 4
    out_type = low if base is None else wide

    def body(flag_ref, *refs):
        own = pl.program_id(2) == flag_ref[1]

        @pl.when(own)
        def _():
            got = refs[0][...]
            refs[-1][...] = got if base is None else refs[2][...].astype(wide) + got.astype(wide)

        @pl.when(jnp.logical_not(own))
        def _():
            got = refs[1][...]
            refs[-1][...] = got if base is None else refs[2][...].astype(wide) + got.astype(wide)

    piece = pl.BlockSpec((part, model), lambda i, cc, yy, f: ((cc ^ f[0]) * n_seq + i, 0))
    slot = pl.BlockSpec((part, model), lambda i, cc, yy, f: (4 * i + 2 * cc + yy, 0))
    in_specs = [piece, piece]
    args = [mine, other]
    if base is not None:
        in_specs.append(slot)
        args.append(base.reshape(n_seq * n_slot, model))
    out = call(
        body,
        "place_rows",
        (n_seq, 2, 2),
        flags,
        in_specs,
        args,
        slot,
        jax.ShapeDtypeStruct((n_seq * n_slot, model), out_type),
        0,
        12 * n_seq * n_slot * model,
        [],
    )
    return out.reshape(n_seq, n_slot, model)


def stack_rows(flags, parts, deps):
    rows, model = parts[0].shape
    step = min(rows, 256)
    steps = rows // step

    def body(flag_ref, *refs):
        for n in range(len(parts)):

            @pl.when(pl.program_id(0) == n)
            def _():
                refs[-1][...] = refs[n][...]

    def at(n, i, j, f):
        return (jnp.where(i < n, 0, jnp.where(i > n, steps - 1, j)), 0)

    return call(
        body,
        "stack_rows",
        (len(parts), steps),
        flags,
        [pl.BlockSpec((step, model), partial(at, n)) for n in range(len(parts))],
        list(parts),
        pl.BlockSpec((step, model), lambda i, j, f: (i * steps + j, 0)),
        jax.ShapeDtypeStruct((len(parts) * rows, model), parts[0].dtype),
        0,
        4 * len(parts) * rows * model,
        deps,
    )


def never(*arrays):
    firsts = [v[(0,) * v.ndim] for v in arrays]
    return sum((v != v).astype(jnp.int32) for v in firsts)


def on_device(
    tokens,
    group_order,
    grad_out,
    norm_gain,
    norm_bias,
    w_qkv,
    b_qkv,
    w_out,
    b_out,
    w_fc1,
    b_fc1,
    w_fc2,
    b_fc2,
):
    n_dp = lax.axis_size("x") * lax.axis_size("core")
    n_ctx, n_mp = lax.axis_size("ctx"), lax.axis_size("mp")
    n_seq, n_slot, model = tokens.shape
    groups = group_order.shape[1]
    assert n_dp == 4 and 2 * n_seq == n_ctx == 4
    z, y = lax.axis_index("ctx"), lax.axis_index("mp")
    x, c = lax.axis_index("x"), lax.axis_index("core")
    dp = 2 * x + c
    half = model // 2
    part = n_slot // (2 * n_mp)
    rows_own = n_ctx * part
    block_len = SEQ_LEN // groups
    d_own = w_qkv.shape[0]
    flag_x = x.astype(jnp.int32).reshape(1)
    flag_cy = jnp.stack([c, y]).astype(jnp.int32)

    def to_core(v):
        return lax.ppermute(v, "core", [(0, 1), (1, 0)])

    def to_x(v):
        return lax.ppermute(v, "x", [(0, 1), (1, 0)])

    def to_z(v, k):
        return lax.ppermute(v, "ctx", [(i, i ^ k) for i in range(n_ctx)])

    def to_y(v):
        return lax.ppermute(v, "mp", [(0, 1), (1, 0)])

    def in_order(bit, mine, other, axis):
        return jnp.where(
            bit == 0,
            jnp.concatenate([mine, other], axis),
            jnp.concatenate([other, mine], axis),
        )

    def to_ctx(v):
        return lax.all_to_all(v, "ctx", 0, 0, tiled=True)

    def send_away(v, wait=0):
        cut = v.reshape(n_seq, 2, n_mp, part, model)

        def of_core(at):
            got = lax.dynamic_slice(
                cut, (0, at, y + wait, 0, 0), (n_seq, 1, 1, part, model)
            )
            return got.reshape(n_seq, part, model)

        return to_ctx(in_order(c, of_core(c), to_core(of_core(1 - c)), 0)).reshape(rows_own, model)

    def send_home(v):
        got = to_ctx(v.reshape(n_ctx, part, model))
        mine = lax.dynamic_slice_in_dim(got, n_seq * c, n_seq, 0)
        other = to_core(lax.dynamic_slice_in_dim(got, n_seq * (1 - c), n_seq, 0))
        homes = jnp.concatenate([mine, other], axis=0).reshape(rows_own, model)
        return homes, (to_y(homes) if n_mp == 2 else homes)

    def placed_home(homes, others, base=None):
        if n_mp == 2:
            return place_rows(flag_cy, homes, others, n_seq, n_slot, base)
        homes = lax.all_gather(homes.reshape(2, n_seq, part, model), "mp", axis=2, tiled=True)
        homes = jnp.where(c == 0, homes, homes[::-1])
        got = jnp.swapaxes(homes, 0, 1).reshape(n_seq, n_slot, model)
        return got if base is None else base.astype(wide) + got.astype(wide)

    def gather_rows(parts, deps_own, deps_all):
        if n_mp == 2:
            own = stack_rows(flag_x, [*parts, *[to_y(v) for v in parts]], deps_own)
        else:
            own = lax.all_gather(jnp.concatenate(parts, axis=0), "mp", axis=0, tiled=True)
        return stack_rows(flag_x, [own, to_core(own)], deps_all)

    small = jnp.concatenate(
        [norm_gain, norm_bias, b_out, b_fc2, b_qkv.reshape(-1), b_fc1.reshape(-1)]
    )
    small = jnp.pad(small, (0, -small.shape[0] % 128))[None]
    small = in_order(z % 2, small, to_z(small, 1), 0)
    small = in_order(z // 2, small, to_z(small, 2), 0)
    small = in_order(c, small, to_core(small), 0)
    small = in_order(x, small, to_x(small), 0)

    parts_in = send_away(tokens, never(small))

    pairs = w_qkv.shape[2] // PAIR // 2
    head_chunks = 2 if pairs % 2 == 0 else 1
    chunk_pairs = pairs // head_chunks
    qkv_cols = chunk_pairs * 3 * PAIR
    out_cols = chunk_pairs * PAIR
    hid = w_fc1.shape[1] // 2
    mlp_chunks = 2
    mlp_cols = hid // mlp_chunks
    qkv_split = w_qkv.reshape(d_own, 3, 2, head_chunks, chunk_pairs, PAIR).transpose(2, 3, 0, 4, 1, 5)
    qkv_split = qkv_split.reshape(2, head_chunks, d_own, qkv_cols)
    out_split = w_out.T.reshape(d_own, 2, head_chunks, out_cols).transpose(1, 2, 0, 3)
    heads_split = jnp.concatenate([qkv_split, out_split], axis=-1)
    fc1_split = w_fc1.reshape(d_own, 2, hid).transpose(1, 0, 2)
    fc2_split = w_fc2.T.reshape(d_own, 2, hid).transpose(1, 0, 2)

    def swap_cores(split):
        mine = lax.dynamic_index_in_dim(split, c, 0, keepdims=False)
        return mine, to_core(lax.dynamic_index_in_dim(split, 1 - c, 0, keepdims=False))

    def gather_weight(pair, at, width, wait=0):
        mine, other = (v[:, at : at + width] for v in pair)
        shard = in_order(c + wait, mine[None], other[None], 0)
        got = lax.all_gather(shard, ("x", "ctx"), axis=1, tiled=True)
        return got.reshape(model, width)

    first_cols = qkv_cols + out_cols
    heads_w = [gather_weight(swap_cores(heads_split[:, 0]), 0, first_cols)]
    more_split = jnp.concatenate([*(heads_split[:, n] for n in range(1, head_chunks)), fc1_split, fc2_split], axis=-1)
    more_pair = swap_cores(more_split)
    tokens_there = never(parts_in)
    parts_grad = send_away(grad_out, tokens_there)
    for n in range(1, head_chunks):
        heads_w.append(gather_weight(more_pair, (n - 1) * first_cols, first_cols, tokens_there))
    at = (head_chunks - 1) * first_cols
    fc1_w = gather_weight(more_pair, at, hid, tokens_there)
    fc2_w = gather_weight(more_pair, at + hid, hid, tokens_there)

    n_own = n_dp * n_ctx
    at = 0

    def take(count):
        nonlocal at
        got = small[:, at : at + count]
        at += count
        return got

    gain, shift, out_bias, fc2_bias = (take(d_own).reshape(model).astype(wide) for _ in range(4))
    heads_here, dims_here = b_qkv.shape[1:]
    qkv_bias = take(b_qkv.size).reshape(n_own, 3, heads_here, dims_here)
    qkv_bias = qkv_bias.transpose(1, 2, 0, 3).reshape(3, 2, head_chunks, chunk_pairs, PAIR)
    qkv_bias = lax.dynamic_index_in_dim(qkv_bias, c, 1, keepdims=False)
    qkv_bias = qkv_bias.transpose(1, 2, 0, 3).reshape(head_chunks, 1, qkv_cols).astype(wide)
    fc1_bias = take(b_fc1.size).reshape(n_own, b_fc1.shape[0], b_fc1.shape[1])
    fc1_bias = fc1_bias.transpose(1, 0, 2).reshape(2, 1, hid)
    fc1_bias = lax.dynamic_index_in_dim(fc1_bias, c, 0, keepdims=False).astype(wide)

    order_row = jnp.where(z // 2 == c, group_order, to_core(group_order))
    order_row = lax.dynamic_index_in_dim(order_row, z % 2, 0, keepdims=False)
    ids = jnp.arange(2 * n_mp * n_ctx, dtype=jnp.int32)
    at_core = (ids // (n_mp * n_ctx)) ^ c
    at_mp = (ids // n_ctx) % n_mp
    at_mp = at_mp ^ y if n_mp == 2 else at_mp
    at_ctx = ids % n_ctx
    slot = at_ctx * n_slot + at_core * (n_slot // 2) + at_mp * part
    chosen = (slot // block_len)[:, None] == jnp.arange(groups, dtype=jnp.int32)[None, :]
    block_at = jnp.sum(jnp.where(chosen, order_row[None, :], 0), axis=1)
    position = block_at * block_len + slot % block_len
    order = jnp.sum(jnp.where((position // part)[None, :] == ids[:, None], ids[None, :], 0), axis=1)
    tables = rotary_rows(SEQ_LEN)

    rows_in = parts_in.astype(wide)
    row_mean = jnp.mean(rows_in, axis=-1, keepdims=True)
    centered = rows_in - row_mean
    variance = jnp.mean(centered * centered, axis=-1, keepdims=True)
    inv_std = lax.rsqrt(variance + norm_eps)
    normed = centered * inv_std
    ln_out = gather_rows([(normed * gain + shift).astype(low)], [], [parts_grad])
    last = []

    def step(make, *deps):
        nonlocal last
        got = make([*last, *deps])
        last = [got[0] if isinstance(got, (tuple, list)) else got]
        return got

    def rows_step(a, chunks, width, kind, extra=None, deps=()):
        return step(lambda d: product_nn(flag_x, a, chunks, width, kind, extra, d), *deps)

    def far_sums(out, *deps):
        return out, to_x(step(lambda d: product_tn(flag_x, [out], 1, n_ctx, None, d), *deps)[0])

    def near_sums(far, *deps):
        out, came = far
        total = step(lambda d: product_tn(flag_x, [out], 0, n_ctx, came, d), *deps)[0]
        total = total.reshape(half, total.shape[-1])
        return lax.psum_scatter(total, "ctx", scatter_dimension=0, tiled=True)

    def feature_sums(lefts, weights, cols, *deps):
        rows = lefts[0][0].shape[0] // 2

        def run(block, add, split, more):
            return step(
                lambda d: product_nt(flag_x, lefts, weights, cols, block, rows, add, split, d), *more
            )

        came = to_core(run(1, None, False, deps))

        def two(*more):
            if n_mp == 2:
                mine, other = run(0, came, True, more)
                return mine, to_y(other)
            got = run(0, came, False, more)
            return lax.psum_scatter(got, "mp", scatter_dimension=0, tiled=True).astype(wide), None

        return two

    def joined(mine, came):
        return mine if came is None else mine + came.astype(wide)

    chunk_ids = range(head_chunks)
    both = range(mlp_chunks)
    qkv = [rows_step(ln_out, [(heads_w[0], 0)], qkv_cols, "bias", qkv_bias[0])]
    grad_rows = gather_rows([parts_grad], qkv, [])
    pulled = [rows_step(grad_rows, [(heads_w[0], 3)], out_cols, "plain")]
    for n in range(1, head_chunks):
        qkv.append(rows_step(ln_out, [(heads_w[n], 0)], qkv_cols, "bias", qkv_bias[n]))
        pulled.append(rows_step(grad_rows, [(heads_w[n], 3)], out_cols, "plain"))
    heads, heads_out, far_heads = [], [], []
    for n in chunk_ids:
        heads.append(step(lambda d: attention(order, qkv[n], pulled[n], tables, d)))
        mixed, grad_qkv = heads[n]
        heads_out.append([(ln_out, grad_qkv, 0, qkv_cols), (grad_rows, mixed, 0, out_cols)])
        far_heads.append(far_sums(heads_out[n]))
    act, slope = rows_step(ln_out, [(fc1_w, n) for n in both], mlp_cols, "gelu", fc1_bias)
    fc2_out = [[(grad_rows, act, n, mlp_cols)] for n in both]
    far_2a = far_sums(fc2_out[0], far_heads[0][1])
    attn_two = feature_sums([(h[0], 0, out_cols) for h in heads], heads_w, [3] * head_chunks)
    far_2b = far_sums(fc2_out[1])
    grad_heads = [near_sums(far_heads[0])]
    grad_pre = rows_step(
        grad_rows, [(fc2_w, n) for n in both], mlp_cols, "times", (slope, 0), (far_heads[-1][1],)
    )
    fc1_out = [[(ln_out, grad_pre, n, mlp_cols)] for n in both]
    far_1a = far_sums(fc1_out[0], far_2a[1])
    mlp_two = feature_sums([(act, 0, hid)], [fc2_w], [0])
    grad_heads += [near_sums(far) for far in far_heads[1:]]
    attn_mine, attn_came = attn_two()
    ln_two = feature_sums(
        [(grad_pre, 0, hid)] + [(h[1], 0, qkv_cols) for h in heads],
        [fc1_w, *heads_w],
        [0] * (1 + head_chunks),
    )
    mlp_mine, mlp_came = mlp_two()
    far_1b = far_sums(fc1_out[1], far_2b[1])
    grad_2 = [near_sums(far_2a, grad_heads[0])]
    grad_2.append(near_sums(far_2b))
    attn_out = joined(attn_mine, attn_came) + out_bias
    mlp_out = joined(mlp_mine, mlp_came) + fc2_bias
    block_rows = (rows_in + attn_out + mlp_out).astype(low)
    block_homes = send_home(block_rows)
    ln_mine, ln_came = ln_two(far_1a[1], block_rows)
    grad_1 = [near_sums(far_1a, grad_heads[-1], far_1b[1], block_homes[0])]
    grad_1.append(near_sums(far_1b, grad_2[0], block_homes[1]))

    grad_ln = ln_mine if ln_came is None else ln_mine + ln_came.astype(wide)
    scaled = grad_ln * gain
    back = inv_std * (
        scaled
        - jnp.mean(scaled, axis=-1, keepdims=True)
        - normed * jnp.mean(scaled * normed, axis=-1, keepdims=True)
    )
    back = back.astype(low)
    grad_homes = send_home(back)
    block_out = placed_home(*block_homes)
    grad_tokens = placed_home(*grad_homes, grad_out)
    gain_sum = jnp.sum(grad_ln * normed, axis=0)
    shift_sum = jnp.sum(grad_ln, axis=0)

    shared = jnp.concatenate(
        [
            gain_sum,
            shift_sum,
            jnp.sum(parts_grad.astype(wide), axis=0),
            jnp.stack(
                [
                    jnp.sum(rows_in * rows_in),
                    jnp.sum(attn_out * attn_out),
                    jnp.sum(mlp_out * mlp_out),
                ]
            ),
            jnp.zeros((125,), wide),
        ]
    )
    own = jnp.concatenate(
        [jnp.sum(v.astype(wide), axis=0) for v in [*(h[1] for h in heads), grad_pre]]
    )
    n_shared = shared.shape[0]
    sums = jnp.concatenate([shared, own])
    sums = sums + to_x(sums)
    sums = sums + to_z(sums, 1)
    sums = sums + to_z(sums, 2)
    if n_mp == 2:
        shared = sums[:n_shared]
        shared = shared + to_y(shared)
    else:
        shared = lax.psum(sums[:n_shared], "mp")
    sums = jnp.concatenate([shared, sums[n_shared:]])
    came = to_core(sums)
    shared = sums[:n_shared] + came[:n_shared]
    own = in_order(c, sums[None, n_shared:], came[None, n_shared:], 0)
    place = dp * n_ctx + z

    def own_slice(v):
        return lax.dynamic_slice_in_dim(v, place * d_own, d_own, 0)

    grad_gain = own_slice(shared[:model])
    grad_shift = own_slice(shared[model : 2 * model])
    grad_bias_out = own_slice(shared[2 * model : 3 * model])
    cells = n_dp * n_seq * SEQ_LEN * model
    root_means = jnp.sqrt(shared[3 * model : 3 * model + 3] / cells)
    n_heads = head_chunks * qkv_cols
    grad_b_qkv = own[:, :n_heads].reshape(2, pairs, 3, PAIR).transpose(2, 0, 1, 3)
    grad_b_qkv = grad_b_qkv.reshape(3, heads_here, HD)
    grad_b_qkv = lax.dynamic_slice_in_dim(grad_b_qkv, place * dims_here, dims_here, 2)
    grad_b_fc1 = own[:, n_heads:].reshape(b_fc1.shape[0], HD)
    grad_b_fc1 = lax.dynamic_slice_in_dim(grad_b_fc1, place * dims_here, dims_here, 1)

    def by_owner(parts):
        whole = jnp.stack([p.reshape(2, d_own, -1) for p in parts], axis=1)
        mine = lax.dynamic_index_in_dim(whole, c, 0, keepdims=True)
        other = to_core(lax.dynamic_index_in_dim(whole, 1 - c, 0, keepdims=True))
        return in_order(c, mine, other, 0)

    def join(v):
        return v.transpose(2, 0, 1, 3).reshape(d_own, -1).astype(wide)

    grad_h = by_owner(grad_heads)
    grad_w_qkv = grad_h[..., :qkv_cols].reshape(2, head_chunks, d_own, chunk_pairs, 3, PAIR)
    grad_w_qkv = grad_w_qkv.transpose(2, 4, 0, 1, 3, 5).reshape(d_own, 3, -1).astype(wide)
    grad_w_out = join(grad_h[..., qkv_cols:]).T
    return (
        block_out,
        grad_tokens,
        grad_gain,
        grad_shift,
        grad_w_qkv,
        grad_b_qkv,
        grad_w_out,
        grad_bias_out,
        join(by_owner(grad_1)),
        grad_b_fc1,
        join(by_owner(grad_2)).T,
        grad_bias_out,
        root_means,
    )


def solution(mesh):
    n_dp, n_ctx, n_mp = (mesh.shape[name] for name in ("dp", "ctx", "mp"))
    split = jax.sharding.Mesh(
        mesh.devices.reshape(n_dp // 2, 2, n_ctx, n_mp), ("x", "core", "ctx", "mp")
    )
    rows = ("x", "core")
    owners = ("x", "core", "ctx")
    return jax.shard_map(
        on_device,
        mesh=split,
        in_specs=(
            P(rows, "ctx", None),
            P(rows, None),
            P(rows, "ctx", None),
            P(owners),
            P(owners),
            P(owners, None, "mp"),
            P(None, "mp", owners),
            P("mp", owners),
            P(owners),
            P(owners, "mp"),
            P("mp", owners),
            P("mp", owners),
            P(owners),
        ),
        out_specs=(
            P(rows, "ctx", None),
            P(rows, "ctx", None),
            P(owners),
            P(owners),
            P(owners, None, "mp"),
            P(None, "mp", owners),
            P("mp", owners),
            P(owners),
            P(owners, "mp"),
            P("mp", owners),
            P("mp", owners),
            P(owners),
            P(),
        ),
        check_vma=False,
    )
```

time: 1490 us -> 1040 us (0.70)
  matrix products: 268 us -> 0 us
  blocking collectives: 253 us -> 0 us
  Pallas kernels: 184 us -> 402 us
  local copies, waits for them, and re-layouts: 132 us -> 74.9 us
  waiting for transfers between devices: 489 us -> 436 us
  other arithmetic: 84.2 us -> 51.8 us
    dot_general x18 -> x0, matrix products: 268 us -> none  [the longest x4 93.4 us: mm(): return jnp.dot(a, b, preferred_element_type=wide)]
    ppermute x51 -> x37, waiting for transfers between devices: 489 us -> 240 us  [the longest x8 182 us: to_y(): return lax.ppermute(v, 'mp', [(0, 1), (1, 0)])]
    pallas_call x1 -> x32, Pallas kernels: 184 us -> 402 us  [the longest x30 318 us: call(): pl.pallas_call(inner, grid_spec=pltpu.PrefetchScalarGridSpec(num_scalar_p...]
    unnamed x1 -> x0, blocking collectives: 187 us -> none
    all_to_all x0 -> x4, waiting for transfers between devices: none -> 180 us  [to_ctx(): return lax.all_to_all(v, 'ctx', 0, 0, tiled=True)]
    psum x2 -> x0, blocking collectives: 65.8 us -> none  [the longest x1 46.3 us: on_device(): shared = lax.psum(shared, ('dp', 'ctx', 'mp'))]
    unnamed x139 -> x127, local copies, waits for them, and re-layouts: 70.5 us -> 37.4 us
    ppermute x51 -> x37, starting transfers between devices: 56.5 us -> 28.7 us  [the longest x8 10.7 us: to_y(): return lax.ppermute(v, 'mp', [(0, 1), (1, 0)])]
  transfers between devices with their start and end apart: 58 -> 51, of which waited for: 21 -> 27; matrix products, arithmetic and copies ran while one was open for 32% -> 8% of each run, Pallas kernels for 12% -> 39%
where the time goes in v2:
time: 1040 us; the launch traced here: 1030 us
  waiting for transfers between devices  436 us (42%)
  Pallas kernels  402 us (39%)
  local copies, waits for them, and re-layouts  74.9 us (7%)
  other arithmetic  51.8 us (5%)
  starting transfers between devices  47.8 us (5%)
  between operations  18.1 us (2%)
    pallas_call x30, Pallas kernels, call(): pl.pallas_call(inner, grid_spec=pltpu.PrefetchScalarGridSpec(num_scalar_p...  318 us
    ppermute x8, waiting for transfers between devices, to_y(): return lax.ppermute(v, 'mp', [(0, 1), (1, 0)])  182 us
    all_to_all x4, waiting for transfers between devices, to_ctx(): return lax.all_to_all(v, 'ctx', 0, 0, tiled=True)  180 us
    pallas_call x2, Pallas kernels, attention(): pl.pallas_call(inner, grid_spec=pltpu.PrefetchScalarGridSpec(num_scalar_p...  84.4 us
    unnamed x127, local copies, waits for them, and re-layouts  37.4 us
    ppermute x8, waiting for transfers between devices, to_x(): return lax.ppermute(v, 'x', [(0, 1), (1, 0)])  33.7 us
  transfers between devices with their start and end apart: 51, of which 27 were waited for; matrix products, arithmetic and copies ran while one was open for 8% of the time, Pallas kernels for 39%

profile of v2, /device:TPU:0, one launch (start us, length us, event | category | flops | bytes accessed | tf_op | source)
XLA Modules:
  0.0 1030.5 jit_solution(4575858686913090020)
XLA Ops:
  54.5 71.4 %all-to-all-done = bf16[4,128,2048]{2,1,0:T(8,128)(2,1)S(1)} async-done(((bf16[4,128,2048]{2,1,0:T(8,128)(2,1)}), bf16[4,128,2048]{2,1,0:T(8,128)(2,1)S(1)}, u32[]{:S(2)}, u32[]{:S(2)}) %all-to-all-start) | async-done | bytes 2097184 | tf_op jit(solution)/shard_map/all_to_all | solution.py:552
  149.7 35.7 %collective-permute-done.7.refs_1_ = bf16[512,2048]{1,0:T(8,128)(2,1)} collective-permute-done((bf16[512,2048]{1,0:T(8,128)(2,1)}, bf16[512,2048]{1,0:T(8,128)(2,1)}, u32[]{:S(2)}, u32[]{:S(2)}) %collective-permute-start.7) | collective-permute-done | bytes 2097184 | tf_op jit(solution)/shard_map/ppermute | solution.py:542
  190.7 41.9 %all-to-all-done.1 = bf16[4,128,2048]{2,1,0:T(8,128)(2,1)S(1)} async-done(((bf16[4,128,2048]{2,1,0:T(8,128)(2,1)}), bf16[4,128,2048]{2,1,0:T(8,128)(2,1)S(1)}, u32[]{:S(2)}, u32[]{:S(2)}) %all-to-all-start.1) | async-done | bytes 2097184 | tf_op jit(solution)/shard_map/all_to_all | solution.py:552
  236.6 9.5 stack_rows.5.refs_0_.refs_1_.refs_2_.refs_3_.refs_4_
  248.7 10.3 %rows_bias.2.refs_0_.refs_1_ = f32[2048,768]{1,0:T(8,128)} custom-call(s32[1]{0:T(128)} %bitcast.7.flag_ref, bf16[2048,2048]{1,0:T(8,128)(2,1)} %stack_rows.5.refs_0_.refs_1_.refs_2_.refs_3_.refs_4_, bf16[2048,2048]{1,0:T(8,128)(2,1)} %stack_rows.5.refs_0_.refs_1_.refs_2_.refs_3_.refs_4_, ...), custom_call_target="tpu_custom_call" | custom-call | flops 6442450944 | bytes 17825792 | tf_op jit(solution)/shard_map/rows_bias/pallas_call | solution.py:243
  259.0 21.0 %collective-permute-done.10.refs_2_ = bf16[512,2048]{1,0:T(8,128)(2,1)} collective-permute-done((bf16[512,2048]{1,0:T(8,128)(2,1)S(1)}, bf16[512,2048]{1,0:T(8,128)(2,1)}, u32[]{:S(2)}, u32[]{:S(2)}) %collective-permute-start.10) | collective-permute-done | bytes 2097184 | tf_op jit(solution)/shard_map/ppermute | solution.py:542
  310.9 10.5 %rows_bias.3.refs_0_.refs_1_ = f32[2048,768]{1,0:T(8,128)} custom-call(s32[1]{0:T(128)} %bitcast.7.flag_ref, bf16[2048,256]{1,0:T(8,128)(2,1)S(1)} %rows_plain.2.refs_0_.refs_2_, bf16[2048,2048]{1,0:T(8,128)(2,1)} %stack_rows.5.refs_0_.refs_1_.refs_2_.refs_3_.refs_4_, bf16[2048,2048]{1,0:T(8,128)(2,1)} %stack_rows.5.refs_0_.refs_1_.refs_2_.refs_3_.refs_4_, ...), custom_call_target="tpu_custom_call" | custom-call | flops 6442450944 | bytes 17825792 | tf_op jit(solution)/shard_map/rows_bias/pallas_call | solution.py:243
  328.3 42.6 %attention.2 = (bf16[2048,256]{1,0:T(8,128)(2,1)S(1)}, bf16[2048,768]{1,0:T(8,128)(2,1)}) custom-call(s32[16]{0:T(128)S(1)} %select_reduce_fusion.order_ref, bf16[2048,256]{1,0:T(8,128)(2,1)S(1)} %rows_plain.3.refs_0_.refs_2_, f32[2048,768]{1,0:T(8,128)} %rows_bias.2.refs_0_.refs_1_, bf16[2048,256]{1,0:T(8,128)(2,1)S(1)} %copy-done.25, ...), custom_call_target="tpu_custom_call" | custom-call | flops 25769803776 | bytes 30000000 | tf_op jit(solution)/shard_map/attention/pallas_call | solution.py:202
  370.8 9.5 weight_sums.12.refs_0_
  381.9 41.8 %attention.3 = (bf16[2048,256]{1,0:T(8,128)(2,1)S(1)}, bf16[2048,768]{1,0:T(8,128)(2,1)}) custom-call(s32[16]{0:T(128)S(1)} %select_reduce_fusion.order_ref, bf16[4,2,128,1024]{3,2,1,0:T(8,128)(2,1)} %weight_sums.12.refs_0_, f32[2048,768]{1,0:T(8,128)} %rows_bias.3.refs_0_.refs_1_, bf16[2048,256]{1,0:T(8,128)(2,1)S(1)} %rows_plain.3.refs_0_.refs_2_, ...), custom_call_target="tpu_custom_call" | custom-call | flops 25769803776 | bytes 30000000 | tf_op jit(solution)/shard_map/attention/pallas_call | solution.py:202
  433.5 31.0 %rows_gelu.1 = (bf16[2048,2048]{1,0:T(8,128)(2,1)}, bf16[2048,2048]{1,0:T(8,128)(2,1)}) custom-call(s32[1]{0:T(128)} %bitcast.7.flag_ref, bf16[4,2,128,1024]{3,2,1,0:T(8,128)(2,1)} %weight_sums.13.refs_0_, bf16[2048,2048]{1,0:T(8,128)(2,1)} %stack_rows.5.refs_0_.refs_1_.refs_2_.refs_3_.refs_4_, ...), custom_call_target="tpu_custom_call" | custom-call | flops 17179869184 | bytes 33554432 | tf_op jit(solution)/shard_map/rows_gelu/pallas_call | solution.py:243
  498.7 21.7 %collective-permute-done.14.refs_1_.refs_5_ = bf16[4,2,128,1024]{3,2,1,0:T(8,128)(2,1)} collective-permute-done((bf16[4,2,128,1024]{3,2,1,0:T(8,128)(2,1)}, bf16[4,2,128,1024]{3,2,1,0:T(8,128)(2,1)}, u32[]{:S(2)}, u32[]{:S(2)}) %collective-permute-start.14) | collective-permute-done | bytes 2097184 | tf_op jit(solution)/shard_map/ppermute | solution.py:536
  520.3 12.8 %all-gather.11.cloned.1.call-done = bf16[2,1024,2048]{2,1,0:T(8,128)(2,1)} async-done(((bf16[2,128,2048]{2,1,0:T(8,128)(2,1)}), bf16[2,1024,2048]{2,1,0:T(8,128)(2,1)}) %all-gather.11.cloned.1.call-update) | async-done | bytes 8388624 | tf_op jit(solution)/shard_map/all_gather | solution.py:620
  534.7 24.6 %rows_times.1.refs_0_.refs_3_.refs_1_.refs_5_.refs_4_ = bf16[2048,2048]{1,0:T(8,128)(2,1)} custom-call(s32[1]{0:T(128)} %bitcast.7.flag_ref, bf16[4,2,128,1024]{3,2,1,0:T(8,128)(2,1)S(1)} %copy-done.15, bf16[4,2,128,1024]{3,2,1,0:T(8,128)(2,1)} %collective-permute-done.14.refs_1_.refs_5_, ...), custom_call_target="tpu_custom_call" | custom-call | flops 17179869184 | bytes 33554432 | tf_op jit(solution)/shard_map/rows_times/pallas_call | solution.py:243
  572.8 14.2 %feature_sums.7.refs_0_ = bf16[1024,2048]{1,0:T(8,128)(2,1)} custom-call(s32[1]{0:T(128)} %bitcast.7.flag_ref, bf16[4,2,128,1024]{3,2,1,0:T(8,128)(2,1)S(1)} %weight_sums.17.refs_0_, bf16[2048,2048]{1,0:T(8,128)(2,1)} %get-tuple-element.29.refs_0_.refs_3_.refs_2_.refs_1_, bf16[2048,2048]{1,0:T(8,128)(2,1)} %bitcast.177), custom_call_target="tpu_custom_call" | custom-call | flops 8589934592 | bytes 20971520 | tf_op jit(solution)/shard_map/feature_sums/pallas_call | solution.py:243
  608.1 21.1 %feature_sums.9.refs_0_ = bf16[1024,2048]{1,0:T(8,128)(2,1)} custom-call(s32[1]{0:T(128)} %bitcast.7.flag_ref, f32[512,2048]{1,0:T(8,128)} %get-tuple-element.31.refs_0_, bf16[2048,2048]{1,0:T(8,128)(2,1)} %rows_times.1.refs_0_.refs_3_.refs_1_.refs_5_.refs_4_, bf16[2048,768]{1,0:T(8,128)(2,1)S(1)} %copy-done.4, ...), custom_call_target="tpu_custom_call" | custom-call | flops 15032385536 | bytes 30408704 | tf_op jit(solution)/shard_map/feature_sums/pallas_call | solution.py:243
  629.2 13.9 %feature_sums.10 = (f32[512,2048]{1,0:T(8,128)}, bf16[512,2048]{1,0:T(8,128)(2,1)}) custom-call(s32[1]{0:T(128)} %bitcast.7.flag_ref, bf16[1024,2048]{1,0:T(8,128)(2,1)} %feature_sums.9.refs_0_, bf16[2048,2048]{1,0:T(8,128)(2,1)} %get-tuple-element.29.refs_0_.refs_3_.refs_2_.refs_1_, bf16[2048,2048]{1,0:T(8,128)(2,1)} %bitcast.178, ...), custom_call_target="tpu_custom_call" | custom-call | flops 8589934592 | bytes 20971520 | tf_op jit(solution)/shard_map/feature_sums/pallas_call | solution.py:243
  667.7 31.5 %collective-permute-done.19 = bf16[512,2048]{1,0:T(8,128)(2,1)} collective-permute-done((bf16[512,2048]{1,0:T(8,128)(2,1)}, bf16[512,2048]{1,0:T(8,128)(2,1)}, u32[]{:S(2)}, u32[]{:S(2)}) %collective-permute-start.19) | collective-permute-done | bytes 2097184 | tf_op jit(solution)/shard_map/ppermute | solution.py:542
  725.2 66.9 %all-to-all-done.2 = bf16[4,128,2048]{2,1,0:T(8,128)(2,1)} async-done(((bf16[4,128,2048]{2,1,0:T(8,128)(2,1)}), bf16[4,128,2048]{2,1,0:T(8,128)(2,1)}, u32[]{:S(2)}, u32[]{:S(2)}) %all-to-all-start.2) | async-done | bytes 2097184 | tf_op jit(solution)/shard_map/all_to_all | solution.py:552
  794.3 22.2 %feature_sums.11 = (f32[512,2048]{1,0:T(8,128)}, bf16[512,2048]{1,0:T(8,128)(2,1)}) custom-call(s32[1]{0:T(128)} %bitcast.7.flag_ref, bf16[4,2,128,1024]{3,2,1,0:T(8,128)(2,1)S(1)} %copy-done.19, bf16[4,2,128,1024]{3,2,1,0:T(8,128)(2,1)} %collective-permute-done.23.refs_1_.refs_6_, bf16[512,2048]{1,0:T(8,128)(2,1)} %get-tuple-element.83.refs_2_, ...), custom_call_target="tpu_custom_call" | custom-call | flops 15032385536 | bytes 30408704 | tf_op jit(solution)/shard_map/feature_sums/pallas_call | solution.py:243
  830.4 34.4 %collective-permute-done.25 = bf16[512,2048]{1,0:T(8,128)(2,1)} collective-permute-done((bf16[512,2048]{1,0:T(8,128)(2,1)}, bf16[512,2048]{1,0:T(8,128)(2,1)}, u32[]{:S(2)}, u32[]{:S(2)}) %collective-permute-start.25) | collective-permute-done | bytes 2097184 | tf_op jit(solution)/shard_map/ppermute | solution.py:542
  879.9 37.1 %collective-permute-done.21.refs_1_.refs_2_ = bf16[512,2048]{1,0:T(8,128)(2,1)} collective-permute-done((bf16[512,2048]{1,0:T(8,128)(2,1)}, bf16[512,2048]{1,0:T(8,128)(2,1)}, u32[]{:S(2)}, u32[]{:S(2)}) %collective-permute-start.21) | collective-permute-done | bytes 2097184 | tf_op jit(solution)/shard_map/ppermute | solution.py:542
  989.6 21.8 %collective-permute-done.27.refs_1_ = bf16[512,2048]{1,0:T(8,128)(2,1)} collective-permute-done((bf16[512,2048]{1,0:T(8,128)(2,1)S(1)}, bf16[512,2048]{1,0:T(8,128)(2,1)}, u32[]{:S(2)}, u32[]{:S(2)}) %collective-permute-start.27) | collective-permute-done | bytes 2097184 | tf_op jit(solution)/shard_map/ppermute | solution.py:542
  1011.4 9.5 place_rows.3
  (365 shorter events, 355.6 us)
Async XLA Ops:
  7.2 239.0 %all-gather.5.cloned.1.call-start = ((), (), s32[]{:S(2)}) async-start(), calls=%async_computation.10 | async-start | bytes 4718592 | tf_op jit(solution)/shard_map/all_gather | solution.py:620
  38.2 87.6 %all-to-all-start = ((bf16[4,128,2048]{2,1,0:T(8,128)(2,1)}), bf16[4,128,2048]{2,1,0:T(8,128)(2,1)S(1)}, u32[]{:S(2)}, u32[]{:S(2)}) async-start(bf16[4,128,2048]{2,1,0:T(8,128)(2,1)} %maximum_select_fusion), calls=%async_computation | async-start | bytes 4194304 | tf_op jit(solution)/shard_map/all_to_all | solution.py:552
  43.6 264.7 %all-gather.7.cloned.1.call-start = ((), (), s32[]{:S(2)}) async-start(), calls=%async_computation.11 | async-start | bytes 4718592 | tf_op jit(solution)/shard_map/all_gather | solution.py:620
  129.8 303.7 %all-gather.9.cloned.1.call-start = ((), (), s32[]{:S(2)}) async-start(), calls=%async_computation.12 | async-start | bytes 9437184 | tf_op jit(solution)/shard_map/all_gather | solution.py:620
  146.0 86.6 %all-to-all-start.1 = ((bf16[4,128,2048]{2,1,0:T(8,128)(2,1)}), bf16[4,128,2048]{2,1,0:T(8,128)(2,1)S(1)}, u32[]{:S(2)}, u32[]{:S(2)}) async-start(bf16[4,128,2048]{2,1,0:T(8,128)(2,1)} %maximum_select_fusion.1), calls=%async_computation.1 | async-start | bytes 4194304 | tf_op jit(solution)/shard_map/all_to_all | solution.py:552
  149.7 383.5 %all-gather.11.cloned.1.call-start = ((), (), s32[]{:S(2)}) async-start(), calls=%async_computation.13 | async-start | bytes 9437184 | tf_op jit(solution)/shard_map/all_gather | solution.py:620
  236.0 419.5 %reduce-scatter.7.cloned.1.call-start = ((), (), s32[]{:S(2)}) async-start(), calls=%async_computation.14 | async-start | bytes 2621440 | tf_op jit(solution)/shard_map/reduce_scatter | solution.py:693
  380.3 84.2 %collective-permute-start.13 = (bf16[4,2,128,1024]{3,2,1,0:T(8,128)(2,1)}, bf16[4,2,128,1024]{3,2,1,0:T(8,128)(2,1)}, u32[]{:S(2)}, u32[]{:S(2)}) collective-permute-start(bf16[4,2,128,1024]{3,2,1,0:T(8,128)(2,1)} %weight_sums.12.refs_0_), channel_id=1, source_target_pairs={{0,16},{16,0},{1,17},{17,1},{2,18},{18,2},{3,19},{19,3},{4,20},{20... | collective-permute-start | bytes 6291464 | tf_op jit(solution)/shard_map/ppermute | solution.py:536
  433.0 87.3 %collective-permute-start.14 = (bf16[4,2,128,1024]{3,2,1,0:T(8,128)(2,1)}, bf16[4,2,128,1024]{3,2,1,0:T(8,128)(2,1)}, u32[]{:S(2)}, u32[]{:S(2)}) collective-permute-start(bf16[4,2,128,1024]{3,2,1,0:T(8,128)(2,1)} %weight_sums.13.refs_0_), channel_id=1, source_target_pairs={{0,16},{16,0},{1,17},{17,1},{2,18},{18,2},{3,19},{19,3},{4,20},{20... | collective-permute-start | bytes 6291464 | tf_op jit(solution)/shard_map/ppermute | solution.py:536
  473.2 91.9 %collective-permute-start.15 = (bf16[4,2,128,1024]{3,2,1,0:T(8,128)(2,1)}, bf16[4,2,128,1024]{3,2,1,0:T(8,128)(2,1)}, u32[]{:S(2)}, u32[]{:S(2)}) collective-permute-start(bf16[4,2,128,1024]{3,2,1,0:T(8,128)(2,1)} %weight_sums.14.refs_0_), channel_id=1, source_target_pairs={{0,16},{16,0},{1,17},{17,1},{2,18},{18,2},{3,19},{19,3},{4,20},{20... | collective-permute-start | bytes 6291464 | tf_op jit(solution)/shard_map/ppermute | solution.py:536
  488.1 109.2 %collective-permute-start.16 = (bf16[1024,2048]{1,0:T(8,128)(2,1)}, bf16[1024,2048]{1,0:T(8,128)(2,1)}, u32[]{:S(2)}, u32[]{:S(2)}) collective-permute-start(bf16[1024,2048]{1,0:T(8,128)(2,1)} %feature_sums.6.refs_0_), channel_id=1, source_target_pairs={{0,8},{8,0},{1,9},{9,1},{2,10},{10,2},{3,11},{11,3},{4,12},{12,4},... | collective-permute-start | bytes 12582920 | tf_op jit(solution)/shard_map/ppermute | solution.py:533
  498.6 321.3 %reduce-scatter.9.cloned.1.call-start = ((), (), s32[]{:S(2)}) async-start(), calls=%async_computation.15 | async-start | bytes 2621440 | tf_op jit(solution)/shard_map/reduce_scatter | solution.py:693
  596.8 283.0 %reduce-scatter.13.cloned.1.call-start = ((), (), s32[]{:S(2)}) async-start(), calls=%async_computation.17 | async-start | bytes 2621440 | tf_op jit(solution)/shard_map/reduce_scatter | solution.py:693
  606.3 61.5 %collective-permute-start.17 = (bf16[512,2048]{1,0:T(8,128)(2,1)}, bf16[512,2048]{1,0:T(8,128)(2,1)}, u32[]{:S(2)}, u32[]{:S(2)}) collective-permute-start(bf16[512,2048]{1,0:T(8,128)(2,1)} %get-tuple-element.32), channel_id=1, source_target_pairs={{0,1},{1,0},{2,3},{3,2},{4,5},{5,4},{6,7},{7,6},{8,9},{9,8},{10,11... | collective-permute-start | bytes 6291464 | tf_op jit(solution)/shard_map/ppermute | solution.py:542
  643.1 56.1 %collective-permute-start.19 = (bf16[512,2048]{1,0:T(8,128)(2,1)}, bf16[512,2048]{1,0:T(8,128)(2,1)}, u32[]{:S(2)}, u32[]{:S(2)}) collective-permute-start(bf16[512,2048]{1,0:T(8,128)(2,1)} %get-tuple-element.34), channel_id=1, source_target_pairs={{0,1},{1,0},{2,3},{3,2},{4,5},{5,4},{6,7},{7,6},{8,9},{9,8},{10,11... | collective-permute-start | bytes 6291464 | tf_op jit(solution)/shard_map/ppermute | solution.py:542
  667.6 126.5 %collective-permute-start.24 = (bf16[1024,2048]{1,0:T(8,128)(2,1)}, bf16[1024,2048]{1,0:T(8,128)(2,1)}, u32[]{:S(2)}, u32[]{:S(2)}) collective-permute-start(bf16[1024,2048]{1,0:T(8,128)(2,1)} %feature_sums.9.refs_0_), channel_id=1, source_target_pairs={{0,8},{8,0},{1,9},{9,1},{2,10},{10,2},{3,11},{11,3},{4,12},{12,4},... | collective-permute-start | bytes 12582920 | tf_op jit(solution)/shard_map/ppermute | solution.py:533
  707.4 84.7 %all-to-all-start.2 = ((bf16[4,128,2048]{2,1,0:T(8,128)(2,1)}), bf16[4,128,2048]{2,1,0:T(8,128)(2,1)}, u32[]{:S(2)}, u32[]{:S(2)}) async-start(bf16[4,128,2048]{2,1,0:T(8,128)(2,1)} %bitcast.183), calls=%async_computation.2 | async-start | bytes 4194304 | tf_op jit(solution)/shard_map/all_to_all | solution.py:552
  712.1 247.2 %reduce-scatter.17.cloned.1.call-start = ((), (), s32[]{:S(2)}) async-start(), calls=%async_computation.19 | async-start | bytes 2621440 | tf_op jit(solution)/shard_map/reduce_scatter | solution.py:693
  712.1 82.0 %collective-permute-start.23 = (bf16[4,2,128,1024]{3,2,1,0:T(8,128)(2,1)}, bf16[4,2,128,1024]{3,2,1,0:T(8,128)(2,1)}, u32[]{:S(2)}, u32[]{:S(2)}) collective-permute-start(bf16[4,2,128,1024]{3,2,1,0:T(8,128)(2,1)} %copy-done.32), channel_id=1, source_target_pairs={{0,16},{16,0},{1,17},{17,1},{2,18},{18,2},{3,19},{19,3},{4,20},{20... | collective-permute-start | bytes 6291464 | tf_op jit(solution)/shard_map/ppermute | solution.py:536
  724.5 244.1 %reduce-scatter.11.cloned.1.call-start = ((), (), s32[]{:S(2)}) async-start(), calls=%async_computation.16 | async-start | bytes 2621440 | tf_op jit(solution)/shard_map/reduce_scatter | solution.py:693
  724.5 95.4 %collective-permute-start.34 = (bf16[4,2,128,1024]{3,2,1,0:T(8,128)(2,1)}, bf16[4,2,128,1024]{3,2,1,0:T(8,128)(2,1)}, u32[]{:S(2)}, u32[]{:S(2)}) collective-permute-start(bf16[4,2,128,1024]{3,2,1,0:T(8,128)(2,1)} %copy-done.20), channel_id=1, source_target_pairs={{0,16},{16,0},{1,17},{17,1},{2,18},{18,2},{3,19},{19,3},{4,20},{20... | collective-permute-start | bytes 6291464 | tf_op jit(solution)/shard_map/ppermute | solution.py:536
  816.5 48.3 %collective-permute-start.25 = (bf16[512,2048]{1,0:T(8,128)(2,1)}, bf16[512,2048]{1,0:T(8,128)(2,1)}, u32[]{:S(2)}, u32[]{:S(2)}) collective-permute-start(bf16[512,2048]{1,0:T(8,128)(2,1)} %get-tuple-element.36), channel_id=1, source_target_pairs={{0,1},{1,0},{2,3},{3,2},{4,5},{5,4},{6,7},{7,6},{8,9},{9,8},{10,11... | collective-permute-start | bytes 6291464 | tf_op jit(solution)/shard_map/ppermute | solution.py:542
  875.3 58.3 %all-to-all-start.3 = ((bf16[4,128,2048]{2,1,0:T(8,128)(2,1)}), bf16[4,128,2048]{2,1,0:T(8,128)(2,1)}, u32[]{:S(2)}, u32[]{:S(2)}) async-start(bf16[4,128,2048]{2,1,0:T(8,128)(2,1)} %bitcast.182), calls=%async_computation.4 | async-start | bytes 4194304 | tf_op jit(solution)/shard_map/all_to_all | solution.py:552
  879.8 93.3 %reduce-scatter.15.cloned.1.call-start = ((), (), s32[]{:S(2)}) async-start(), calls=%async_computation.18 | async-start | bytes 2621440 | tf_op jit(solution)/shard_map/reduce_scatter | solution.py:693
  (87 other events, 1165.5 us)
Sparse Core Ops, SparseCore 0:
  15.3 106.3 all-gather.4
  129.9 106.6 all-gather.6
  238.8 123.8 all-gather.8
  364.7 168.3 all-gather.10
  535.3 42.0 reduce-scatter.6
  597.0 44.0 reduce-scatter.8
  667.7 43.8 reduce-scatter.12
  724.6 66.5 reduce-scatter.16
  830.5 40.9 reduce-scatter.10
  929.4 43.6 reduce-scatter.14

commit v3 on v2

--- a/solution.py
+++ b/solution.py
@@ -422,28 +422,36 @@
     return out if split else out[0]
 
 
-def place_rows(flags, mine, other, n_seq, n_slot, base):
+def place_rows(flags, mine, mine_y, came, n_seq, n_slot, base):
     model = mine.shape[1]
     part = n_slot // 4
     out_type = low if base is None else wide
 
     def body(flag_ref, *refs):
-        own = pl.program_id(2) == flag_ref[1]
-
-        @pl.when(own)
+        own_core = pl.program_id(1) == flag_ref[0]
+        own_mp = pl.program_id(2) == flag_ref[1]
+
+        def put(ref):
+            got = ref[...]
+            refs[-1][...] = got if base is None else refs[3][...].astype(wide) + got.astype(wide)
+
+        @pl.when(own_core & own_mp)
         def _():
-            got = refs[0][...]
-            refs[-1][...] = got if base is None else refs[2][...].astype(wide) + got.astype(wide)
-
-        @pl.when(jnp.logical_not(own))
+            put(refs[0])
+
+        @pl.when(own_core & jnp.logical_not(own_mp))
         def _():
-            got = refs[1][...]
-            refs[-1][...] = got if base is None else refs[2][...].astype(wide) + got.astype(wide)
-
-    piece = pl.BlockSpec((part, model), lambda i, cc, yy, f: ((cc ^ f[0]) * n_seq + i, 0))
+            put(refs[1])
+
+        @pl.when(jnp.logical_not(own_core))
+        def _():
+            put(refs[2])
+
+    piece = pl.BlockSpec((part, model), lambda i, cc, yy, f: (n_seq * f[0] + i, 0))
+    other = pl.BlockSpec((part, model), lambda i, cc, yy, f: (n_seq * (yy ^ f[1]) + i, 0))
     slot = pl.BlockSpec((part, model), lambda i, cc, yy, f: (4 * i + 2 * cc + yy, 0))
-    in_specs = [piece, piece]
-    args = [mine, other]
+    in_specs = [piece, piece, other]
+    args = [mine, mine_y, came]
     if base is not None:
         in_specs.append(slot)
         args.append(base.reshape(n_seq * n_slot, model))
@@ -563,18 +571,23 @@
         return to_ctx(in_order(c, of_core(c), to_core(of_core(1 - c)), 0)).reshape(rows_own, model)
 
     def send_home(v):
-        got = to_ctx(v.reshape(n_ctx, part, model))
-        mine = lax.dynamic_slice_in_dim(got, n_seq * c, n_seq, 0)
-        other = to_core(lax.dynamic_slice_in_dim(got, n_seq * (1 - c), n_seq, 0))
-        homes = jnp.concatenate([mine, other], axis=0).reshape(rows_own, model)
-        return homes, (to_y(homes) if n_mp == 2 else homes)
-
-    def placed_home(homes, others, base=None):
+        return to_ctx(v.reshape(n_ctx, part, model))
+
+    def other_mp(got, wait=0):
+        return to_y(got + jnp.asarray(wait, got.dtype)) if n_mp == 2 else got
+
+    def placed_home(got, got_y, base=None):
+        def of_core(at):
+            return [lax.dynamic_slice_in_dim(v, n_seq * at, n_seq, 0) for v in (got, got_y)]
+
         if n_mp == 2:
-            return place_rows(flag_cy, homes, others, n_seq, n_slot, base)
-        homes = lax.all_gather(homes.reshape(2, n_seq, part, model), "mp", axis=2, tiled=True)
-        homes = jnp.where(c == 0, homes, homes[::-1])
-        got = jnp.swapaxes(homes, 0, 1).reshape(n_seq, n_slot, model)
+            came = to_core(jnp.concatenate(of_core(1 - c), axis=0))
+            flat = [v.reshape(rows_own, model) for v in (got, got_y, came)]
+            return place_rows(flag_cy, *flat, n_seq, n_slot, base)
+        mine = lax.all_gather(of_core(c)[0], "mp", axis=1, tiled=True)
+        other = to_core(lax.all_gather(of_core(1 - c)[0], "mp", axis=1, tiled=True))
+        got = jnp.where(c == 0, jnp.stack([mine, other]), jnp.stack([other, mine]))
+        got = jnp.swapaxes(got, 0, 1).reshape(n_seq, n_slot, model)
         return got if base is None else base.astype(wide) + got.astype(wide)
 
     def gather_rows(parts, deps_own, deps_all):
@@ -734,30 +747,30 @@
     attn_two = feature_sums([(h[0], 0, out_cols) for h in heads], heads_w, [3] * head_chunks)
     far_2b = far_sums(fc2_out[1])
     grad_heads = [near_sums(far_heads[0])]
-    grad_pre = rows_step(
-        grad_rows, [(fc2_w, n) for n in both], mlp_cols, "times", (slope, 0), (far_heads[-1][1],)
-    )
+    attn_mine, attn_came = attn_two()
+    mlp_two = feature_sums([(act, 0, hid)], [fc2_w], [0], far_heads[-1][1])
+    grad_heads += [near_sums(far) for far in far_heads[1:]]
+    mlp_mine, mlp_came = mlp_two()
+    grad_pre = rows_step(grad_rows, [(fc2_w, n) for n in both], mlp_cols, "times", (slope, 0))
     fc1_out = [[(ln_out, grad_pre, n, mlp_cols)] for n in both]
     far_1a = far_sums(fc1_out[0], far_2a[1])
-    mlp_two = feature_sums([(act, 0, hid)], [fc2_w], [0])
-    grad_heads += [near_sums(far) for far in far_heads[1:]]
-    attn_mine, attn_came = attn_two()
     ln_two = feature_sums(
         [(grad_pre, 0, hid)] + [(h[1], 0, qkv_cols) for h in heads],
         [fc1_w, *heads_w],
         [0] * (1 + head_chunks),
-    )
-    mlp_mine, mlp_came = mlp_two()
+        *([] if attn_came is None else [attn_came]),
+    )
     far_1b = far_sums(fc1_out[1], far_2b[1])
-    grad_2 = [near_sums(far_2a, grad_heads[0])]
-    grad_2.append(near_sums(far_2b))
     attn_out = joined(attn_mine, attn_came) + out_bias
     mlp_out = joined(mlp_mine, mlp_came) + fc2_bias
     block_rows = (rows_in + attn_out + mlp_out).astype(low)
-    block_homes = send_home(block_rows)
-    ln_mine, ln_came = ln_two(far_1a[1], block_rows)
-    grad_1 = [near_sums(far_1a, grad_heads[-1], far_1b[1], block_homes[0])]
-    grad_1.append(near_sums(far_1b, grad_2[0], block_homes[1]))
+    block_got = send_home(block_rows)
+    grad_2 = [near_sums(far_2a, grad_heads[0], block_rows)]
+    grad_2.append(near_sums(far_2b))
+    ln_mine, ln_came = ln_two(far_1a[1], block_got)
+    grad_1 = [near_sums(far_1a, grad_heads[-1], far_1b[1])]
+    block_y = other_mp(block_got, 0 if ln_came is None else never(ln_came))
+    grad_1.append(near_sums(far_1b, grad_2[0], block_y))
 
     grad_ln = ln_mine if ln_came is None else ln_mine + ln_came.astype(wide)
     scaled = grad_ln * gain
@@ -767,9 +780,9 @@
         - normed * jnp.mean(scaled * normed, axis=-1, keepdims=True)
     )
     back = back.astype(low)
-    grad_homes = send_home(back)
-    block_out = placed_home(*block_homes)
-    grad_tokens = placed_home(*grad_homes, grad_out)
+    grad_got = send_home(back)
+    block_out = placed_home(block_got, block_y)
+    grad_tokens = placed_home(grad_got, other_mp(grad_got), grad_out)
     gain_sum = jnp.sum(grad_ln * normed, axis=0)
     shift_sum = jnp.sum(grad_ln, axis=0)
 

time: 1040 us -> 999 us (0.961)
  waiting for transfers between devices: 436 us -> 378 us
    ppermute x8, waiting for transfers between devices: 182 us -> 143 us  [to_y(): return lax.ppermute(v, 'mp', [(0, 1), (1, 0)])]
    all_to_all x4, waiting for transfers between devices: 180 us -> 145 us  [to_ctx(): return lax.all_to_all(v, 'ctx', 0, 0, tiled=True)]
    ppermute x8, waiting for transfers between devices: 33.7 us -> 65.2 us  [to_x(): return lax.ppermute(v, 'x', [(0, 1), (1, 0)])]
    all_gather x4, waiting for transfers between devices: 12.8 us -> 0.03 us  [gather_weight(): got = lax.all_gather(shard, ('x', 'ctx'), axis=1, tiled=True)]
    unnamed x127 -> x121, local copies, waits for them, and re-layouts: 37.4 us -> 39.5 us
  transfers between devices with their start and end apart: 51 -> 51, of which waited for: 27 -> 22; matrix products, arithmetic and copies ran while one was open for 8% -> 10% of each run, Pallas kernels for 39% -> 40%
where the time goes in v3:
time: 999 us; the launch traced here: 989 us
  Pallas kernels  406 us (41%)
  waiting for transfers between devices  378 us (38%)
  local copies, waits for them, and re-layouts  80.3 us (8%)
  other arithmetic  55.4 us (6%)
  starting transfers between devices  50.3 us (5%)
  between operations  19.3 us (2%)
    pallas_call x30, Pallas kernels, call(): pl.pallas_call(inner, grid_spec=pltpu.PrefetchScalarGridSpec(num_scalar_p...  321 us
    all_to_all x4, waiting for transfers between devices, to_ctx(): return lax.all_to_all(v, 'ctx', 0, 0, tiled=True)  145 us
    ppermute x8, waiting for transfers between devices, to_y(): return lax.ppermute(v, 'mp', [(0, 1), (1, 0)])  143 us
    pallas_call x2, Pallas kernels, attention(): pl.pallas_call(inner, grid_spec=pltpu.PrefetchScalarGridSpec(num_scalar_p...  84.8 us
    ppermute x8, waiting for transfers between devices, to_x(): return lax.ppermute(v, 'x', [(0, 1), (1, 0)])  65.2 us
    unnamed x121, local copies, waits for them, and re-layouts  39.5 us
  transfers between devices with their start and end apart: 51, of which 22 were waited for; matrix products, arithmetic and copies ran while one was open for 10% of the time, Pallas kernels for 40%

profile of v3, /device:TPU:0, one launch (start us, length us, event | category | flops | bytes accessed | tf_op | source)
XLA Modules:
  0.0 989.1 jit_solution(7227195806708928696)
XLA Ops:
  54.5 71.3 %all-to-all-done = bf16[4,128,2048]{2,1,0:T(8,128)(2,1)S(1)} async-done(((bf16[4,128,2048]{2,1,0:T(8,128)(2,1)}), bf16[4,128,2048]{2,1,0:T(8,128)(2,1)S(1)}, u32[]{:S(2)}, u32[]{:S(2)}) %all-to-all-start) | async-done | bytes 2097184 | tf_op jit(solution)/shard_map/all_to_all | solution.py:560
  150.0 35.4 %collective-permute-done.7.refs_1_ = bf16[512,2048]{1,0:T(8,128)(2,1)} collective-permute-done((bf16[512,2048]{1,0:T(8,128)(2,1)}, bf16[512,2048]{1,0:T(8,128)(2,1)}, u32[]{:S(2)}, u32[]{:S(2)}) %collective-permute-start.7) | collective-permute-done | bytes 2097184 | tf_op jit(solution)/shard_map/ppermute | solution.py:550
  190.7 42.1 %all-to-all-done.1 = bf16[4,128,2048]{2,1,0:T(8,128)(2,1)S(1)} async-done(((bf16[4,128,2048]{2,1,0:T(8,128)(2,1)}), bf16[4,128,2048]{2,1,0:T(8,128)(2,1)S(1)}, u32[]{:S(2)}, u32[]{:S(2)}) %all-to-all-start.1) | async-done | bytes 2097184 | tf_op jit(solution)/shard_map/all_to_all | solution.py:560
  235.0 9.5 stack_rows.5.refs_0_.refs_1_.refs_2_.refs_3_.refs_4_
  247.2 10.5 %rows_bias.2.refs_0_.refs_1_ = f32[2048,768]{1,0:T(8,128)} custom-call(s32[1]{0:T(128)} %bitcast.7.flag_ref, bf16[2048,2048]{1,0:T(8,128)(2,1)} %stack_rows.5.refs_0_.refs_1_.refs_2_.refs_3_.refs_4_, bf16[2048,2048]{1,0:T(8,128)(2,1)} %stack_rows.5.refs_0_.refs_1_.refs_2_.refs_3_.refs_4_, ...), custom_call_target="tpu_custom_call" | custom-call | flops 6442450944 | bytes 17825792 | tf_op jit(solution)/shard_map/rows_bias/pallas_call | solution.py:243
  257.7 22.4 %collective-permute-done.10.refs_2_ = bf16[512,2048]{1,0:T(8,128)(2,1)} collective-permute-done((bf16[512,2048]{1,0:T(8,128)(2,1)S(1)}, bf16[512,2048]{1,0:T(8,128)(2,1)}, u32[]{:S(2)}, u32[]{:S(2)}) %collective-permute-start.10) | collective-permute-done | bytes 2097184 | tf_op jit(solution)/shard_map/ppermute | solution.py:550
  311.6 10.5 %rows_bias.3.refs_0_.refs_1_ = f32[2048,768]{1,0:T(8,128)} custom-call(s32[1]{0:T(128)} %bitcast.7.flag_ref, bf16[2048,256]{1,0:T(8,128)(2,1)S(1)} %rows_plain.2.refs_0_.refs_2_, bf16[2048,2048]{1,0:T(8,128)(2,1)} %stack_rows.5.refs_0_.refs_1_.refs_2_.refs_3_.refs_4_, bf16[2048,2048]{1,0:T(8,128)(2,1)} %stack_rows.5.refs_0_.refs_1_.refs_2_.refs_3_.refs_4_, ...), custom_call_target="tpu_custom_call" | custom-call | flops 6442450944 | bytes 17825792 | tf_op jit(solution)/shard_map/rows_bias/pallas_call | solution.py:243
  327.8 42.6 %attention.2 = (bf16[2048,256]{1,0:T(8,128)(2,1)S(1)}, bf16[2048,768]{1,0:T(8,128)(2,1)}) custom-call(s32[16]{0:T(128)S(1)} %select_reduce_fusion.order_ref, bf16[2048,256]{1,0:T(8,128)(2,1)S(1)} %rows_plain.3.refs_0_.refs_2_, f32[2048,768]{1,0:T(8,128)} %rows_bias.2.refs_0_.refs_1_, bf16[2048,256]{1,0:T(8,128)(2,1)S(1)} %rows_plain.2.refs_0_.refs_2_, ...), custom_call_target="tpu_custom_call" | custom-call | flops 25769803776 | bytes 30000000 | tf_op jit(solution)/shard_map/attention/pallas_call | solution.py:202
  370.4 10.1 %weight_sums.12.refs_0_ = bf16[4,2,128,1024]{3,2,1,0:T(8,128)(2,1)} custom-call(s32[1]{0:T(128)} %bitcast.7.flag_ref, bf16[2048,256]{1,0:T(8,128)(2,1)S(1)} %get-tuple-element.25.refs_0_.refs_4_.refs_1_, bf16[2048,2048]{1,0:T(8,128)(2,1)} %stack_rows.5.refs_0_.refs_1_.refs_2_.refs_3_.refs_4_, bf16[2048,2048]{1,0:T(8,128)(2,1)} %stack_rows.7.refs_1_.refs_2_.refs_3_.refs_4_, ...), custom_call_target="tpu_custom_call" | custom-call | flops 4294967296 | bytes 14680064 | tf_op jit(solution)/shard_map/weight_sums/pallas_call | solution.py:243
  381.9 42.2 %attention.3 = (bf16[2048,256]{1,0:T(8,128)(2,1)S(1)}, bf16[2048,768]{1,0:T(8,128)(2,1)}) custom-call(s32[16]{0:T(128)S(1)} %select_reduce_fusion.order_ref, bf16[4,2,128,1024]{3,2,1,0:T(8,128)(2,1)} %weight_sums.12.refs_0_, f32[2048,768]{1,0:T(8,128)} %rows_bias.3.refs_0_.refs_1_, bf16[2048,256]{1,0:T(8,128)(2,1)S(1)} %rows_plain.3.refs_0_.refs_2_, ...), custom_call_target="tpu_custom_call" | custom-call | flops 25769803776 | bytes 30000000 | tf_op jit(solution)/shard_map/attention/pallas_call | solution.py:202
  424.1 9.0 weight_sums.13.refs_0_
  433.1 30.9 %rows_gelu.1 = (bf16[2048,2048]{1,0:T(8,128)(2,1)}, bf16[2048,2048]{1,0:T(8,128)(2,1)}) custom-call(s32[1]{0:T(128)} %bitcast.7.flag_ref, bf16[4,2,128,1024]{3,2,1,0:T(8,128)(2,1)} %weight_sums.13.refs_0_, bf16[2048,2048]{1,0:T(8,128)(2,1)} %stack_rows.5.refs_0_.refs_1_.refs_2_.refs_3_.refs_4_, ...), custom_call_target="tpu_custom_call" | custom-call | flops 17179869184 | bytes 33554432 | tf_op jit(solution)/shard_map/rows_gelu/pallas_call | solution.py:243
  506.1 20.8 %collective-permute-done.16.refs_1_.refs_5_ = bf16[4,2,128,1024]{3,2,1,0:T(8,128)(2,1)} collective-permute-done((bf16[4,2,128,1024]{3,2,1,0:T(8,128)(2,1)}, bf16[4,2,128,1024]{3,2,1,0:T(8,128)(2,1)}, u32[]{:S(2)}, u32[]{:S(2)}) %collective-permute-start.16) | collective-permute-done | bytes 2097184 | tf_op jit(solution)/shard_map/ppermute | solution.py:544
  526.8 13.4 %feature_sums.8.refs_0_ = bf16[1024,2048]{1,0:T(8,128)(2,1)} custom-call(s32[1]{0:T(128)} %bitcast.7.flag_ref, f32[512,2048]{1,0:T(8,128)} %get-tuple-element.30.refs_0_, bf16[4,2,128,1024]{3,2,1,0:T(8,128)(2,1)} %collective-permute-done.16.refs_1_.refs_5_, bf16[2048,2048]{1,0:T(8,128)(2,1)} %get-tuple-element.29.refs_0_.refs_3_.refs_2_.refs_1_.refs_4_, ...), custom_call_target="tpu_custom_call" | custom-call | flops 8589934592 | bytes 20971520 | tf_op jit(solution)/shard_map/feature_sums/pallas_call | solution.py:243
  555.5 14.1 %feature_sums.9 = (f32[512,2048]{1,0:T(8,128)}, bf16[512,2048]{1,0:T(8,128)(2,1)S(1)}) custom-call(s32[1]{0:T(128)} %bitcast.7.flag_ref, bf16[4,2,128,1024]{3,2,1,0:T(8,128)(2,1)S(1)} %copy-done.18, bf16[2048,2048]{1,0:T(8,128)(2,1)} %get-tuple-element.29.refs_0_.refs_3_.refs_2_.refs_1_.refs_4_, bf16[2048,2048]{1,0:T(8,128)(2,1)} %bitcast.179, ...), custom_call_target="tpu_custom_call" | custom-call | flops 8589934592 | bytes 20971520 | tf_op jit(solution)/shard_map/feature_sums/pallas_call | solution.py:243
  572.2 24.6 %rows_times.1.refs_0_.refs_3_.refs_2_.refs_4_ = bf16[2048,2048]{1,0:T(8,128)(2,1)} custom-call(s32[1]{0:T(128)} %bitcast.7.flag_ref, f32[512,2048]{1,0:T(8,128)S(1)} %copy-done.13, bf16[2048,2048]{1,0:T(8,128)(2,1)} %stack_rows.7.refs_1_.refs_2_.refs_3_.refs_4_, bf16[2048,2048]{1,0:T(8,128)(2,1)} %stack_rows.7.refs_1_.refs_2_.refs_3_.refs_4_, ...), custom_call_target="tpu_custom_call" | custom-call | flops 17179869184 | bytes 33554432 | tf_op jit(solution)/shard_map/rows_times/pallas_call | solution.py:243
  604.5 22.3 %feature_sums.10.refs_0_ = bf16[1024,2048]{1,0:T(8,128)(2,1)} custom-call(s32[1]{0:T(128)} %bitcast.7.flag_ref, bf16[4,2,128,1024]{3,2,1,0:T(8,128)(2,1)S(1)} %weight_sums.18.refs_0_, bf16[512,2048]{1,0:T(8,128)(2,1)} %collective-permute-done.15.refs_1_, bf16[2048,2048]{1,0:T(8,128)(2,1)} %rows_times.1.refs_0_.refs_3_.refs_2_.refs_4_, ...), custom_call_target="tpu_custom_call" | custom-call | flops 15032385536 | bytes 30408704 | tf_op jit(solution)/shard_map/feature_sums/pallas_call | solution.py:243
  679.2 35.6 %collective-permute-done.21.refs_1_.refs_5_ = bf16[4,2,128,1024]{3,2,1,0:T(8,128)(2,1)} collective-permute-done((bf16[4,2,128,1024]{3,2,1,0:T(8,128)(2,1)}, bf16[4,2,128,1024]{3,2,1,0:T(8,128)(2,1)}, u32[]{:S(2)}, u32[]{:S(2)}) %collective-permute-start.21) | collective-permute-done | bytes 2097184 | tf_op jit(solution)/shard_map/ppermute | solution.py:544
  714.8 31.9 %all-to-all-done.2.refs_2_ = bf16[4,128,2048]{2,1,0:T(8,128)(2,1)} async-done(((bf16[4,128,2048]{2,1,0:T(8,128)(2,1)}), bf16[4,128,2048]{2,1,0:T(8,128)(2,1)}, u32[]{:S(2)}, u32[]{:S(2)}) %all-to-all-start.2) | async-done | bytes 2097184 | tf_op jit(solution)/shard_map/all_to_all | solution.py:560
  748.3 22.3 %feature_sums.11 = (f32[512,2048]{1,0:T(8,128)}, bf16[512,2048]{1,0:T(8,128)(2,1)}) custom-call(s32[1]{0:T(128)} %bitcast.7.flag_ref, bf16[4,2,128,1024]{3,2,1,0:T(8,128)(2,1)S(1)} %copy-done.16, bf16[4,2,128,1024]{3,2,1,0:T(8,128)(2,1)} %collective-permute-done.21.refs_1_.refs_5_, bf16[4,128,2048]{2,1,0:T(8,128)(2,1)} %all-to-all-done.2.refs_2_, ...), custom_call_target="tpu_custom_call" | custom-call | flops 15032385536 | bytes 30408704 | tf_op jit(solution)/shard_map/feature_sums/pallas_call | solution.py:243
  782.7 35.8 %collective-permute-done.23 = bf16[512,2048]{1,0:T(8,128)(2,1)} collective-permute-done((bf16[512,2048]{1,0:T(8,128)(2,1)}, bf16[512,2048]{1,0:T(8,128)(2,1)}, u32[]{:S(2)}, u32[]{:S(2)}) %collective-permute-start.23) | collective-permute-done | bytes 2097184 | tf_op jit(solution)/shard_map/ppermute | solution.py:550
  844.0 40.6 %collective-permute-done.24.refs_2_ = bf16[4,128,2048]{2,1,0:T(8,128)(2,1)} collective-permute-done((bf16[4,128,2048]{2,1,0:T(8,128)(2,1)}, bf16[4,128,2048]{2,1,0:T(8,128)(2,1)}, u32[]{:S(2)}, u32[]{:S(2)}) %collective-permute-start.24) | collective-permute-done | bytes 2097184 | tf_op jit(solution)/shard_map/ppermute | solution.py:550
  887.3 8.9 weight_sums.23
  971.7 9.9 place_rows.3
  (363 shorter events, 353.0 us)
Async XLA Ops:
  7.2 237.4 %all-gather.5.cloned.1.call-start = ((), (), s32[]{:S(2)}) async-start(), calls=%async_computation.10 | async-start | bytes 4718592 | tf_op jit(solution)/shard_map/all_gather | solution.py:633
  38.3 87.6 %all-to-all-start = ((bf16[4,128,2048]{2,1,0:T(8,128)(2,1)}), bf16[4,128,2048]{2,1,0:T(8,128)(2,1)S(1)}, u32[]{:S(2)}, u32[]{:S(2)}) async-start(bf16[4,128,2048]{2,1,0:T(8,128)(2,1)} %maximum_select_fusion), calls=%async_computation | async-start | bytes 4194304 | tf_op jit(solution)/shard_map/all_to_all | solution.py:560
  43.7 265.8 %all-gather.7.cloned.1.call-start = ((), (), s32[]{:S(2)}) async-start(), calls=%async_computation.11 | async-start | bytes 4718592 | tf_op jit(solution)/shard_map/all_gather | solution.py:633
  129.8 303.2 %all-gather.9.cloned.1.call-start = ((), (), s32[]{:S(2)}) async-start(), calls=%async_computation.12 | async-start | bytes 9437184 | tf_op jit(solution)/shard_map/all_gather | solution.py:633
  146.2 86.6 %all-to-all-start.1 = ((bf16[4,128,2048]{2,1,0:T(8,128)(2,1)}), bf16[4,128,2048]{2,1,0:T(8,128)(2,1)S(1)}, u32[]{:S(2)}, u32[]{:S(2)}) async-start(bf16[4,128,2048]{2,1,0:T(8,128)(2,1)} %maximum_select_fusion.1), calls=%async_computation.1 | async-start | bytes 4194304 | tf_op jit(solution)/shard_map/all_to_all | solution.py:560
  149.8 377.1 %all-gather.11.cloned.1.call-start = ((), (), s32[]{:S(2)}) async-start(), calls=%async_computation.13 | async-start | bytes 9437184 | tf_op jit(solution)/shard_map/all_gather | solution.py:633
  286.2 362.6 %reduce-scatter.7.cloned.1.call-start = ((), (), s32[]{:S(2)}) async-start(), calls=%async_computation.14 | async-start | bytes 2621440 | tf_op jit(solution)/shard_map/reduce_scatter | solution.py:706
  380.5 83.5 %collective-permute-start.13 = (bf16[4,2,128,1024]{3,2,1,0:T(8,128)(2,1)}, bf16[4,2,128,1024]{3,2,1,0:T(8,128)(2,1)}, u32[]{:S(2)}, u32[]{:S(2)}) collective-permute-start(bf16[4,2,128,1024]{3,2,1,0:T(8,128)(2,1)} %weight_sums.12.refs_0_), channel_id=1, source_target_pairs={{0,16},{16,0},{1,17},{17,1},{2,18},{18,2},{3,19},{19,3},{4,20},{20... | collective-permute-start | bytes 6291464 | tf_op jit(solution)/shard_map/ppermute | solution.py:544
  478.5 48.4 %collective-permute-start.16 = (bf16[4,2,128,1024]{3,2,1,0:T(8,128)(2,1)}, bf16[4,2,128,1024]{3,2,1,0:T(8,128)(2,1)}, u32[]{:S(2)}, u32[]{:S(2)}) collective-permute-start(bf16[4,2,128,1024]{3,2,1,0:T(8,128)(2,1)} %weight_sums.13.refs_0_), channel_id=1, source_target_pairs={{0,16},{16,0},{1,17},{17,1},{2,18},{18,2},{3,19},{19,3},{4,20},{20... | collective-permute-start | bytes 6291464 | tf_op jit(solution)/shard_map/ppermute | solution.py:544
  497.6 274.5 %reduce-scatter.9.cloned.1.call-start = ((), (), s32[]{:S(2)}) async-start(), calls=%async_computation.15 | async-start | bytes 2621440 | tf_op jit(solution)/shard_map/reduce_scatter | solution.py:706
  540.3 56.5 %collective-permute-start.19 = (bf16[4,2,128,1024]{3,2,1,0:T(8,128)(2,1)}, bf16[4,2,128,1024]{3,2,1,0:T(8,128)(2,1)}, u32[]{:S(2)}, u32[]{:S(2)}) collective-permute-start(bf16[4,2,128,1024]{3,2,1,0:T(8,128)(2,1)} %weight_sums.14.refs_0_), channel_id=1, source_target_pairs={{0,16},{16,0},{1,17},{17,1},{2,18},{18,2},{3,19},{19,3},{4,20},{20... | collective-permute-start | bytes 6291464 | tf_op jit(solution)/shard_map/ppermute | solution.py:544
  541.0 92.6 %collective-permute-start.20 = (bf16[4,2,128,1024]{3,2,1,0:T(8,128)(2,1)}, bf16[4,2,128,1024]{3,2,1,0:T(8,128)(2,1)}, u32[]{:S(2)}, u32[]{:S(2)}) collective-permute-start(bf16[4,2,128,1024]{3,2,1,0:T(8,128)(2,1)} %weight_sums.15.refs_0_), channel_id=1, source_target_pairs={{0,16},{16,0},{1,17},{17,1},{2,18},{18,2},{3,19},{19,3},{4,20},{20... | collective-permute-start | bytes 6291464 | tf_op jit(solution)/shard_map/ppermute | solution.py:544
  542.3 62.2 %collective-permute-start.15 = (bf16[512,2048]{1,0:T(8,128)(2,1)}, bf16[512,2048]{1,0:T(8,128)(2,1)}, u32[]{:S(2)}, u32[]{:S(2)}) collective-permute-start(bf16[512,2048]{1,0:T(8,128)(2,1)} %get-tuple-element.31), channel_id=1, source_target_pairs={{0,1},{1,0},{2,3},{3,2},{4,5},{5,4},{6,7},{7,6},{8,9},{9,8},{10,11... | collective-permute-start | bytes 6291464 | tf_op jit(solution)/shard_map/ppermute | solution.py:550
  553.9 290.2 %reduce-scatter.13.cloned.1.call-start = ((), (), s32[]{:S(2)}) async-start(), calls=%async_computation.17 | async-start | bytes 2621440 | tf_op jit(solution)/shard_map/reduce_scatter | solution.py:706
  569.6 73.1 %collective-permute-start.18 = (bf16[512,2048]{1,0:T(8,128)(2,1)S(1)}, bf16[512,2048]{1,0:T(8,128)(2,1)}, u32[]{:S(2)}, u32[]{:S(2)}) collective-permute-start(bf16[512,2048]{1,0:T(8,128)(2,1)S(1)} %get-tuple-element.33), channel_id=1, source_target_pairs={{0,1},{1,0},{2,3},{3,2},{4,5},{5,4},{6,7},{7,6},{8,9},{9,8},{10,11... | collective-permute-start | bytes 6291464 | tf_op jit(solution)/shard_map/ppermute | solution.py:550
  661.4 53.4 %collective-permute-start.22 = (bf16[1024,2048]{1,0:T(8,128)(2,1)}, bf16[1024,2048]{1,0:T(8,128)(2,1)}, u32[]{:S(2)}, u32[]{:S(2)}) collective-permute-start(bf16[1024,2048]{1,0:T(8,128)(2,1)} %feature_sums.10.refs_0_), channel_id=1, source_target_pairs={{0,8},{8,0},{1,9},{9,1},{2,10},{10,2},{3,11},{11,3},{4,12},{12,4},... | collective-permute-start | bytes 12582920 | tf_op jit(solution)/shard_map/ppermute | solution.py:541
  661.4 85.3 %all-to-all-start.2 = ((bf16[4,128,2048]{2,1,0:T(8,128)(2,1)}), bf16[4,128,2048]{2,1,0:T(8,128)(2,1)}, u32[]{:S(2)}, u32[]{:S(2)}) async-start(bf16[4,128,2048]{2,1,0:T(8,128)(2,1)} %bitcast.182), calls=%async_computation.2 | async-start | bytes 4194304 | tf_op jit(solution)/shard_map/all_to_all | solution.py:560
  665.9 256.2 %reduce-scatter.17.cloned.1.call-start = ((), (), s32[]{:S(2)}) async-start(), calls=%async_computation.19 | async-start | bytes 2621440 | tf_op jit(solution)/shard_map/reduce_scatter | solution.py:706
  666.0 48.8 %collective-permute-start.21 = (bf16[4,2,128,1024]{3,2,1,0:T(8,128)(2,1)}, bf16[4,2,128,1024]{3,2,1,0:T(8,128)(2,1)}, u32[]{:S(2)}, u32[]{:S(2)}) collective-permute-start(bf16[4,2,128,1024]{3,2,1,0:T(8,128)(2,1)} %copy-done.29), channel_id=1, source_target_pairs={{0,16},{16,0},{1,17},{17,1},{2,18},{18,2},{3,19},{19,3},{4,20},{20... | collective-permute-start | bytes 6291464 | tf_op jit(solution)/shard_map/ppermute | solution.py:544
  677.7 274.9 %reduce-scatter.11.cloned.1.call-start = ((), (), s32[]{:S(2)}) async-start(), calls=%async_computation.16 | async-start | bytes 2621440 | tf_op jit(solution)/shard_map/reduce_scatter | solution.py:706
  677.8 94.3 %collective-permute-start.34 = (bf16[4,2,128,1024]{3,2,1,0:T(8,128)(2,1)}, bf16[4,2,128,1024]{3,2,1,0:T(8,128)(2,1)}, u32[]{:S(2)}, u32[]{:S(2)}) collective-permute-start(bf16[4,2,128,1024]{3,2,1,0:T(8,128)(2,1)} %copy-done.19), channel_id=1, source_target_pairs={{0,16},{16,0},{1,17},{17,1},{2,18},{18,2},{3,19},{19,3},{4,20},{20... | collective-permute-start | bytes 6291464 | tf_op jit(solution)/shard_map/ppermute | solution.py:544
  829.8 68.3 %all-to-all-start.3 = ((bf16[4,128,2048]{2,1,0:T(8,128)(2,1)}), bf16[4,128,2048]{2,1,0:T(8,128)(2,1)}, u32[]{:S(2)}, u32[]{:S(2)}) async-start(bf16[4,128,2048]{2,1,0:T(8,128)(2,1)} %bitcast.185), calls=%async_computation.4 | async-start | bytes 4194304 | tf_op jit(solution)/shard_map/all_to_all | solution.py:560
  834.3 119.7 %reduce-scatter.15.cloned.1.call-start = ((), (), s32[]{:S(2)}) async-start(), calls=%async_computation.18 | async-start | bytes 2621440 | tf_op jit(solution)/shard_map/reduce_scatter | solution.py:706
  898.1 48.6 %collective-permute-start.26 = (bf16[4,128,2048]{2,1,0:T(8,128)(2,1)}, bf16[4,128,2048]{2,1,0:T(8,128)(2,1)S(1)}, u32[]{:S(2)}, u32[]{:S(2)}) collective-permute-start(bf16[4,128,2048]{2,1,0:T(8,128)(2,1)} %all-to-all-done.3), channel_id=1, source_target_pairs={{0,1},{1,0},{2,3},{3,2},{4,5},{5,4},{6,7},{7,6},{8,9},{9,8},{10,11... | collective-permute-start | bytes 6291464 | tf_op jit(solution)/shard_map/ppermute | solution.py:550
  (84 other events, 958.0 us)
Sparse Core Ops, SparseCore 0:
  15.3 106.3 all-gather.4
  130.0 106.8 all-gather.6
  239.6 123.8 all-gather.8
  365.4 137.2 all-gather.10
  504.9 42.0 reduce-scatter.6
  554.0 40.1 reduce-scatter.8
  661.5 71.3 reduce-scatter.12
  735.3 53.7 reduce-scatter.16
  791.4 43.1 reduce-scatter.10
  896.3 46.7 reduce-scatter.14

commit v4 on v3

--- a/solution.py
+++ b/solution.py
@@ -422,6 +422,38 @@
     return out if split else out[0]
 
 
+def place_two(flags, mine, mine_y, n_seq, n_slot):
+    model = mine.shape[1]
+    part = n_slot // 4
+
+    def body(flag_ref, mine_ref, other_ref, out_ref):
+        own = pl.program_id(2) == flag_ref[1]
+
+        @pl.when(own)
+        def _():
+            out_ref[...] = mine_ref[...]
+
+        @pl.when(jnp.logical_not(own))
+        def _():
+            out_ref[...] = other_ref[...]
+
+    piece = pl.BlockSpec((part, model), lambda i, cc, yy, f: ((cc ^ f[0]) * n_seq + i, 0))
+    out = call(
+        body,
+        "place_two",
+        (n_seq, 2, 2),
+        flags,
+        [piece, piece],
+        [mine, mine_y],
+        pl.BlockSpec((part, model), lambda i, cc, yy, f: (4 * i + 2 * cc + yy, 0)),
+        jax.ShapeDtypeStruct((n_seq * n_slot, model), low),
+        0,
+        8 * n_seq * n_slot * model,
+        [],
+    )
+    return out.reshape(n_seq, n_slot, model)
+
+
 def place_rows(flags, mine, mine_y, came, n_seq, n_slot, base):
     model = mine.shape[1]
     part = n_slot // 4
@@ -576,6 +608,19 @@
     def other_mp(got, wait=0):
         return to_y(got + jnp.asarray(wait, got.dtype)) if n_mp == 2 else got
 
+    def with_core(got):
+        mine = lax.dynamic_slice_in_dim(got, n_seq * c, n_seq, 0)
+        other = to_core(lax.dynamic_slice_in_dim(got, n_seq * (1 - c), n_seq, 0))
+        return jnp.concatenate([mine, other], axis=0)
+
+    def placed_rows(homes, homes_y):
+        if n_mp == 2:
+            flat = [v.reshape(rows_own, model) for v in (homes, homes_y)]
+            return place_two(flag_cy, *flat, n_seq, n_slot)
+        homes = lax.all_gather(homes.reshape(2, n_seq, part, model), "mp", axis=2, tiled=True)
+        homes = jnp.where(c == 0, homes, homes[::-1])
+        return jnp.swapaxes(homes, 0, 1).reshape(n_seq, n_slot, model)
+
     def placed_home(got, got_y, base=None):
         def of_core(at):
             return [lax.dynamic_slice_in_dim(v, n_seq * at, n_seq, 0) for v in (got, got_y)]
@@ -754,23 +799,26 @@
     grad_pre = rows_step(grad_rows, [(fc2_w, n) for n in both], mlp_cols, "times", (slope, 0))
     fc1_out = [[(ln_out, grad_pre, n, mlp_cols)] for n in both]
     far_1a = far_sums(fc1_out[0], far_2a[1])
+    grad_2 = [near_sums(far_2a, grad_heads[0])]
     ln_two = feature_sums(
         [(grad_pre, 0, hid)] + [(h[1], 0, qkv_cols) for h in heads],
         [fc1_w, *heads_w],
         [0] * (1 + head_chunks),
         *([] if attn_came is None else [attn_came]),
-    )
-    far_1b = far_sums(fc1_out[1], far_2b[1])
+        far_2b[1],
+    )
     attn_out = joined(attn_mine, attn_came) + out_bias
     mlp_out = joined(mlp_mine, mlp_came) + fc2_bias
     block_rows = (rows_in + attn_out + mlp_out).astype(low)
+    far_1b = far_sums(fc1_out[1], block_rows)
     block_got = send_home(block_rows)
-    grad_2 = [near_sums(far_2a, grad_heads[0], block_rows)]
-    grad_2.append(near_sums(far_2b))
-    ln_mine, ln_came = ln_two(far_1a[1], block_got)
+    grad_2.append(near_sums(far_2b, far_1a[1]))
+    ln_mine, ln_came = ln_two(block_got)
     grad_1 = [near_sums(far_1a, grad_heads[-1], far_1b[1])]
-    block_y = other_mp(block_got, 0 if ln_came is None else never(ln_came))
-    grad_1.append(near_sums(far_1b, grad_2[0], block_y))
+    block_homes = with_core(block_got)
+    block_y = other_mp(block_homes, 0 if ln_came is None else never(ln_came))
+    block_out = placed_rows(block_homes, block_y)
+    grad_1.append(near_sums(far_1b, grad_2[0], block_out))
 
     grad_ln = ln_mine if ln_came is None else ln_mine + ln_came.astype(wide)
     scaled = grad_ln * gain
@@ -781,7 +829,6 @@
     )
     back = back.astype(low)
     grad_got = send_home(back)
-    block_out = placed_home(block_got, block_y)
     grad_tokens = placed_home(grad_got, other_mp(grad_got), grad_out)
     gain_sum = jnp.sum(grad_ln * normed, axis=0)
     shift_sum = jnp.sum(grad_ln, axis=0)

time: 999 us -> 975 us (0.976)
  waiting for transfers between devices: 378 us -> 357 us
    all_to_all x4, waiting for transfers between devices: 145 us -> 115 us  [to_ctx(): return lax.all_to_all(v, 'ctx', 0, 0, tiled=True)]
    ppermute x8, waiting for transfers between devices: 65.2 us -> 94.4 us  [to_x(): return lax.ppermute(v, 'x', [(0, 1), (1, 0)])]
    ppermute x8, waiting for transfers between devices: 143 us -> 123 us  [to_y(): return lax.ppermute(v, 'mp', [(0, 1), (1, 0)])]
    unnamed x121 -> x123, local copies, waits for them, and re-layouts: 39.5 us -> 42.1 us
  transfers between devices with their start and end apart: 51 -> 51, of which waited for: 22 -> 25; matrix products, arithmetic and copies ran while one was open for 10% -> 10% of each run, Pallas kernels for 40% -> 41%
where the time goes in v4:
time: 975 us; the launch traced here: 966 us
  Pallas kernels  402 us (41%)
  waiting for transfers between devices  357 us (37%)
  local copies, waits for them, and re-layouts  79.4 us (8%)
  other arithmetic  55.8 us (6%)
  starting transfers between devices  51.3 us (5%)
  between operations  19.6 us (2%)
    pallas_call x30, Pallas kernels, call(): pl.pallas_call(inner, grid_spec=pltpu.PrefetchScalarGridSpec(num_scalar_p...  317 us
    ppermute x8, waiting for transfers between devices, to_y(): return lax.ppermute(v, 'mp', [(0, 1), (1, 0)])  123 us
    all_to_all x4, waiting for transfers between devices, to_ctx(): return lax.all_to_all(v, 'ctx', 0, 0, tiled=True)  115 us
    ppermute x8, waiting for transfers between devices, to_x(): return lax.ppermute(v, 'x', [(0, 1), (1, 0)])  94.4 us
    pallas_call x2, Pallas kernels, attention(): pl.pallas_call(inner, grid_spec=pltpu.PrefetchScalarGridSpec(num_scalar_p...  84.7 us
    unnamed x123, local copies, waits for them, and re-layouts  42.1 us
  transfers between devices with their start and end apart: 51, of which 25 were waited for; matrix products, arithmetic and copies ran while one was open for 10% of the time, Pallas kernels for 41%

profile of v4, /device:TPU:0, one launch (start us, length us, event | category | flops | bytes accessed | tf_op | source)
XLA Modules:
  0.0 965.5 jit_solution(11954420204226837333)
XLA Ops:
  53.6 71.4 %all-to-all-done = bf16[4,128,2048]{2,1,0:T(8,128)(2,1)S(1)} async-done(((bf16[4,128,2048]{2,1,0:T(8,128)(2,1)}), bf16[4,128,2048]{2,1,0:T(8,128)(2,1)S(1)}, u32[]{:S(2)}, u32[]{:S(2)}) %all-to-all-start) | async-done | bytes 2097184 | tf_op jit(solution)/shard_map/all_to_all | solution.py:592
  149.0 35.5 %collective-permute-done.7.refs_1_ = bf16[512,2048]{1,0:T(8,128)(2,1)} collective-permute-done((bf16[512,2048]{1,0:T(8,128)(2,1)}, bf16[512,2048]{1,0:T(8,128)(2,1)}, u32[]{:S(2)}, u32[]{:S(2)}) %collective-permute-start.7) | collective-permute-done | bytes 2097184 | tf_op jit(solution)/shard_map/ppermute | solution.py:582
  189.8 42.0 %all-to-all-done.1 = bf16[4,128,2048]{2,1,0:T(8,128)(2,1)S(1)} async-done(((bf16[4,128,2048]{2,1,0:T(8,128)(2,1)}), bf16[4,128,2048]{2,1,0:T(8,128)(2,1)S(1)}, u32[]{:S(2)}, u32[]{:S(2)}) %all-to-all-start.1) | async-done | bytes 2097184 | tf_op jit(solution)/shard_map/all_to_all | solution.py:592
  234.0 9.5 stack_rows.5.refs_0_.refs_1_.refs_2_.refs_3_.refs_4_
  246.2 10.5 %rows_bias.2.refs_0_.refs_1_ = f32[2048,768]{1,0:T(8,128)} custom-call(s32[1]{0:T(128)} %bitcast.7.flag_ref, bf16[2048,2048]{1,0:T(8,128)(2,1)} %stack_rows.5.refs_0_.refs_1_.refs_2_.refs_3_.refs_4_, bf16[2048,2048]{1,0:T(8,128)(2,1)} %stack_rows.5.refs_0_.refs_1_.refs_2_.refs_3_.refs_4_, ...), custom_call_target="tpu_custom_call" | custom-call | flops 6442450944 | bytes 17825792 | tf_op jit(solution)/shard_map/rows_bias/pallas_call | solution.py:243
  256.7 22.4 %collective-permute-done.10.refs_2_ = bf16[512,2048]{1,0:T(8,128)(2,1)} collective-permute-done((bf16[512,2048]{1,0:T(8,128)(2,1)S(1)}, bf16[512,2048]{1,0:T(8,128)(2,1)}, u32[]{:S(2)}, u32[]{:S(2)}) %collective-permute-start.10) | collective-permute-done | bytes 2097184 | tf_op jit(solution)/shard_map/ppermute | solution.py:582
  310.6 10.5 %rows_bias.3.refs_0_.refs_1_ = f32[2048,768]{1,0:T(8,128)} custom-call(s32[1]{0:T(128)} %bitcast.7.flag_ref, bf16[2048,256]{1,0:T(8,128)(2,1)S(1)} %rows_plain.2.refs_0_.refs_2_, bf16[2048,2048]{1,0:T(8,128)(2,1)} %stack_rows.5.refs_0_.refs_1_.refs_2_.refs_3_.refs_4_, bf16[2048,2048]{1,0:T(8,128)(2,1)} %stack_rows.5.refs_0_.refs_1_.refs_2_.refs_3_.refs_4_, ...), custom_call_target="tpu_custom_call" | custom-call | flops 6442450944 | bytes 17825792 | tf_op jit(solution)/shard_map/rows_bias/pallas_call | solution.py:243
  326.7 42.5 %attention.2 = (bf16[2048,256]{1,0:T(8,128)(2,1)S(1)}, bf16[2048,768]{1,0:T(8,128)(2,1)}) custom-call(s32[16]{0:T(128)S(1)} %select_reduce_fusion.order_ref, bf16[2048,256]{1,0:T(8,128)(2,1)S(1)} %rows_plain.3.refs_0_.refs_2_, f32[2048,768]{1,0:T(8,128)} %rows_bias.2.refs_0_.refs_1_, bf16[2048,256]{1,0:T(8,128)(2,1)S(1)} %rows_plain.2.refs_0_.refs_2_, ...), custom_call_target="tpu_custom_call" | custom-call | flops 25769803776 | bytes 30000000 | tf_op jit(solution)/shard_map/attention/pallas_call | solution.py:202
  369.3 10.1 %weight_sums.12.refs_0_ = bf16[4,2,128,1024]{3,2,1,0:T(8,128)(2,1)} custom-call(s32[1]{0:T(128)} %bitcast.7.flag_ref, bf16[2048,256]{1,0:T(8,128)(2,1)S(1)} %get-tuple-element.25.refs_0_.refs_4_.refs_1_, bf16[2048,2048]{1,0:T(8,128)(2,1)} %stack_rows.5.refs_0_.refs_1_.refs_2_.refs_3_.refs_4_, bf16[2048,2048]{1,0:T(8,128)(2,1)} %stack_rows.7.refs_1_.refs_2_.refs_3_.refs_4_, ...), custom_call_target="tpu_custom_call" | custom-call | flops 4294967296 | bytes 14680064 | tf_op jit(solution)/shard_map/weight_sums/pallas_call | solution.py:243
  380.8 42.2 %attention.3 = (bf16[2048,256]{1,0:T(8,128)(2,1)S(1)}, bf16[2048,768]{1,0:T(8,128)(2,1)}) custom-call(s32[16]{0:T(128)S(1)} %select_reduce_fusion.order_ref, bf16[4,2,128,1024]{3,2,1,0:T(8,128)(2,1)} %weight_sums.12.refs_0_, f32[2048,768]{1,0:T(8,128)} %rows_bias.3.refs_0_.refs_1_, bf16[2048,256]{1,0:T(8,128)(2,1)S(1)} %rows_plain.3.refs_0_.refs_2_, ...), custom_call_target="tpu_custom_call" | custom-call | flops 25769803776 | bytes 30000000 | tf_op jit(solution)/shard_map/attention/pallas_call | solution.py:202
  432.0 30.9 %rows_gelu.1 = (bf16[2048,2048]{1,0:T(8,128)(2,1)}, bf16[2048,2048]{1,0:T(8,128)(2,1)}) custom-call(s32[1]{0:T(128)} %bitcast.7.flag_ref, bf16[4,2,128,1024]{3,2,1,0:T(8,128)(2,1)} %weight_sums.13.refs_0_, bf16[2048,2048]{1,0:T(8,128)(2,1)} %stack_rows.5.refs_0_.refs_1_.refs_2_.refs_3_.refs_4_, ...), custom_call_target="tpu_custom_call" | custom-call | flops 17179869184 | bytes 33554432 | tf_op jit(solution)/shard_map/rows_gelu/pallas_call | solution.py:243
  485.4 9.2 weight_sums.16.refs_0_
  504.9 20.4 %collective-permute-done.16.refs_1_.refs_5_ = bf16[4,2,128,1024]{3,2,1,0:T(8,128)(2,1)} collective-permute-done((bf16[4,2,128,1024]{3,2,1,0:T(8,128)(2,1)}, bf16[4,2,128,1024]{3,2,1,0:T(8,128)(2,1)}, u32[]{:S(2)}, u32[]{:S(2)}) %collective-permute-start.16) | collective-permute-done | bytes 2097184 | tf_op jit(solution)/shard_map/ppermute | solution.py:576
  525.3 13.5 %feature_sums.8.refs_0_ = bf16[1024,2048]{1,0:T(8,128)(2,1)} custom-call(s32[1]{0:T(128)} %bitcast.7.flag_ref, f32[512,2048]{1,0:T(8,128)} %get-tuple-element.30.refs_0_, bf16[4,2,128,1024]{3,2,1,0:T(8,128)(2,1)} %collective-permute-done.16.refs_1_.refs_5_, bf16[2048,2048]{1,0:T(8,128)(2,1)} %get-tuple-element.29.refs_0_.refs_3_.refs_2_.refs_1_, ...), custom_call_target="tpu_custom_call" | custom-call | flops 8589934592 | bytes 20971520 | tf_op jit(solution)/shard_map/feature_sums/pallas_call | solution.py:243
  554.2 14.1 %feature_sums.9 = (f32[512,2048]{1,0:T(8,128)}, bf16[512,2048]{1,0:T(8,128)(2,1)}) custom-call(s32[1]{0:T(128)} %bitcast.7.flag_ref, bf16[4,2,128,1024]{3,2,1,0:T(8,128)(2,1)S(1)} %copy-done.24, bf16[2048,2048]{1,0:T(8,128)(2,1)} %get-tuple-element.29.refs_0_.refs_3_.refs_2_.refs_1_, bf16[2048,2048]{1,0:T(8,128)(2,1)} %bitcast.181, ...), custom_call_target="tpu_custom_call" | custom-call | flops 8589934592 | bytes 20971520 | tf_op jit(solution)/shard_map/feature_sums/pallas_call | solution.py:243
  571.0 24.5 %rows_times.1.refs_0_.refs_3_.refs_2_.refs_4_ = bf16[2048,2048]{1,0:T(8,128)(2,1)} custom-call(s32[1]{0:T(128)} %bitcast.7.flag_ref, f32[512,2048]{1,0:T(8,128)S(1)} %copy-done.12, bf16[2048,2048]{1,0:T(8,128)(2,1)} %stack_rows.7.refs_1_.refs_2_.refs_3_.refs_4_, bf16[2048,2048]{1,0:T(8,128)(2,1)} %stack_rows.7.refs_1_.refs_2_.refs_3_.refs_4_, ...), custom_call_target="tpu_custom_call" | custom-call | flops 17179869184 | bytes 33554432 | tf_op jit(solution)/shard_map/rows_times/pallas_call | solution.py:243
  617.7 24.3 %collective-permute-done.21.refs_2_.refs_4_ = bf16[4,2,128,1024]{3,2,1,0:T(8,128)(2,1)} collective-permute-done((bf16[4,2,128,1024]{3,2,1,0:T(8,128)(2,1)}, bf16[4,2,128,1024]{3,2,1,0:T(8,128)(2,1)}, u32[]{:S(2)}, u32[]{:S(2)}) %collective-permute-start.21) | collective-permute-done | bytes 2097184 | tf_op jit(solution)/shard_map/ppermute | solution.py:576
  643.7 21.7 %feature_sums.10.refs_0_ = bf16[1024,2048]{1,0:T(8,128)(2,1)} custom-call(s32[1]{0:T(128)} %bitcast.7.flag_ref, bf16[4,2,128,1024]{3,2,1,0:T(8,128)(2,1)S(1)} %copy-done.16, bf16[512,2048]{1,0:T(8,128)(2,1)} %collective-permute-done.15.refs_1_, bf16[4,2,128,1024]{3,2,1,0:T(8,128)(2,1)} %collective-permute-done.21.refs_2_.refs_4_, ...), custom_call_target="tpu_custom_call" | custom-call | flops 15032385536 | bytes 30408704 | tf_op jit(solution)/shard_map/feature_sums/pallas_call | solution.py:243
  686.2 27.5 %collective-permute-done.22.refs_1_.refs_5_ = bf16[4,2,128,1024]{3,2,1,0:T(8,128)(2,1)} collective-permute-done((bf16[4,2,128,1024]{3,2,1,0:T(8,128)(2,1)}, bf16[4,2,128,1024]{3,2,1,0:T(8,128)(2,1)}, u32[]{:S(2)}, u32[]{:S(2)}) %collective-permute-start.22) | collective-permute-done | bytes 2097184 | tf_op jit(solution)/shard_map/ppermute | solution.py:576
  727.5 22.0 %feature_sums.11 = (f32[512,2048]{1,0:T(8,128)}, bf16[512,2048]{1,0:T(8,128)(2,1)}) custom-call(s32[1]{0:T(128)} %bitcast.7.flag_ref, bf16[4,2,128,1024]{3,2,1,0:T(8,128)(2,1)S(1)} %copy-done.22, bf16[4,128,2048]{2,1,0:T(8,128)(2,1)} %all-to-all-done.2.refs_1_, bf16[2048,2048]{1,0:T(8,128)(2,1)} %rows_times.1.refs_0_.refs_3_.refs_2_.refs_4_, ...), custom_call_target="tpu_custom_call" | custom-call | flops 15032385536 | bytes 30408704 | tf_op jit(solution)/shard_map/feature_sums/pallas_call | solution.py:243
  753.7 17.1 %collective-permute-done.34.refs_2_.refs_5_ = bf16[4,2,128,1024]{3,2,1,0:T(8,128)(2,1)} collective-permute-done((bf16[4,2,128,1024]{3,2,1,0:T(8,128)(2,1)}, bf16[4,2,128,1024]{3,2,1,0:T(8,128)(2,1)}, u32[]{:S(2)}, u32[]{:S(2)}) %collective-permute-start.34) | collective-permute-done | bytes 2097184 | tf_op jit(solution)/shard_map/ppermute | solution.py:576
  781.3 15.3 %collective-permute-done.24 = bf16[512,2048]{1,0:T(8,128)(2,1)} collective-permute-done((bf16[512,2048]{1,0:T(8,128)(2,1)}, bf16[512,2048]{1,0:T(8,128)(2,1)}, u32[]{:S(2)}, u32[]{:S(2)}) %collective-permute-start.24) | collective-permute-done | bytes 2097184 | tf_op jit(solution)/shard_map/ppermute | solution.py:582
  817.6 44.5 %collective-permute-done.25 = bf16[4,128,2048]{2,1,0:T(8,128)(2,1)} collective-permute-done((bf16[4,128,2048]{2,1,0:T(8,128)(2,1)}, bf16[4,128,2048]{2,1,0:T(8,128)(2,1)}, u32[]{:S(2)}, u32[]{:S(2)}) %collective-permute-start.25) | collective-permute-done | bytes 2097184 | tf_op jit(solution)/shard_map/ppermute | solution.py:582
  947.8 9.9 %place_rows.1 = f32[1024,2048]{1,0:T(8,128)} custom-call(s32[2]{0:T(128)S(1)} %pad_add_fusion.flag_ref, bf16[512,2048]{1,0:T(8,128)(2,1)} %bitcast.61.refs_0_, bf16[512,2048]{1,0:T(8,128)(2,1)S(1)} %bitcast.175, bf16[512,2048]{1,0:T(8,128)(2,1)} %bitcast.63.refs_2_, bf16[1024,2048]{1,0:T(8,128)(2,1)} %bitcast.187), custom_call_target="tpu_custom_call" | custom-call | bytes 25165824 | tf_op jit(solution)/shard_map/place_rows/pallas_call | solution.py:243
  (363 shorter events, 354.4 us)
Async XLA Ops:
  7.2 236.3 %all-gather.5.cloned.1.call-start = ((), (), s32[]{:S(2)}) async-start(), calls=%async_computation.10 | async-start | bytes 4718592 | tf_op jit(solution)/shard_map/all_gather | solution.py:678
  37.3 87.6 %all-to-all-start = ((bf16[4,128,2048]{2,1,0:T(8,128)(2,1)}), bf16[4,128,2048]{2,1,0:T(8,128)(2,1)S(1)}, u32[]{:S(2)}, u32[]{:S(2)}) async-start(bf16[4,128,2048]{2,1,0:T(8,128)(2,1)} %maximum_select_fusion), calls=%async_computation | async-start | bytes 4194304 | tf_op jit(solution)/shard_map/all_to_all | solution.py:592
  42.7 265.7 %all-gather.7.cloned.1.call-start = ((), (), s32[]{:S(2)}) async-start(), calls=%async_computation.11 | async-start | bytes 4718592 | tf_op jit(solution)/shard_map/all_gather | solution.py:678
  128.9 303.0 %all-gather.9.cloned.1.call-start = ((), (), s32[]{:S(2)}) async-start(), calls=%async_computation.12 | async-start | bytes 9437184 | tf_op jit(solution)/shard_map/all_gather | solution.py:678
  145.2 86.6 %all-to-all-start.1 = ((bf16[4,128,2048]{2,1,0:T(8,128)(2,1)}), bf16[4,128,2048]{2,1,0:T(8,128)(2,1)S(1)}, u32[]{:S(2)}, u32[]{:S(2)}) async-start(bf16[4,128,2048]{2,1,0:T(8,128)(2,1)} %maximum_select_fusion.1), calls=%async_computation.1 | async-start | bytes 4194304 | tf_op jit(solution)/shard_map/all_to_all | solution.py:592
  148.8 376.5 %all-gather.11.cloned.1.call-start = ((), (), s32[]{:S(2)}) async-start(), calls=%async_computation.13 | async-start | bytes 9437184 | tf_op jit(solution)/shard_map/all_gather | solution.py:678
  285.2 322.0 %reduce-scatter.7.cloned.1.call-start = ((), (), s32[]{:S(2)}) async-start(), calls=%async_computation.14 | async-start | bytes 2621440 | tf_op jit(solution)/shard_map/reduce_scatter | solution.py:751
  379.4 83.5 %collective-permute-start.13 = (bf16[4,2,128,1024]{3,2,1,0:T(8,128)(2,1)}, bf16[4,2,128,1024]{3,2,1,0:T(8,128)(2,1)}, u32[]{:S(2)}, u32[]{:S(2)}) collective-permute-start(bf16[4,2,128,1024]{3,2,1,0:T(8,128)(2,1)} %weight_sums.12.refs_0_), channel_id=1, source_target_pairs={{0,16},{16,0},{1,17},{17,1},{2,18},{18,2},{3,19},{19,3},{4,20},{20... | collective-permute-start | bytes 6291464 | tf_op jit(solution)/shard_map/ppermute | solution.py:576
  477.0 48.4 %collective-permute-start.16 = (bf16[4,2,128,1024]{3,2,1,0:T(8,128)(2,1)}, bf16[4,2,128,1024]{3,2,1,0:T(8,128)(2,1)}, u32[]{:S(2)}, u32[]{:S(2)}) collective-permute-start(bf16[4,2,128,1024]{3,2,1,0:T(8,128)(2,1)} %weight_sums.13.refs_0_), channel_id=1, source_target_pairs={{0,16},{16,0},{1,17},{17,1},{2,18},{18,2},{3,19},{19,3},{4,20},{20... | collective-permute-start | bytes 6291464 | tf_op jit(solution)/shard_map/ppermute | solution.py:576
  496.0 257.8 %reduce-scatter.9.cloned.1.call-start = ((), (), s32[]{:S(2)}) async-start(), calls=%async_computation.15 | async-start | bytes 2621440 | tf_op jit(solution)/shard_map/reduce_scatter | solution.py:751
  548.6 322.4 %reduce-scatter.13.cloned.1.call-start = ((), (), s32[]{:S(2)}) async-start(), calls=%async_computation.17 | async-start | bytes 2621440 | tf_op jit(solution)/shard_map/reduce_scatter | solution.py:751
  548.7 48.7 %collective-permute-start.20 = (bf16[4,2,128,1024]{3,2,1,0:T(8,128)(2,1)}, bf16[4,2,128,1024]{3,2,1,0:T(8,128)(2,1)S(1)}, u32[]{:S(2)}, u32[]{:S(2)}) collective-permute-start(bf16[4,2,128,1024]{3,2,1,0:T(8,128)(2,1)} %copy-done.19), channel_id=1, source_target_pairs={{0,16},{16,0},{1,17},{17,1},{2,18},{18,2},{3,19},{19,3},{4,20},{20... | collective-permute-start | bytes 6291464 | tf_op jit(solution)/shard_map/ppermute | solution.py:576
  549.4 92.6 %collective-permute-start.21 = (bf16[4,2,128,1024]{3,2,1,0:T(8,128)(2,1)}, bf16[4,2,128,1024]{3,2,1,0:T(8,128)(2,1)}, u32[]{:S(2)}, u32[]{:S(2)}) collective-permute-start(bf16[4,2,128,1024]{3,2,1,0:T(8,128)(2,1)} %copy-done.14), channel_id=1, source_target_pairs={{0,16},{16,0},{1,17},{17,1},{2,18},{18,2},{3,19},{19,3},{4,20},{20... | collective-permute-start | bytes 6291464 | tf_op jit(solution)/shard_map/ppermute | solution.py:576
  550.8 91.2 %collective-permute-start.15 = (bf16[512,2048]{1,0:T(8,128)(2,1)}, bf16[512,2048]{1,0:T(8,128)(2,1)}, u32[]{:S(2)}, u32[]{:S(2)}) collective-permute-start(bf16[512,2048]{1,0:T(8,128)(2,1)} %copy-done.32), channel_id=1, source_target_pairs={{0,1},{1,0},{2,3},{3,2},{4,5},{5,4},{6,7},{7,6},{8,9},{9,8},{10,11... | collective-permute-start | bytes 6291464 | tf_op jit(solution)/shard_map/ppermute | solution.py:582
  568.3 97.8 %collective-permute-start.18 = (bf16[512,2048]{1,0:T(8,128)(2,1)}, bf16[512,2048]{1,0:T(8,128)(2,1)}, u32[]{:S(2)}, u32[]{:S(2)}) collective-permute-start(bf16[512,2048]{1,0:T(8,128)(2,1)} %get-tuple-element.33), channel_id=1, source_target_pairs={{0,1},{1,0},{2,3},{3,2},{4,5},{5,4},{6,7},{7,6},{8,9},{9,8},{10,11... | collective-permute-start | bytes 6291464 | tf_op jit(solution)/shard_map/ppermute | solution.py:582
  665.4 58.5 %collective-permute-start.23 = (bf16[1024,2048]{1,0:T(8,128)(2,1)}, bf16[1024,2048]{1,0:T(8,128)(2,1)}, u32[]{:S(2)}, u32[]{:S(2)}) collective-permute-start(bf16[1024,2048]{1,0:T(8,128)(2,1)} %feature_sums.10.refs_0_), channel_id=1, source_target_pairs={{0,8},{8,0},{1,9},{9,1},{2,10},{10,2},{3,11},{11,3},{4,12},{12,4},... | collective-permute-start | bytes 12582920 | tf_op jit(solution)/shard_map/ppermute | solution.py:573
  665.4 48.4 %collective-permute-start.22 = (bf16[4,2,128,1024]{3,2,1,0:T(8,128)(2,1)}, bf16[4,2,128,1024]{3,2,1,0:T(8,128)(2,1)}, u32[]{:S(2)}, u32[]{:S(2)}) collective-permute-start(bf16[4,2,128,1024]{3,2,1,0:T(8,128)(2,1)} %weight_sums.18.refs_0_), channel_id=1, source_target_pairs={{0,16},{16,0},{1,17},{17,1},{2,18},{18,2},{3,19},{19,3},{4,20},{20... | collective-permute-start | bytes 6291464 | tf_op jit(solution)/shard_map/ppermute | solution.py:576
  672.2 53.4 %all-to-all-start.2 = ((bf16[4,128,2048]{2,1,0:T(8,128)(2,1)}), bf16[4,128,2048]{2,1,0:T(8,128)(2,1)}, u32[]{:S(2)}, u32[]{:S(2)}) async-start(bf16[4,128,2048]{2,1,0:T(8,128)(2,1)} %bitcast.169), calls=%async_computation.2 | async-start | bytes 4194304 | tf_op jit(solution)/shard_map/all_to_all | solution.py:592
  676.7 235.0 %reduce-scatter.17.cloned.1.call-start = ((), (), s32[]{:S(2)}) async-start(), calls=%async_computation.19 | async-start | bytes 2621440 | tf_op jit(solution)/shard_map/reduce_scatter | solution.py:751
  723.1 212.5 %reduce-scatter.11.cloned.1.call-start = ((), (), s32[]{:S(2)}) async-start(), calls=%async_computation.16 | async-start | bytes 2621440 | tf_op jit(solution)/shard_map/reduce_scatter | solution.py:751
  723.2 47.6 %collective-permute-start.34 = (bf16[4,2,128,1024]{3,2,1,0:T(8,128)(2,1)}, bf16[4,2,128,1024]{3,2,1,0:T(8,128)(2,1)}, u32[]{:S(2)}, u32[]{:S(2)}) collective-permute-start(bf16[4,2,128,1024]{3,2,1,0:T(8,128)(2,1)} %copy-done.25), channel_id=1, source_target_pairs={{0,16},{16,0},{1,17},{17,1},{2,18},{18,2},{3,19},{19,3},{4,20},{20... | collective-permute-start | bytes 6291464 | tf_op jit(solution)/shard_map/ppermute | solution.py:576
  753.7 58.6 %collective-permute-start.19 = (bf16[2,128,2048]{2,1,0:T(8,128)(2,1)}, bf16[2,128,2048]{2,1,0:T(8,128)(2,1)}, u32[]{:S(2)}, u32[]{:S(2)}) collective-permute-start(bf16[2,128,2048]{2,1,0:T(8,128)(2,1)} %get-tuple-element.94), channel_id=1, source_target_pairs={{0,8},{8,0},{1,9},{9,1},{2,10},{10,2},{3,11},{11,3},{4,12},{12,4},... | collective-permute-start | bytes 3145736 | tf_op jit(solution)/shard_map/ppermute | solution.py:573
  805.3 78.1 %all-to-all-start.3 = ((bf16[4,128,2048]{2,1,0:T(8,128)(2,1)}), bf16[4,128,2048]{2,1,0:T(8,128)(2,1)}, u32[]{:S(2)}, u32[]{:S(2)}) async-start(bf16[4,128,2048]{2,1,0:T(8,128)(2,1)} %bitcast.188), calls=%async_computation.4 | async-start | bytes 4194304 | tf_op jit(solution)/shard_map/all_to_all | solution.py:592
  809.8 127.2 %reduce-scatter.15.cloned.1.call-start = ((), (), s32[]{:S(2)}) async-start(), calls=%async_computation.18 | async-start | bytes 2621440 | tf_op jit(solution)/shard_map/reduce_scatter | solution.py:751
  (85 other events, 936.8 us)
Sparse Core Ops, SparseCore 0:
  14.4 106.3 all-gather.4
  129.0 106.6 all-gather.6
  238.5 123.8 all-gather.8
  364.4 137.2 all-gather.10
  504.4 42.0 reduce-scatter.6
  549.3 43.1 reduce-scatter.8
  617.8 41.4 reduce-scatter.12
  723.2 41.3 reduce-scatter.16
  781.4 55.4 reduce-scatter.10
  883.2 46.8 reduce-scatter.14

commit v5 on v4

--- a/solution.py
+++ b/solution.py
@@ -793,10 +793,10 @@
     far_2b = far_sums(fc2_out[1])
     grad_heads = [near_sums(far_heads[0])]
     attn_mine, attn_came = attn_two()
+    grad_pre = rows_step(grad_rows, [(fc2_w, n) for n in both], mlp_cols, "times", (slope, 0))
     mlp_two = feature_sums([(act, 0, hid)], [fc2_w], [0], far_heads[-1][1])
     grad_heads += [near_sums(far) for far in far_heads[1:]]
     mlp_mine, mlp_came = mlp_two()
-    grad_pre = rows_step(grad_rows, [(fc2_w, n) for n in both], mlp_cols, "times", (slope, 0))
     fc1_out = [[(ln_out, grad_pre, n, mlp_cols)] for n in both]
     far_1a = far_sums(fc1_out[0], far_2a[1])
     grad_2 = [near_sums(far_2a, grad_heads[0])]

time: 975 us -> 983 us (level)
    unnamed x123 -> x121, local copies, waits for them, and re-layouts: 42.1 us -> 42.3 us
  transfers between devices with their start and end apart: 51 -> 51, of which waited for: 25 -> 24; matrix products, arithmetic and copies ran while one was open for 10% -> 10% of each run, Pallas kernels for 41% -> 40%
where the time goes in v5:
time: 983 us; the launch traced here: 974 us
  Pallas kernels  402 us (41%)
  waiting for transfers between devices  364 us (37%)
  local copies, waits for them, and re-layouts  80.4 us (8%)
  other arithmetic  55.8 us (6%)
  starting transfers between devices  51.7 us (5%)
  between operations  19.3 us (2%)
    pallas_call x30, Pallas kernels, call(): pl.pallas_call(inner, grid_spec=pltpu.PrefetchScalarGridSpec(num_scalar_p...  318 us
    ppermute x8, waiting for transfers between devices, to_y(): return lax.ppermute(v, 'mp', [(0, 1), (1, 0)])  125 us
    all_to_all x4, waiting for transfers between devices, to_ctx(): return lax.all_to_all(v, 'ctx', 0, 0, tiled=True)  115 us
    ppermute x8, waiting for transfers between devices, to_x(): return lax.ppermute(v, 'x', [(0, 1), (1, 0)])  99.9 us
    pallas_call x2, Pallas kernels, attention(): pl.pallas_call(inner, grid_spec=pltpu.PrefetchScalarGridSpec(num_scalar_p...  84.7 us
    unnamed x121, local copies, waits for them, and re-layouts  42.3 us
  transfers between devices with their start and end apart: 51, of which 24 were waited for; matrix products, arithmetic and copies ran while one was open for 10% of the time, Pallas kernels for 40%

profile of v5, /device:TPU:0, one launch (start us, length us, event | category | flops | bytes accessed | tf_op | source)
XLA Modules:
  0.0 973.8 jit_solution(8524753849433900816)
XLA Ops:
  54.5 71.4 %all-to-all-done = bf16[4,128,2048]{2,1,0:T(8,128)(2,1)S(1)} async-done(((bf16[4,128,2048]{2,1,0:T(8,128)(2,1)}), bf16[4,128,2048]{2,1,0:T(8,128)(2,1)S(1)}, u32[]{:S(2)}, u32[]{:S(2)}) %all-to-all-start) | async-done | bytes 2097184 | tf_op jit(solution)/shard_map/all_to_all | solution.py:592
  149.9 35.5 %collective-permute-done.7.refs_1_ = bf16[512,2048]{1,0:T(8,128)(2,1)} collective-permute-done((bf16[512,2048]{1,0:T(8,128)(2,1)}, bf16[512,2048]{1,0:T(8,128)(2,1)}, u32[]{:S(2)}, u32[]{:S(2)}) %collective-permute-start.7) | collective-permute-done | bytes 2097184 | tf_op jit(solution)/shard_map/ppermute | solution.py:582
  190.7 42.0 %all-to-all-done.1 = bf16[4,128,2048]{2,1,0:T(8,128)(2,1)S(1)} async-done(((bf16[4,128,2048]{2,1,0:T(8,128)(2,1)}), bf16[4,128,2048]{2,1,0:T(8,128)(2,1)S(1)}, u32[]{:S(2)}, u32[]{:S(2)}) %all-to-all-start.1) | async-done | bytes 2097184 | tf_op jit(solution)/shard_map/all_to_all | solution.py:592
  234.9 9.5 stack_rows.5.refs_0_.refs_1_.refs_2_.refs_3_.refs_4_
  247.1 10.5 %rows_bias.2.refs_0_.refs_1_ = f32[2048,768]{1,0:T(8,128)} custom-call(s32[1]{0:T(128)} %bitcast.7.flag_ref, bf16[2048,2048]{1,0:T(8,128)(2,1)} %stack_rows.5.refs_0_.refs_1_.refs_2_.refs_3_.refs_4_, bf16[2048,2048]{1,0:T(8,128)(2,1)} %stack_rows.5.refs_0_.refs_1_.refs_2_.refs_3_.refs_4_, ...), custom_call_target="tpu_custom_call" | custom-call | flops 6442450944 | bytes 17825792 | tf_op jit(solution)/shard_map/rows_bias/pallas_call | solution.py:243
  257.6 22.4 %collective-permute-done.10.refs_2_ = bf16[512,2048]{1,0:T(8,128)(2,1)} collective-permute-done((bf16[512,2048]{1,0:T(8,128)(2,1)S(1)}, bf16[512,2048]{1,0:T(8,128)(2,1)}, u32[]{:S(2)}, u32[]{:S(2)}) %collective-permute-start.10) | collective-permute-done | bytes 2097184 | tf_op jit(solution)/shard_map/ppermute | solution.py:582
  311.5 10.5 %rows_bias.3.refs_0_.refs_1_ = f32[2048,768]{1,0:T(8,128)} custom-call(s32[1]{0:T(128)} %bitcast.7.flag_ref, bf16[2048,256]{1,0:T(8,128)(2,1)S(1)} %rows_plain.2.refs_0_.refs_2_, bf16[2048,2048]{1,0:T(8,128)(2,1)} %stack_rows.5.refs_0_.refs_1_.refs_2_.refs_3_.refs_4_, bf16[2048,2048]{1,0:T(8,128)(2,1)} %stack_rows.5.refs_0_.refs_1_.refs_2_.refs_3_.refs_4_, ...), custom_call_target="tpu_custom_call" | custom-call | flops 6442450944 | bytes 17825792 | tf_op jit(solution)/shard_map/rows_bias/pallas_call | solution.py:243
  327.6 42.6 %attention.2 = (bf16[2048,256]{1,0:T(8,128)(2,1)S(1)}, bf16[2048,768]{1,0:T(8,128)(2,1)}) custom-call(s32[16]{0:T(128)S(1)} %select_reduce_fusion.order_ref, bf16[2048,256]{1,0:T(8,128)(2,1)S(1)} %rows_plain.3.refs_0_.refs_2_, f32[2048,768]{1,0:T(8,128)} %rows_bias.2.refs_0_.refs_1_, bf16[2048,256]{1,0:T(8,128)(2,1)S(1)} %rows_plain.2.refs_0_.refs_2_, ...), custom_call_target="tpu_custom_call" | custom-call | flops 25769803776 | bytes 30000000 | tf_op jit(solution)/shard_map/attention/pallas_call | solution.py:202
  370.2 10.1 %weight_sums.12.refs_0_ = bf16[4,2,128,1024]{3,2,1,0:T(8,128)(2,1)} custom-call(s32[1]{0:T(128)} %bitcast.7.flag_ref, bf16[2048,256]{1,0:T(8,128)(2,1)S(1)} %get-tuple-element.25.refs_0_.refs_4_.refs_1_, bf16[2048,2048]{1,0:T(8,128)(2,1)} %stack_rows.5.refs_0_.refs_1_.refs_2_.refs_3_.refs_4_, bf16[2048,2048]{1,0:T(8,128)(2,1)} %stack_rows.7.refs_1_.refs_2_.refs_3_.refs_4_, ...), custom_call_target="tpu_custom_call" | custom-call | flops 4294967296 | bytes 14680064 | tf_op jit(solution)/shard_map/weight_sums/pallas_call | solution.py:243
  381.6 42.2 %attention.3 = (bf16[2048,256]{1,0:T(8,128)(2,1)S(1)}, bf16[2048,768]{1,0:T(8,128)(2,1)}) custom-call(s32[16]{0:T(128)S(1)} %select_reduce_fusion.order_ref, bf16[4,2,128,1024]{3,2,1,0:T(8,128)(2,1)} %weight_sums.12.refs_0_, f32[2048,768]{1,0:T(8,128)} %rows_bias.3.refs_0_.refs_1_, bf16[2048,256]{1,0:T(8,128)(2,1)S(1)} %rows_plain.3.refs_0_.refs_2_, ...), custom_call_target="tpu_custom_call" | custom-call | flops 25769803776 | bytes 30000000 | tf_op jit(solution)/shard_map/attention/pallas_call | solution.py:202
  432.8 30.9 %rows_gelu.1 = (bf16[2048,2048]{1,0:T(8,128)(2,1)}, bf16[2048,2048]{1,0:T(8,128)(2,1)}) custom-call(s32[1]{0:T(128)} %bitcast.7.flag_ref, bf16[4,2,128,1024]{3,2,1,0:T(8,128)(2,1)} %weight_sums.13.refs_0_, bf16[2048,2048]{1,0:T(8,128)(2,1)} %stack_rows.5.refs_0_.refs_1_.refs_2_.refs_3_.refs_4_, ...), custom_call_target="tpu_custom_call" | custom-call | flops 17179869184 | bytes 33554432 | tf_op jit(solution)/shard_map/rows_gelu/pallas_call | solution.py:243
  486.2 9.2 weight_sums.16.refs_0_
  507.9 24.9 %rows_times.1.refs_0_.refs_3_.refs_2_.refs_4_ = bf16[2048,2048]{1,0:T(8,128)(2,1)} custom-call(s32[1]{0:T(128)} %bitcast.7.flag_ref, f32[512,2048]{1,0:T(8,128)S(1)} %copy-done.12, bf16[2048,2048]{1,0:T(8,128)(2,1)} %stack_rows.7.refs_1_.refs_2_.refs_3_.refs_4_, bf16[2048,2048]{1,0:T(8,128)(2,1)} %stack_rows.7.refs_1_.refs_2_.refs_3_.refs_4_, ...), custom_call_target="tpu_custom_call" | custom-call | flops 17179869184 | bytes 33554432 | tf_op jit(solution)/shard_map/rows_times/pallas_call | solution.py:243
  532.8 13.5 %feature_sums.8.refs_0_ = bf16[1024,2048]{1,0:T(8,128)(2,1)} custom-call(s32[1]{0:T(128)} %bitcast.7.flag_ref, bf16[2048,2048]{1,0:T(8,128)(2,1)} %rows_times.1.refs_0_.refs_3_.refs_2_.refs_4_, bf16[4,2,128,1024]{3,2,1,0:T(8,128)(2,1)} %collective-permute-done.16.refs_1_.refs_5_, bf16[2048,2048]{1,0:T(8,128)(2,1)} %get-tuple-element.29.refs_0_.refs_3_.refs_2_.refs_1_, ...), custom_call_target="tpu_custom_call" | custom-call | flops 8589934592 | bytes 20971520 | tf_op jit(solution)/shard_map/feature_sums/pallas_call | solution.py:243
  561.9 14.0 %feature_sums.9 = (f32[512,2048]{1,0:T(8,128)}, bf16[512,2048]{1,0:T(8,128)(2,1)}) custom-call(s32[1]{0:T(128)} %bitcast.7.flag_ref, bf16[4,2,128,1024]{3,2,1,0:T(8,128)(2,1)S(1)} %copy-done.24, bf16[2048,2048]{1,0:T(8,128)(2,1)} %get-tuple-element.29.refs_0_.refs_3_.refs_2_.refs_1_, bf16[2048,2048]{1,0:T(8,128)(2,1)} %bitcast.183, ...), custom_call_target="tpu_custom_call" | custom-call | flops 8589934592 | bytes 20971520 | tf_op jit(solution)/shard_map/feature_sums/pallas_call | solution.py:243
  576.2 28.9 %collective-permute-done.20.refs_1_.refs_4_ = bf16[4,2,128,1024]{3,2,1,0:T(8,128)(2,1)S(1)} collective-permute-done((bf16[4,2,128,1024]{3,2,1,0:T(8,128)(2,1)}, bf16[4,2,128,1024]{3,2,1,0:T(8,128)(2,1)S(1)}, u32[]{:S(2)}, u32[]{:S(2)}) %collective-permute-start.20) | collective-permute-done | bytes 2097184 | tf_op jit(solution)/shard_map/ppermute | solution.py:576
  625.4 24.1 %collective-permute-done.21.refs_2_.refs_4_ = bf16[4,2,128,1024]{3,2,1,0:T(8,128)(2,1)} collective-permute-done((bf16[4,2,128,1024]{3,2,1,0:T(8,128)(2,1)}, bf16[4,2,128,1024]{3,2,1,0:T(8,128)(2,1)}, u32[]{:S(2)}, u32[]{:S(2)}) %collective-permute-start.21) | collective-permute-done | bytes 2097184 | tf_op jit(solution)/shard_map/ppermute | solution.py:576
  651.1 21.8 %feature_sums.10.refs_0_ = bf16[1024,2048]{1,0:T(8,128)(2,1)} custom-call(s32[1]{0:T(128)} %bitcast.7.flag_ref, bf16[4,2,128,1024]{3,2,1,0:T(8,128)(2,1)S(1)} %copy-done.16, bf16[512,2048]{1,0:T(8,128)(2,1)} %collective-permute-done.15.refs_1_, bf16[4,2,128,1024]{3,2,1,0:T(8,128)(2,1)} %collective-permute-done.21.refs_2_.refs_4_, ...), custom_call_target="tpu_custom_call" | custom-call | flops 15032385536 | bytes 30408704 | tf_op jit(solution)/shard_map/feature_sums/pallas_call | solution.py:243
  694.6 26.6 %collective-permute-done.22.refs_1_.refs_5_ = bf16[4,2,128,1024]{3,2,1,0:T(8,128)(2,1)} collective-permute-done((bf16[4,2,128,1024]{3,2,1,0:T(8,128)(2,1)}, bf16[4,2,128,1024]{3,2,1,0:T(8,128)(2,1)}, u32[]{:S(2)}, u32[]{:S(2)}) %collective-permute-start.22) | collective-permute-done | bytes 2097184 | tf_op jit(solution)/shard_map/ppermute | solution.py:576
  735.5 22.0 %feature_sums.11 = (f32[512,2048]{1,0:T(8,128)}, bf16[512,2048]{1,0:T(8,128)(2,1)}) custom-call(s32[1]{0:T(128)} %bitcast.7.flag_ref, bf16[4,2,128,1024]{3,2,1,0:T(8,128)(2,1)S(1)} %copy-done.22, bf16[4,128,2048]{2,1,0:T(8,128)(2,1)} %all-to-all-done.2.refs_1_, bf16[2048,2048]{1,0:T(8,128)(2,1)} %rows_times.1.refs_0_.refs_3_.refs_2_.refs_4_, ...), custom_call_target="tpu_custom_call" | custom-call | flops 15032385536 | bytes 30408704 | tf_op jit(solution)/shard_map/feature_sums/pallas_call | solution.py:243
  762.0 16.3 %collective-permute-done.34.refs_2_.refs_5_ = bf16[4,2,128,1024]{3,2,1,0:T(8,128)(2,1)} collective-permute-done((bf16[4,2,128,1024]{3,2,1,0:T(8,128)(2,1)}, bf16[4,2,128,1024]{3,2,1,0:T(8,128)(2,1)}, u32[]{:S(2)}, u32[]{:S(2)}) %collective-permute-start.34) | collective-permute-done | bytes 2097184 | tf_op jit(solution)/shard_map/ppermute | solution.py:576
  788.8 16.0 %collective-permute-done.24 = bf16[512,2048]{1,0:T(8,128)(2,1)} collective-permute-done((bf16[512,2048]{1,0:T(8,128)(2,1)}, bf16[512,2048]{1,0:T(8,128)(2,1)}, u32[]{:S(2)}, u32[]{:S(2)}) %collective-permute-start.24) | collective-permute-done | bytes 2097184 | tf_op jit(solution)/shard_map/ppermute | solution.py:582
  826.0 44.6 %collective-permute-done.25 = bf16[4,128,2048]{2,1,0:T(8,128)(2,1)} collective-permute-done((bf16[4,128,2048]{2,1,0:T(8,128)(2,1)}, bf16[4,128,2048]{2,1,0:T(8,128)(2,1)}, u32[]{:S(2)}, u32[]{:S(2)}) %collective-permute-start.25) | collective-permute-done | bytes 2097184 | tf_op jit(solution)/shard_map/ppermute | solution.py:582
  956.4 9.9 %place_rows.1 = f32[1024,2048]{1,0:T(8,128)} custom-call(s32[2]{0:T(128)S(1)} %pad_add_fusion.flag_ref, bf16[512,2048]{1,0:T(8,128)(2,1)} %bitcast.61.refs_0_, bf16[512,2048]{1,0:T(8,128)(2,1)S(1)} %bitcast.175, bf16[512,2048]{1,0:T(8,128)(2,1)} %bitcast.63.refs_2_, bf16[1024,2048]{1,0:T(8,128)(2,1)} %bitcast.187), custom_call_target="tpu_custom_call" | custom-call | bytes 25165824 | tf_op jit(solution)/shard_map/place_rows/pallas_call | solution.py:243
  (361 shorter events, 355.3 us)
Async XLA Ops:
  7.2 237.2 %all-gather.5.cloned.1.call-start = ((), (), s32[]{:S(2)}) async-start(), calls=%async_computation.10 | async-start | bytes 4718592 | tf_op jit(solution)/shard_map/all_gather | solution.py:678
  38.2 87.6 %all-to-all-start = ((bf16[4,128,2048]{2,1,0:T(8,128)(2,1)}), bf16[4,128,2048]{2,1,0:T(8,128)(2,1)S(1)}, u32[]{:S(2)}, u32[]{:S(2)}) async-start(bf16[4,128,2048]{2,1,0:T(8,128)(2,1)} %maximum_select_fusion), calls=%async_computation | async-start | bytes 4194304 | tf_op jit(solution)/shard_map/all_to_all | solution.py:592
  43.6 265.7 %all-gather.7.cloned.1.call-start = ((), (), s32[]{:S(2)}) async-start(), calls=%async_computation.11 | async-start | bytes 4718592 | tf_op jit(solution)/shard_map/all_gather | solution.py:678
  129.8 303.0 %all-gather.9.cloned.1.call-start = ((), (), s32[]{:S(2)}) async-start(), calls=%async_computation.12 | async-start | bytes 9437184 | tf_op jit(solution)/shard_map/all_gather | solution.py:678
  146.0 86.6 %all-to-all-start.1 = ((bf16[4,128,2048]{2,1,0:T(8,128)(2,1)}), bf16[4,128,2048]{2,1,0:T(8,128)(2,1)S(1)}, u32[]{:S(2)}, u32[]{:S(2)}) async-start(bf16[4,128,2048]{2,1,0:T(8,128)(2,1)} %maximum_select_fusion.1), calls=%async_computation.1 | async-start | bytes 4194304 | tf_op jit(solution)/shard_map/all_to_all | solution.py:592
  149.6 356.1 %all-gather.11.cloned.1.call-start = ((), (), s32[]{:S(2)}) async-start(), calls=%async_computation.13 | async-start | bytes 9437184 | tf_op jit(solution)/shard_map/all_gather | solution.py:678
  286.1 328.8 %reduce-scatter.7.cloned.1.call-start = ((), (), s32[]{:S(2)}) async-start(), calls=%async_computation.14 | async-start | bytes 2621440 | tf_op jit(solution)/shard_map/reduce_scatter | solution.py:751
  380.3 83.4 %collective-permute-start.13 = (bf16[4,2,128,1024]{3,2,1,0:T(8,128)(2,1)}, bf16[4,2,128,1024]{3,2,1,0:T(8,128)(2,1)}, u32[]{:S(2)}, u32[]{:S(2)}) collective-permute-start(bf16[4,2,128,1024]{3,2,1,0:T(8,128)(2,1)} %weight_sums.12.refs_0_), channel_id=1, source_target_pairs={{0,16},{16,0},{1,17},{17,1},{2,18},{18,2},{3,19},{19,3},{4,20},{20... | collective-permute-start | bytes 6291464 | tf_op jit(solution)/shard_map/ppermute | solution.py:576
  477.7 55.0 %collective-permute-start.16 = (bf16[4,2,128,1024]{3,2,1,0:T(8,128)(2,1)}, bf16[4,2,128,1024]{3,2,1,0:T(8,128)(2,1)}, u32[]{:S(2)}, u32[]{:S(2)}) collective-permute-start(bf16[4,2,128,1024]{3,2,1,0:T(8,128)(2,1)} %weight_sums.13.refs_0_), channel_id=1, source_target_pairs={{0,16},{16,0},{1,17},{17,1},{2,18},{18,2},{3,19},{19,3},{4,20},{20... | collective-permute-start | bytes 6291464 | tf_op jit(solution)/shard_map/ppermute | solution.py:576
  496.8 265.2 %reduce-scatter.9.cloned.1.call-start = ((), (), s32[]{:S(2)}) async-start(), calls=%async_computation.15 | async-start | bytes 2621440 | tf_op jit(solution)/shard_map/reduce_scatter | solution.py:751
  556.3 323.2 %reduce-scatter.13.cloned.1.call-start = ((), (), s32[]{:S(2)}) async-start(), calls=%async_computation.17 | async-start | bytes 2621440 | tf_op jit(solution)/shard_map/reduce_scatter | solution.py:751
  556.3 48.7 %collective-permute-start.20 = (bf16[4,2,128,1024]{3,2,1,0:T(8,128)(2,1)}, bf16[4,2,128,1024]{3,2,1,0:T(8,128)(2,1)S(1)}, u32[]{:S(2)}, u32[]{:S(2)}) collective-permute-start(bf16[4,2,128,1024]{3,2,1,0:T(8,128)(2,1)} %copy-done.19), channel_id=1, source_target_pairs={{0,16},{16,0},{1,17},{17,1},{2,18},{18,2},{3,19},{19,3},{4,20},{20... | collective-permute-start | bytes 6291464 | tf_op jit(solution)/shard_map/ppermute | solution.py:576
  557.7 91.7 %collective-permute-start.21 = (bf16[4,2,128,1024]{3,2,1,0:T(8,128)(2,1)}, bf16[4,2,128,1024]{3,2,1,0:T(8,128)(2,1)}, u32[]{:S(2)}, u32[]{:S(2)}) collective-permute-start(bf16[4,2,128,1024]{3,2,1,0:T(8,128)(2,1)} %copy-done.14), channel_id=1, source_target_pairs={{0,16},{16,0},{1,17},{17,1},{2,18},{18,2},{3,19},{19,3},{4,20},{20... | collective-permute-start | bytes 6291464 | tf_op jit(solution)/shard_map/ppermute | solution.py:576
  558.4 91.1 %collective-permute-start.15 = (bf16[512,2048]{1,0:T(8,128)(2,1)}, bf16[512,2048]{1,0:T(8,128)(2,1)}, u32[]{:S(2)}, u32[]{:S(2)}) collective-permute-start(bf16[512,2048]{1,0:T(8,128)(2,1)} %copy-done.32), channel_id=1, source_target_pairs={{0,1},{1,0},{2,3},{3,2},{4,5},{5,4},{6,7},{7,6},{8,9},{9,8},{10,11... | collective-permute-start | bytes 6291464 | tf_op jit(solution)/shard_map/ppermute | solution.py:582
  575.9 98.3 %collective-permute-start.18 = (bf16[512,2048]{1,0:T(8,128)(2,1)}, bf16[512,2048]{1,0:T(8,128)(2,1)}, u32[]{:S(2)}, u32[]{:S(2)}) collective-permute-start(bf16[512,2048]{1,0:T(8,128)(2,1)} %get-tuple-element.34), channel_id=1, source_target_pairs={{0,1},{1,0},{2,3},{3,2},{4,5},{5,4},{6,7},{7,6},{8,9},{9,8},{10,11... | collective-permute-start | bytes 6291464 | tf_op jit(solution)/shard_map/ppermute | solution.py:582
  672.9 59.2 %collective-permute-start.23 = (bf16[1024,2048]{1,0:T(8,128)(2,1)}, bf16[1024,2048]{1,0:T(8,128)(2,1)}, u32[]{:S(2)}, u32[]{:S(2)}) collective-permute-start(bf16[1024,2048]{1,0:T(8,128)(2,1)} %feature_sums.10.refs_0_), channel_id=1, source_target_pairs={{0,8},{8,0},{1,9},{9,1},{2,10},{10,2},{3,11},{11,3},{4,12},{12,4},... | collective-permute-start | bytes 12582920 | tf_op jit(solution)/shard_map/ppermute | solution.py:573
  672.9 48.4 %collective-permute-start.22 = (bf16[4,2,128,1024]{3,2,1,0:T(8,128)(2,1)}, bf16[4,2,128,1024]{3,2,1,0:T(8,128)(2,1)}, u32[]{:S(2)}, u32[]{:S(2)}) collective-permute-start(bf16[4,2,128,1024]{3,2,1,0:T(8,128)(2,1)} %weight_sums.18.refs_0_), channel_id=1, source_target_pairs={{0,16},{16,0},{1,17},{17,1},{2,18},{18,2},{3,19},{19,3},{4,20},{20... | collective-permute-start | bytes 6291464 | tf_op jit(solution)/shard_map/ppermute | solution.py:576
  680.3 53.4 %all-to-all-start.2 = ((bf16[4,128,2048]{2,1,0:T(8,128)(2,1)}), bf16[4,128,2048]{2,1,0:T(8,128)(2,1)}, u32[]{:S(2)}, u32[]{:S(2)}) async-start(bf16[4,128,2048]{2,1,0:T(8,128)(2,1)} %bitcast.169), calls=%async_computation.2 | async-start | bytes 4194304 | tf_op jit(solution)/shard_map/all_to_all | solution.py:592
  684.8 235.1 %reduce-scatter.17.cloned.1.call-start = ((), (), s32[]{:S(2)}) async-start(), calls=%async_computation.19 | async-start | bytes 2621440 | tf_op jit(solution)/shard_map/reduce_scatter | solution.py:751
  730.6 212.6 %reduce-scatter.11.cloned.1.call-start = ((), (), s32[]{:S(2)}) async-start(), calls=%async_computation.16 | async-start | bytes 2621440 | tf_op jit(solution)/shard_map/reduce_scatter | solution.py:751
  730.6 47.6 %collective-permute-start.34 = (bf16[4,2,128,1024]{3,2,1,0:T(8,128)(2,1)}, bf16[4,2,128,1024]{3,2,1,0:T(8,128)(2,1)}, u32[]{:S(2)}, u32[]{:S(2)}) collective-permute-start(bf16[4,2,128,1024]{3,2,1,0:T(8,128)(2,1)} %copy-done.25), channel_id=1, source_target_pairs={{0,16},{16,0},{1,17},{17,1},{2,18},{18,2},{3,19},{19,3},{4,20},{20... | collective-permute-start | bytes 6291464 | tf_op jit(solution)/shard_map/ppermute | solution.py:576
  762.0 58.6 %collective-permute-start.19 = (bf16[2,128,2048]{2,1,0:T(8,128)(2,1)}, bf16[2,128,2048]{2,1,0:T(8,128)(2,1)}, u32[]{:S(2)}, u32[]{:S(2)}) collective-permute-start(bf16[2,128,2048]{2,1,0:T(8,128)(2,1)} %get-tuple-element.94), channel_id=1, source_target_pairs={{0,8},{8,0},{1,9},{9,1},{2,10},{10,2},{3,11},{11,3},{4,12},{12,4},... | collective-permute-start | bytes 3145736 | tf_op jit(solution)/shard_map/ppermute | solution.py:573
  813.6 78.2 %all-to-all-start.3 = ((bf16[4,128,2048]{2,1,0:T(8,128)(2,1)}), bf16[4,128,2048]{2,1,0:T(8,128)(2,1)}, u32[]{:S(2)}, u32[]{:S(2)}) async-start(bf16[4,128,2048]{2,1,0:T(8,128)(2,1)} %bitcast.188), calls=%async_computation.4 | async-start | bytes 4194304 | tf_op jit(solution)/shard_map/all_to_all | solution.py:592
  818.1 126.4 %reduce-scatter.15.cloned.1.call-start = ((), (), s32[]{:S(2)}) async-start(), calls=%async_computation.18 | async-start | bytes 2621440 | tf_op jit(solution)/shard_map/reduce_scatter | solution.py:751
  (84 other events, 942.5 us)
Sparse Core Ops, SparseCore 0:
  15.3 106.3 all-gather.4
  129.9 106.6 all-gather.6
  239.4 123.8 all-gather.8
  365.2 137.2 all-gather.10
  505.3 42.0 reduce-scatter.6
  556.4 42.2 reduce-scatter.8
  625.5 42.1 reduce-scatter.12
  730.7 42.2 reduce-scatter.16
  788.9 56.1 reduce-scatter.10
  891.6 46.1 reduce-scatter.14
